TPU v7x, 32 devices: a whole 2x2x4 slice. The times are simulated.
32 devices in a mesh: fsdp: 2 (over x), expert: 16 (over z, y, core).
Axes of the slice: x: 2, y: 2, z: 4, core: 2. Of those that a mesh axis runs over, the one named last changes fastest.
Arguments:
- tokens: bfloat16 [4096, 1024], P(('fsdp', 'expert')), may hold values from -6 to 6
- attention_gain: float32 [1024], replicated, may hold values from 0.1 to 1.9
- attention_in: bfloat16 [1024, 3072], P(('fsdp', 'expert')), may hold values from -0.1875 to 0.1875
- attention_out: bfloat16 [1024, 1024], P(('fsdp', 'expert')), may hold values from -0.1875 to 0.1875
- expert_gain: float32 [1024], replicated, may hold values from 0.1 to 1.9
- routes: int32 [4096, 6], P(('fsdp', 'expert')), may hold values from 0 to 15, all different within a row; in each aligned block of 128 rows (0 to 127, 128 to 255, ...) at most 60 rows name the same one
- route_weights: float32 [4096, 6], P(('fsdp', 'expert')), may hold values from 0.1 to 1
- gate_weight: bfloat16 [16, 1024, 704], P('expert'), may hold values from -0.1875 to 0.1875
- up_weight: bfloat16 [16, 1024, 704], P('expert'), may hold values from -0.1875 to 0.1875
- down_weight: bfloat16 [16, 704, 1024], P('expert'), may hold values from -0.21875 to 0.21875
Outputs:
- mixed: bfloat16 [4096, 1024], P(('fsdp', 'expert'))
Inputs may be any that keep to these rules, and one draw needn't show every extreme that they name: `routes`: the 6 experts of a token differ. Among the token-expert pairs of the tokens of one device, no expert is named more than 60 times, a bound that some block reaches.
All inputs are finite; a program needn't handle non-finite values.
Results may differ from a plain program's by a relative error of at most 0.0075.
Values may be sent and summed in bfloat16 or wider, within the bound.
No kernel may reach another device: no remote copies, remote signals or barrier semaphores. Data moves between devices by JAX's collectives and lax.ppermute only.
A program may use at most 64 MiB of HBM per device.

v0:
```python
import functools
import math

import jax
import jax.numpy as jnp
from jax import lax
from jax.experimental import pallas as pl
from jax.experimental.pallas import tpu as pltpu
from jax.sharding import PartitionSpec as P

HEAD_DIM = 128
BOTH = ("fsdp", "expert")
VMEM = pl.BlockSpec(memory_space=pltpu.VMEM)
SMEM = pl.BlockSpec(memory_space=pltpu.SMEM)
HBM = pl.BlockSpec(memory_space=pltpu.HBM)
ANYWHERE = pl.BlockSpec(memory_space=pl.ANY)
NT = (((1,), (1,)), ((), ()))


def dot_nt(left, right):
    return lax.dot_general(left, right, NT, preferred_element_type=jnp.float32)


def rms_scale(inputs, scale_gain):
    mean_square = jnp.mean(inputs * inputs, axis=-1, keepdims=True)
    return inputs * lax.rsqrt(mean_square + 1e-06) * scale_gain


def limit(mebibytes):
    return pltpu.CompilerParams(vmem_limit_bytes=mebibytes * 2**20)


def chip_weights_kernel(layers, in_ref, out_ref, sent_ref):
    head_count = out_ref.shape[1] // HEAD_DIM
    pairs = []
    for pair in range(head_count // 2):
        parts = []
        for head in (2 * pair, 2 * pair + 1):
            for part in range(3):
                start = (part * head_count + head) * HEAD_DIM
                parts.append(in_ref[:, start : start + HEAD_DIM])
        parts.append(out_ref[:, 2 * pair * HEAD_DIM : (2 * pair + 2) * HEAD_DIM])
        pairs.append(jnp.concatenate(parts, axis=1))
    for chip in range(sent_ref.shape[0]):
        sent_ref[chip] = pairs[(chip // (2 * layers)) % 2 * 2 + chip % 2]


def chip_weights_call(layers, chips, attention_in, attention_out):
    rows = attention_in.shape[0]
    return pl.pallas_call(
        functools.partial(chip_weights_kernel, layers),
        out_shape=jax.ShapeDtypeStruct((chips, rows, 8 * HEAD_DIM), jnp.bfloat16),
        in_specs=[VMEM] * 2,
        out_specs=VMEM,
        compiler_params=limit(12),
        cost_estimate=pl.CostEstimate(
            flops=0, bytes_accessed=16 * chips * rows * HEAD_DIM, transcendentals=0
        ),
    )(attention_in, attention_out)


def group_weights_kernel(place_ref, in_hbm, out_hbm, *refs):
    sent_refs = refs[:4]
    in_ref, out_ref, sems = refs[4:]
    copies = [
        pltpu.make_async_copy(in_hbm, in_ref, sems.at[0]),
        pltpu.make_async_copy(out_hbm, out_ref, sems.at[1]),
    ]
    for copy in copies:
        copy.start()
    for copy in copies:
        copy.wait()
    width = out_ref.shape[1]
    for index, sent_ref in enumerate(sent_refs):
        pair = (place_ref[0] ^ (index % 2)) * 2 + (place_ref[2] ^ (index // 2))
        start = pl.multiple_of(pair * (2 * HEAD_DIM), HEAD_DIM)
        for part in range(3):
            both = in_ref[:, pl.ds(pl.multiple_of(start + part * width, HEAD_DIM), 2 * HEAD_DIM)]
            for head in range(2):
                to = (3 * head + part) * HEAD_DIM
                sent_ref[:, to : to + HEAD_DIM] = both[:, head * HEAD_DIM : (head + 1) * HEAD_DIM]
        sent_ref[:, 6 * HEAD_DIM :] = out_ref[:, pl.ds(start, 2 * HEAD_DIM)]


def group_weights_call(place, attention_in, attention_out):
    rows = attention_in.shape[0]
    one = jax.ShapeDtypeStruct((rows, 8 * HEAD_DIM), jnp.bfloat16)
    return pl.pallas_call(
        group_weights_kernel,
        out_shape=(one,) * 4,
        in_specs=[SMEM, HBM, HBM],
        out_specs=(VMEM,) * 4,
        scratch_shapes=[
            pltpu.VMEM(attention_in.shape, jnp.bfloat16),
            pltpu.VMEM(attention_out.shape, jnp.bfloat16),
            pltpu.SemaphoreType.DMA((2,)),
        ],
        compiler_params=limit(8),
        cost_estimate=pl.CostEstimate(
            flops=0, bytes_accessed=128 * rows * HEAD_DIM, transcendentals=0
        ),
    )(place, attention_in, attention_out)


def attention_kernel(block_count, piece_count, *refs):
    place_ref, gain_ref = refs[:2]
    block_refs = refs[2 : 2 + block_count]
    piece_refs = refs[2 + block_count : 2 + block_count + piece_count]
    keep_top_ref, send_top_ref, keep_low_ref, send_low_ref, weight_ref = refs[-5:]
    rows = block_refs[0].shape[0]
    half = rows // 2
    if piece_count == 1:
        weight_ref = piece_refs[0]
    else:
        layers = piece_count // 2
        for index, piece_ref in enumerate(piece_refs):
            layer, core = place_ref[1] ^ (index // 2), place_ref[3] ^ (index % 2)
            for chip in range(4):
                pair, side = place_ref[0] ^ (chip % 2), place_ref[2] ^ (chip // 2)
                device = ((pair * layers + layer) * 2 + side) * 2 + core
                span = piece_ref.shape[1]
                start = pl.multiple_of(device * span, 16)
                weight_ref[pl.ds(start, span), :] = piece_ref[chip]
    out_weights = weight_ref[:, 6 * HEAD_DIM :]
    causal = lax.broadcasted_iota(jnp.int32, (rows, rows), 0) >= lax.broadcasted_iota(
        jnp.int32, (rows, rows), 1
    )
    inputs = jnp.concatenate(
        [
            rms_scale(ref[...].astype(jnp.float32), gain_ref[...]).astype(jnp.bfloat16)
            for ref in block_refs
        ],
        axis=0,
    )
    heads = []
    for head in range(2):
        projected = jnp.dot(
            inputs,
            weight_ref[:, 3 * head * HEAD_DIM : 3 * (head + 1) * HEAD_DIM],
            preferred_element_type=jnp.float32,
        ).astype(jnp.bfloat16)
        outs = []
        for block in range(block_count):
            own = projected[block * rows : (block + 1) * rows]
            queries = own[:, :HEAD_DIM]
            keys = own[:, HEAD_DIM : 2 * HEAD_DIM]
            values = own[:, 2 * HEAD_DIM :]
            scores = dot_nt(queries, keys) * (1.0 / math.sqrt(HEAD_DIM))
            raised = jnp.where(causal, jnp.exp(jnp.where(causal, scores, 0.0)), 0.0)
            probs = raised / jnp.sum(raised, axis=-1, keepdims=True)
            outs.append(
                jnp.dot(
                    probs.astype(jnp.bfloat16), values, preferred_element_type=jnp.float32
                ).astype(jnp.bfloat16)
            )
        heads.append(jnp.concatenate(outs, axis=0))
    part = dot_nt(jnp.concatenate(heads, axis=1), out_weights).astype(jnp.bfloat16)
    for block in range(block_count):
        across, along = block // 2, block % 2
        top = send_top_ref if across else keep_top_ref
        low = send_low_ref if along else keep_low_ref
        top[along] = part[block * rows : block * rows + half]
        low[across] = part[block * rows + half : (block + 1) * rows]


def attention_call(place, gain, blocks, pieces, after):
    count = len(blocks)
    rows, width = blocks[0].shape
    tokens = count * rows
    out = jax.ShapeDtypeStruct((count // 2, rows // 2, width), jnp.bfloat16)
    return pl.pallas_call(
        functools.partial(attention_kernel, count, len(pieces)),
        out_shape=(out,) * 4,
        in_specs=[SMEM] + [VMEM] * (1 + count + len(pieces)) + [ANYWHERE] * len(after),
        out_specs=(VMEM,) * 4,
        scratch_shapes=[
            pltpu.VMEM((width, 8 * HEAD_DIM) if len(pieces) > 1 else (16, 128), jnp.bfloat16)
        ],
        compiler_params=limit(16),
        cost_estimate=pl.CostEstimate(
            flops=4 * tokens * (width * 4 * HEAD_DIM + 2 * rows * HEAD_DIM),
            bytes_accessed=4 * tokens * width + width * 16 * HEAD_DIM,
            transcendentals=2 * tokens * rows,
        ),
    )(place, gain, *blocks, *pieces, *after)


def sum_kernel(picks, *refs):
    out_ref = refs[-1]
    total = None
    for ref, pick in zip(refs, picks):
        term = (ref[...] if pick is None else ref[pick]).astype(jnp.float32)
        total = term if total is None else total + term
    out_ref[...] = total.astype(out_ref.dtype)


def sum_call(terms, after=()):
    arrays = [term[0] if isinstance(term, tuple) else term for term in terms]
    picks = [term[1] if isinstance(term, tuple) else None for term in terms]
    shape = arrays[0].shape if picks[0] is None else arrays[0].shape[1:]
    return pl.pallas_call(
        functools.partial(sum_kernel, picks),
        out_shape=jax.ShapeDtypeStruct(shape, jnp.bfloat16),
        in_specs=[VMEM] * len(arrays) + [ANYWHERE] * len(after),
        out_specs=VMEM,
        compiler_params=limit(12),
        cost_estimate=pl.CostEstimate(
            flops=len(arrays) * math.prod(shape),
            bytes_accessed=2 * (len(arrays) + 1) * math.prod(shape),
            transcendentals=0,
        ),
    )(*arrays, *after)


def stream_kernel(tokens_ref, gain_ref, *refs):
    hidden_ref, normed_ref = refs[-2:]
    half = tokens_ref.shape[0] // 2
    for index in range(2):
        keep_ref, near_ref, far_ref = refs[3 * index : 3 * index + 3]
        rows = pl.ds(index * half, half)
        hidden = (
            tokens_ref[rows, :].astype(jnp.float32)
            + keep_ref[0].astype(jnp.float32)
            + near_ref[0].astype(jnp.float32)
            + far_ref[...].astype(jnp.float32)
        )
        hidden_ref[rows, :] = hidden
        normed_ref[rows, :] = rms_scale(hidden, gain_ref[...]).astype(jnp.bfloat16)


def stream_call(tokens, gain, *parts):
    return pl.pallas_call(
        stream_kernel,
        out_shape=(
            jax.ShapeDtypeStruct(tokens.shape, jnp.float32),
            jax.ShapeDtypeStruct(tokens.shape, jnp.bfloat16),
        ),
        in_specs=[VMEM] * 8,
        out_specs=(VMEM, VMEM),
        compiler_params=limit(12),
        cost_estimate=pl.CostEstimate(
            flops=6 * tokens.size, bytes_accessed=14 * tokens.size, transcendentals=0
        ),
    )(tokens, gain[None, :], *parts)


def expert_kernel(tiles, pick, *refs):
    place_ref = refs[0]
    block_refs = refs[1:3]
    scale_ref = refs[3]
    weight_refs = refs[4:10]
    own_ref, side_ref = refs[-2:]
    inputs = jnp.concatenate([ref[...] for ref in block_refs], axis=0)
    result = None
    for expert in range(2):
        gate_ref, up_ref, down_ref = weight_refs[3 * expert : 3 * expert + 3]
        scale = jnp.concatenate(
            [scale_ref[*pick, block, pl.ds(place_ref[4 + expert], 1), :] for block in range(2)],
            axis=1,
        )
        for start, size in tiles:
            gate_value = dot_nt(gate_ref[start : start + size, :], inputs)
            up_value = dot_nt(up_ref[start : start + size, :], inputs)
            inner = gate_value / (1.0 + jnp.exp(-gate_value)) * (up_value * scale)
            term = jnp.dot(
                down_ref[:, start : start + size],
                inner.astype(jnp.bfloat16),
                preferred_element_type=jnp.float32,
            )
            result = term if result is None else result + term
    result = result.astype(jnp.bfloat16)
    rows = block_refs[0].shape[0]
    own_ref[...] = result[:, :rows]
    side_ref[...] = result[:, rows:]


def expert_call(place, blocks, picked, weights, after):
    scale_map, pick = picked
    rows, width = blocks[0].shape
    hidden = weights[0].shape[0]
    tiles = [(start, min(256, hidden - start)) for start in range(0, hidden, 256)]
    one = jax.ShapeDtypeStruct((width, rows), jnp.bfloat16)
    return pl.pallas_call(
        functools.partial(expert_kernel, tiles, pick),
        out_shape=(one,) * 2,
        in_specs=[SMEM] + [VMEM] * 9 + [ANYWHERE] * len(after),
        out_specs=(VMEM,) * 2,
        compiler_params=limit(20),
        cost_estimate=pl.CostEstimate(
            flops=2 * 4 * rows * width * hidden * 3,
            bytes_accessed=12 * hidden * width + 8 * rows * width,
            transcendentals=4 * rows * hidden,
        ),
    )(place, *blocks, scale_map, *weights, *after)


def scale_kernel(routes_ref, weights_ref, tokens_ref, gain_ref, map_ref, tokens_out, gain_out):
    top_count, rows = routes_ref.shape
    experts = lax.broadcasted_iota(jnp.int32, (map_ref.shape[0], rows), 0)
    total = jnp.zeros(map_ref.shape, jnp.float32)
    for choice in range(top_count):
        chosen = experts == routes_ref[choice : choice + 1, :]
        total = total + jnp.where(chosen, weights_ref[choice : choice + 1, :], 0.0)
    map_ref[...] = total
    tokens_out[...] = tokens_ref[...]
    gain_out[...] = gain_ref[...]


def scale_call(expert_size, routes, weights, tokens, gain):
    rows = routes.shape[1]
    return pl.pallas_call(
        scale_kernel,
        out_shape=(
            jax.ShapeDtypeStruct((expert_size, rows), jnp.float32),
            jax.ShapeDtypeStruct(tokens.shape, tokens.dtype),
            jax.ShapeDtypeStruct(gain.shape, gain.dtype),
        ),
        in_specs=[VMEM] * 4,
        out_specs=(VMEM,) * 3,
        compiler_params=limit(8),
    )(routes, weights, tokens, gain)


def pair_kernel(first_ref, second_ref, pair_ref):
    pair_ref[0] = first_ref[...]
    pair_ref[1] = second_ref[...]


def pair_call(first, second):
    return pl.pallas_call(
        pair_kernel,
        out_shape=jax.ShapeDtypeStruct((2, *first.shape), first.dtype),
        in_specs=[VMEM] * 2,
        out_specs=VMEM,
        compiler_params=limit(8),
    )(first, second)


def load_kernel(gate_hbm, up_hbm, down_hbm, after_ref, gate_ref, up_ref, turned_ref, down_ref, sems):
    copies = [
        pltpu.make_async_copy(source, target, sems.at[index])
        for index, (source, target) in enumerate(
            ((down_hbm, down_ref), (gate_hbm, gate_ref), (up_hbm, up_ref))
        )
    ]
    for copy in copies:
        copy.start()
    copies[0].wait()
    columns, rows = down_ref.shape
    turned_ref[:, :columns] = down_ref[...].T
    if turned_ref.shape[1] > columns:
        turned_ref[:, columns:] = jnp.zeros((rows, turned_ref.shape[1] - columns), turned_ref.dtype)
    for copy in copies[1:]:
        copy.wait()


def load_call(weights, after):
    gate, _, down = weights
    rows, columns = down.shape
    return pl.pallas_call(
        load_kernel,
        out_shape=(
            jax.ShapeDtypeStruct(gate.shape, gate.dtype),
            jax.ShapeDtypeStruct(gate.shape, gate.dtype),
            jax.ShapeDtypeStruct((columns, -(-rows // 128) * 128), down.dtype),
        ),
        in_specs=[HBM] * 3 + [ANYWHERE],
        out_specs=(VMEM,) * 3,
        scratch_shapes=[pltpu.VMEM(down.shape, down.dtype), pltpu.SemaphoreType.DMA((3,))],
        compiler_params=limit(16),
        cost_estimate=pl.CostEstimate(
            flops=0, bytes_accessed=12 * gate.size, transcendentals=0
        ),
    )(*weights, after)


def mix_kernel(hidden_ref, *refs):
    total = refs[0][...].astype(jnp.float32)
    for ref in refs[1:-1]:
        total = total + ref[...].astype(jnp.float32)
    refs[-1][...] = (hidden_ref[...] + total.T).astype(jnp.bfloat16)


def mix_call(hidden, terms):
    return pl.pallas_call(
        mix_kernel,
        out_shape=jax.ShapeDtypeStruct(hidden.shape, jnp.bfloat16),
        in_specs=[VMEM] * (1 + len(terms)),
        out_specs=VMEM,
        compiler_params=limit(12),
        cost_estimate=pl.CostEstimate(
            flops=(1 + len(terms)) * hidden.size,
            bytes_accessed=(6 + 2 * len(terms)) * hidden.size,
            transcendentals=0,
        ),
    )(hidden, *terms)


def per_device(
    tokens,
    attention_gain,
    attention_in,
    attention_out,
    expert_gain,
    routes,
    route_weights,
    gate_weight,
    up_weight,
    down_weight,
):
    fsdp_size = lax.axis_size("fsdp")
    expert_size = lax.axis_size("expert")
    row_count, model_width = tokens.shape
    weight_rows = attention_out.shape[0]
    layers = expert_size // 4

    def swap_pair(value):
        return lax.ppermute(value, "fsdp", [(f, f ^ 1) for f in range(fsdp_size)])

    def swap_expert(value, mask):
        return lax.ppermute(value, "expert", [(e, e ^ mask) for e in range(expert_size)])

    def swap_core(value):
        return swap_expert(value, 1)

    def swap_side(value):
        return swap_expert(value, 2)

    def swap_layer(value, mask):
        return swap_expert(value, 4 * mask) if mask else value

    hold = lax.optimization_barrier
    my_pair = lax.axis_index("fsdp").astype(jnp.int32)
    my_expert = lax.axis_index("expert").astype(jnp.int32)
    place = jnp.stack(
        [my_pair, my_expert // 4, my_expert // 2 % 2, my_expert % 2, my_expert, my_expert ^ 1]
    )
    chips = fsdp_size * expert_size // 2
    as_tree = fsdp_size == 2 and layers == 4 and weight_rows % 16 == 0

    blocks = [tokens, swap_pair(tokens), swap_side(tokens)]
    gate_rows, up_rows, down_rows = gate_weight[0].T, up_weight[0].T, down_weight[0]
    if as_tree:
        mine, by_pair, by_side, by_both = group_weights_call(place, attention_in, attention_out)
        both_ways = [
            (f * expert_size + e, (f ^ 1) * expert_size + (e ^ 2))
            for f in range(fsdp_size)
            for e in range(expert_size)
        ]
        rows_here = jnp.stack(
            [mine, swap_pair(by_pair), swap_side(by_side), lax.ppermute(by_both, BOTH, both_ways)]
        )
        rows_here, blocks, gate_rows, up_rows, route_weights = hold(
            (rows_here, blocks, gate_rows, up_rows, route_weights)
        )
        far = swap_layer(rows_here, 2)
        near = swap_layer(rows_here, 1)
    else:
        sent = chip_weights_call(layers, chips, attention_in, attention_out)
        same_core = [[2 * chip + core for chip in range(chips)] for core in range(2)]
        got = lax.all_to_all(
            sent, BOTH, split_axis=0, concat_axis=0, axis_index_groups=same_core, tiled=True
        )
        in_order = jnp.stack([got, swap_core(got)], axis=1)
        in_order = jnp.where(my_expert % 2 == 0, in_order, in_order[:, ::-1])
        pieces = [in_order.reshape(model_width, 8 * HEAD_DIM)]
    blocks.append(swap_side(blocks[1]))
    own_expert = [gate_rows, up_rows, down_rows]
    other_expert = [swap_core(gate_rows), swap_core(up_rows)]
    scale_map, own_tokens, own_gain = scale_call(
        expert_size, routes.T, route_weights.T, blocks[0], attention_gain[None, :]
    )
    blocks[0] = own_tokens
    if as_tree:
        far, near, other_expert, scale_map, blocks, down_rows = hold(
            (far, near, other_expert, scale_map, blocks, down_rows)
        )
        pieces = []
        for piece in (rows_here, near, far, swap_layer(far, 1)):
            pieces += [piece, swap_core(piece)]
    other_expert.append(swap_core(down_rows))

    scale_map = pair_call(scale_map, swap_side(scale_map))
    bit = layers // 2
    while bit > 1:
        scale_map = pair_call(scale_map, swap_layer(scale_map, bit))
        bit //= 2

    keep_top, send_top, keep_low, send_low = attention_call(
        place, own_gain, blocks, pieces, [scale_map, other_expert[2]]
    )

    near_top = swap_side(send_top)
    near_low = swap_pair(send_low)
    own_expert = load_call(own_expert, keep_top)
    scale_map, _ = hold((scale_map, keep_top))
    scale_maps = [scale_map, swap_layer(scale_map, 1)]
    near_top, near_low, own_expert, scale_maps = hold(
        (near_top, near_low, own_expert, scale_maps)
    )
    far_top = swap_pair(sum_call([(keep_top, 1), (near_top, 1)]))
    far_low = swap_side(sum_call([(keep_low, 1), (near_low, 1)]))
    other_expert = load_call(other_expert, near_low)
    far_top, far_low, other_expert = hold((far_top, far_low, other_expert))
    hidden_stream, expert_in = stream_call(
        tokens, expert_gain, keep_top, near_top, far_top, keep_low, near_low, far_low
    )

    arrivals = {0: expert_in}
    order = [0] + sorted(range(1, layers), key=lambda mask: (mask == 1, mask))
    sums, finals, crossings = [], [], []
    for step, mask in enumerate(order):
        low = mask & -mask
        source = arrivals[mask ^ low]
        if mask == 1 and step >= 2:
            source, _ = hold((source, block))
        block = swap_layer(source, low)
        if step == 1:
            block, _ = hold((block, crossings[0]))
        arrivals[mask] = block
        own, crossing = expert_call(
            place,
            [block, swap_side(block)],
            (scale_maps[mask % 2], [mask >> bit & 1 for bit in range(1, layers.bit_length() - 1)]),
            [*own_expert, *other_expert],
            (sums[step - 3 : step - 2] if step >= 3 else []) + crossings[-1:],
        )
        crossings.append(crossing)
        if step == 0:
            first = own
        else:
            sums.append(sum_call([own, swap_side(crossing)], finals[:1] if step == 2 else []))
            finals.append(swap_layer(sums[-1], mask))
    crossing, _ = hold((crossings[0], crossings[-1]))
    return mix_call(hidden_stream, [first, *finals, swap_side(crossing)])


def solution(mesh):
    placed = (
        P(("fsdp", "expert"), None),
        P(),
        P(("fsdp", "expert"), None),
        P(("fsdp", "expert"), None),
        P(),
        P(("fsdp", "expert"), None),
        P(("fsdp", "expert"), None),
        P("expert", None, None),
        P("expert", None, None),
        P("expert", None, None),
    )
    return jax.shard_map(
        per_device,
        mesh=mesh,
        in_specs=placed,
        out_specs=P(("fsdp", "expert"), None),
        check_vma=False,
    )
```

profile of v0, /device:TPU:0, one launch (start us, length us, event | category | flops | bytes accessed | tf_op | source)
XLA Modules:
  0.0 123.0 jit_solution(3372555862301065012)
XLA Ops:
  0.0 2.9 %collective-permute-start.3 = (bf16[128,1024]{1,0:T(8,128)(2,1)}, bf16[128,1024]{1,0:T(8,128)(2,1)S(1)}, u32[]{:S(2)}, u32[]{:S(2)}) collective-permute-start(bf16[128,1024]{1,0:T(8,128)(2,1)} %tokens_ref.2), channel_id=1, source_target_pairs={{0,16},{16,0},{1,17},{17,1},{2,18},{18,2},{3,19},{19,3},{4,20},{20... | collective-permute-start | bytes 786440 | tf_op jit(solution)/shard_map/ppermute | solution.py:418
  2.9 1.5 %collective-permute-start.4 = (bf16[128,1024]{1,0:T(8,128)(2,1)}, bf16[128,1024]{1,0:T(8,128)(2,1)S(1)}, u32[]{:S(2)}, u32[]{:S(2)}) collective-permute-start(bf16[128,1024]{1,0:T(8,128)(2,1)} %tokens_ref.2), channel_id=1, source_target_pairs={{0,2},{1,3},{2,0},{3,1},{4,6},{5,7},{6,4},{7,5},{8,10},{9,11},{10,... | collective-permute-start | bytes 786440 | tf_op jit(solution)/shard_map/ppermute | solution.py:421
  4.5 0.9 copy-done.5
  5.5 0.8 copy-done.6
  6.3 0.9 shard_map.100
  7.3 0.6 collective-permute-start.1
  7.8 1.5 %collective-permute-start.2 = (bf16[32,1024]{1,0:T(8,128)(2,1)S(1)}, bf16[32,1024]{1,0:T(8,128)(2,1)S(1)}, u32[]{:S(2)}, u32[]{:S(2)}) collective-permute-start(bf16[32,1024]{1,0:T(8,128)(2,1)S(1)} %get-tuple-element.68), channel_id=1, source_target_pairs={{0,18},{1,19},{2,16},{3,17},{4,22},{5,23},{6,20},{7,21},{8,26},{9,... | collective-permute-start | bytes 196616 | tf_op jit(solution)/shard_map/ppermute | solution.py:451
  9.3 1.5 %collective-permute-start = (bf16[32,1024]{1,0:T(8,128)(2,1)S(1)}, bf16[32,1024]{1,0:T(8,128)(2,1)S(1)}, u32[]{:S(2)}, u32[]{:S(2)}) collective-permute-start(bf16[32,1024]{1,0:T(8,128)(2,1)S(1)} %get-tuple-element.66), channel_id=1, source_target_pairs={{0,16},{16,0},{1,17},{17,1},{2,18},{18,2},{3,19},{19,3},{4,20},{20... | collective-permute-start | bytes 196616 | tf_op jit(solution)/shard_map/ppermute | solution.py:418
  10.8 2.9 %collective-permute-done.1 = bf16[32,1024]{1,0:T(8,128)(2,1)S(1)} collective-permute-done((bf16[32,1024]{1,0:T(8,128)(2,1)S(1)}, bf16[32,1024]{1,0:T(8,128)(2,1)S(1)}, u32[]{:S(2)}, u32[]{:S(2)}) %collective-permute-start.1) | collective-permute-done | bytes 65568 | tf_op jit(solution)/shard_map/ppermute | solution.py:421
  13.9 0.5 collective-permute-start.8
  14.4 2.6 %collective-permute-start.5 = (bf16[4,32,1024]{2,1,0:T(8,128)(2,1)S(1)}, bf16[4,32,1024]{2,1,0:T(8,128)(2,1)S(1)}, u32[]{:S(2)}, u32[]{:S(2)}) collective-permute-start(bf16[4,32,1024]{2,1,0:T(8,128)(2,1)S(1)} %pad_maximum_fusion.refs_6_), channel_id=1, source_target_pairs={{0,8},{1,9},{2,10},{3,11},{4,12},{5,13},{6,14},{7,15},{8,0},{9,1},... | collective-permute-start | bytes 786440 | tf_op jit(solution)/shard_map/ppermute | solution.py:421
  17.0 1.6 %collective-permute-start.6 = (bf16[4,32,1024]{2,1,0:T(8,128)(2,1)S(1)}, bf16[4,32,1024]{2,1,0:T(8,128)(2,1)S(1)}, u32[]{:S(2)}, u32[]{:S(2)}) collective-permute-start(bf16[4,32,1024]{2,1,0:T(8,128)(2,1)S(1)} %pad_maximum_fusion.refs_6_), channel_id=1, source_target_pairs={{0,4},{1,5},{2,6},{3,7},{4,0},{5,1},{6,2},{7,3},{8,12},{9,13},{10,... | collective-permute-start | bytes 786440 | tf_op jit(solution)/shard_map/ppermute | solution.py:421
  18.6 1.5 %collective-permute-start.9 = (bf16[128,1024]{1,0:T(8,128)(2,1)S(1)}, bf16[128,1024]{1,0:T(8,128)(2,1)S(1)}, u32[]{:S(2)}, u32[]{:S(2)}) collective-permute-start(bf16[128,1024]{1,0:T(8,128)(2,1)S(1)} %collective-permute-done.3.refs_3_), channel_id=1, source_target_pairs={{0,2},{1,3},{2,0},{3,1},{4,6},{5,7},{6,4},{7,5},{8,10},{9,11},{10,... | collective-permute-start | bytes 786440 | tf_op jit(solution)/shard_map/ppermute | solution.py:421
  20.1 0.9 copy-done.3
  21.0 0.7 copy-done.7
  21.7 0.7 copy-done.8
  22.4 0.7 copy-done.9
  23.1 6.2 %collective-permute-done.5.refs_10_ = bf16[4,32,1024]{2,1,0:T(8,128)(2,1)S(1)} collective-permute-done((bf16[4,32,1024]{2,1,0:T(8,128)(2,1)S(1)}, bf16[4,32,1024]{2,1,0:T(8,128)(2,1)S(1)}, u32[]{:S(2)}, u32[]{:S(2)}) %collective-permute-start.5) | collective-permute-done | bytes 262176 | tf_op jit(solution)/shard_map/ppermute | solution.py:421
  29.6 1.5 %collective-permute-start.13 = (bf16[4,32,1024]{2,1,0:T(8,128)(2,1)S(1)}, bf16[4,32,1024]{2,1,0:T(8,128)(2,1)S(1)}, u32[]{:S(2)}, u32[]{:S(2)}) collective-permute-start(bf16[4,32,1024]{2,1,0:T(8,128)(2,1)S(1)} %collective-permute-done.5.refs_10_), channel_id=1, source_target_pairs={{0,4},{1,5},{2,6},{3,7},{4,0},{5,1},{6,2},{7,3},{8,12},{9,13},{10,... | collective-permute-start | bytes 786440 | tf_op jit(solution)/shard_map/ppermute | solution.py:421
  31.1 1.5 %collective-permute-start.15 = (f32[16,128]{1,0:T(8,128)S(1)}, f32[16,128]{1,0:T(8,128)S(1)}, u32[]{:S(2)}, u32[]{:S(2)}) collective-permute-start(f32[16,128]{1,0:T(8,128)S(1)} %get-tuple-element.85.first_ref), channel_id=1, source_target_pairs={{0,2},{1,3},{2,0},{3,1},{4,6},{5,7},{6,4},{7,5},{8,10},{9,11},{10,... | collective-permute-start | bytes 24584 | tf_op jit(solution)/shard_map/ppermute | solution.py:421
  32.6 2.2 %collective-permute-done.15.second_ref = f32[16,128]{1,0:T(8,128)S(1)} collective-permute-done((f32[16,128]{1,0:T(8,128)S(1)}, f32[16,128]{1,0:T(8,128)S(1)}, u32[]{:S(2)}, u32[]{:S(2)}) %collective-permute-start.15) | collective-permute-done | bytes 8224 | tf_op jit(solution)/shard_map/ppermute | solution.py:421
  34.7 2.3 %collective-permute-start.16 = (f32[2,16,128]{2,1,0:T(8,128)S(1)}, f32[2,16,128]{2,1,0:T(8,128)S(1)}, u32[]{:S(2)}, u32[]{:S(2)}) collective-permute-start(f32[2,16,128]{2,1,0:T(8,128)S(1)} %shard_map.102.first_ref), channel_id=1, source_target_pairs={{0,8},{1,9},{2,10},{3,11},{4,12},{5,13},{6,14},{7,15},{8,0},{9,1},... | collective-permute-start | bytes 49160 | tf_op jit(solution)/shard_map/ppermute | solution.py:421
  37.1 0.5 collective-permute-start.12
  37.6 1.8 %collective-permute-done.16.second_ref = f32[2,16,128]{2,1,0:T(8,128)S(1)} collective-permute-done((f32[2,16,128]{2,1,0:T(8,128)S(1)}, f32[2,16,128]{2,1,0:T(8,128)S(1)}, u32[]{:S(2)}, u32[]{:S(2)}) %collective-permute-start.16) | collective-permute-done | bytes 16416 | tf_op jit(solution)/shard_map/ppermute | solution.py:421
  39.4 0.5 collective-permute-start.14
  39.9 1.0 collective-permute-done.11.refs_9_
  40.9 0.4 collective-permute-done.14.refs_13_
  41.3 4.0 %shard_map.104 = (bf16[2,64,1024]{2,1,0:T(8,128)(2,1)S(1)}, bf16[2,64,1024]{2,1,0:T(8,128)(2,1)S(1)}, bf16[2,64,1024]{2,1,0:T(8,128)(2,1)S(1)}, bf16[2,64,1024]{2,1,0:T(8,128)(2,1)S(1)}) custom-call(s32[6]{0:T(128)S(1)} %stack.42.place_ref.refs_0_, f32[1,1024]{1,0:T(1,128)S(1)} %get-tuple-element.71.refs_1_, ...), custom_call_target="tpu_custom_call" | custom-call | flops 1140850688 | bytes 4194304 | tf_op jit(solution)/shard_map/pallas_call | solution.py:171
  45.3 1.6 %collective-permute-start.18 = (bf16[2,64,1024]{2,1,0:T(8,128)(2,1)S(1)}, bf16[2,64,1024]{2,1,0:T(8,128)(2,1)S(1)}, u32[]{:S(2)}, u32[]{:S(2)}) collective-permute-start(bf16[2,64,1024]{2,1,0:T(8,128)(2,1)S(1)} %get-tuple-element.88), channel_id=1, source_target_pairs={{0,2},{1,3},{2,0},{3,1},{4,6},{5,7},{6,4},{7,5},{8,10},{9,11},{10,... | collective-permute-start | bytes 786440 | tf_op jit(solution)/shard_map/ppermute | solution.py:421
  46.9 0.5 collective-permute-start.19
  47.4 1.3 %collective-permute-start.20 = (f32[2,2,16,128]{3,2,1,0:T(8,128)S(1)}, f32[2,2,16,128]{3,2,1,0:T(8,128)S(1)}, u32[]{:S(2)}, u32[]{:S(2)}) collective-permute-start(f32[2,2,16,128]{3,2,1,0:T(8,128)S(1)} %shard_map.103.refs_14_.refs_3_), channel_id=1, source_target_pairs={{0,4},{1,5},{2,6},{3,7},{4,0},{5,1},{6,2},{7,3},{8,12},{9,13},{10,... | collective-permute-start | bytes 98312 | tf_op jit(solution)/shard_map/ppermute | solution.py:421
  48.7 1.3 %shard_map.105 = (bf16[704,1024]{1,0:T(8,128)(2,1)S(1)}, bf16[704,1024]{1,0:T(8,128)(2,1)S(1)}, bf16[1024,768]{1,0:T(8,128)(2,1)S(1)}) custom-call(bf16[704,1024]{1,0:T(8,128)(2,1)S(1)} %bitcast.24, bf16[704,1024]{1,0:T(8,128)(2,1)S(1)} %bitcast.26, bf16[704,1024]{1,0:T(8,128)(2,1)S(1)} %bitcast.22, bf16[2,64,1024]{2,1,0:T(8,128)(2,1)S(1)} %get-tuple-element.87.after_ref.refs_0_), custom_call_target="tpu_custom_call" | custom-call | bytes 8650752 | tf_op jit(solution)/shard_map/pallas_call | solution.py:360
  50.0 1.4 %collective-permute-done.20.refs_3_ = f32[2,2,16,128]{3,2,1,0:T(8,128)S(1)} collective-permute-done((f32[2,2,16,128]{3,2,1,0:T(8,128)S(1)}, f32[2,2,16,128]{3,2,1,0:T(8,128)S(1)}, u32[]{:S(2)}, u32[]{:S(2)}) %collective-permute-start.20) | collective-permute-done | bytes 32800 | tf_op jit(solution)/shard_map/ppermute | solution.py:421
  51.3 2.4 %collective-permute-done.18.refs_1_ = bf16[2,64,1024]{2,1,0:T(8,128)(2,1)S(1)} collective-permute-done((bf16[2,64,1024]{2,1,0:T(8,128)(2,1)S(1)}, bf16[2,64,1024]{2,1,0:T(8,128)(2,1)S(1)}, u32[]{:S(2)}, u32[]{:S(2)}) %collective-permute-start.18) | collective-permute-done | bytes 262176 | tf_op jit(solution)/shard_map/ppermute | solution.py:421
  53.7 1.2 collective-permute-done.19.refs_1_.after_ref.refs_4_
  55.0 0.6 collective-permute-start.22
  55.6 1.4 %collective-permute-start.21 = (bf16[64,1024]{1,0:T(8,128)(2,1)S(1)}, bf16[64,1024]{1,0:T(8,128)(2,1)S(1)}, u32[]{:S(2)}, u32[]{:S(2)}) collective-permute-start(bf16[64,1024]{1,0:T(8,128)(2,1)S(1)} %shard_map.106), channel_id=1, source_target_pairs={{0,16},{16,0},{1,17},{17,1},{2,18},{18,2},{3,19},{19,3},{4,20},{20... | collective-permute-start | bytes 393224 | tf_op jit(solution)/shard_map/ppermute | solution.py:418
  57.0 1.4 %shard_map.108 = (bf16[704,1024]{1,0:T(8,128)(2,1)S(1)}, bf16[704,1024]{1,0:T(8,128)(2,1)S(1)}, bf16[1024,768]{1,0:T(8,128)(2,1)S(1)}) custom-call(bf16[704,1024]{1,0:T(8,128)(2,1)S(1)} %collective-permute-done.7.gate_hbm, bf16[704,1024]{1,0:T(8,128)(2,1)S(1)} %collective-permute-done.8.up_hbm, ...), custom_call_target="tpu_custom_call" | custom-call | bytes 8650752 | tf_op jit(solution)/shard_map/pallas_call | solution.py:360
  58.5 1.5 %collective-permute-done.22.refs_5_ = bf16[64,1024]{1,0:T(8,128)(2,1)S(1)} collective-permute-done((bf16[64,1024]{1,0:T(8,128)(2,1)S(1)}, bf16[64,1024]{1,0:T(8,128)(2,1)S(1)}, u32[]{:S(2)}, u32[]{:S(2)}) %collective-permute-start.22) | collective-permute-done | bytes 131104 | tf_op jit(solution)/shard_map/ppermute | solution.py:421
  60.0 0.7 collective-permute-done.21.refs_2_
  60.9 1.6 %collective-permute-start.23 = (bf16[128,1024]{1,0:T(8,128)(2,1)S(1)}, bf16[128,1024]{1,0:T(8,128)(2,1)S(1)}, u32[]{:S(2)}, u32[]{:S(2)}) collective-permute-start(bf16[128,1024]{1,0:T(8,128)(2,1)S(1)} %get-tuple-element.121.refs_1_), channel_id=1, source_target_pairs={{0,2},{1,3},{2,0},{3,1},{4,6},{5,7},{6,4},{7,5},{8,10},{9,11},{10,... | collective-permute-start | bytes 786440 | tf_op jit(solution)/shard_map/ppermute | solution.py:421
  62.5 2.3 %collective-permute-start.24 = (bf16[128,1024]{1,0:T(8,128)(2,1)S(1)}, bf16[128,1024]{1,0:T(8,128)(2,1)S(1)}, u32[]{:S(2)}, u32[]{:S(2)}) collective-permute-start(bf16[128,1024]{1,0:T(8,128)(2,1)S(1)} %get-tuple-element.121.refs_1_), channel_id=1, source_target_pairs={{0,8},{1,9},{2,10},{3,11},{4,12},{5,13},{6,14},{7,15},{8,0},{9,1},... | collective-permute-start | bytes 786440 | tf_op jit(solution)/shard_map/ppermute | solution.py:421
  64.8 2.6 %collective-permute-done.23.refs_2_ = bf16[128,1024]{1,0:T(8,128)(2,1)S(1)} collective-permute-done((bf16[128,1024]{1,0:T(8,128)(2,1)S(1)}, bf16[128,1024]{1,0:T(8,128)(2,1)S(1)}, u32[]{:S(2)}, u32[]{:S(2)}) %collective-permute-start.23) | collective-permute-done | bytes 262176 | tf_op jit(solution)/shard_map/ppermute | solution.py:421
  67.4 4.3 %shard_map.110 = (bf16[1024,128]{1,0:T(8,128)(2,1)S(1)}, bf16[1024,128]{1,0:T(8,128)(2,1)S(1)}) custom-call(s32[6]{0:T(128)S(1)} %stack.42.place_ref.refs_0_, bf16[128,1024]{1,0:T(8,128)(2,1)S(1)} %get-tuple-element.121.refs_1_, bf16[128,1024]{1,0:T(8,128)(2,1)S(1)} %collective-permute-done.23.refs_2_, f32[2,2,16,128]{3,2,1,0:T(8,128)S(1)} %shard_map.103.refs_14_.refs_3_, ...), custom_call_target="tpu_custom_call" | custom-call | flops 2214592512 | bytes 9699328 | tf_op jit(solution)/shard_map/pallas_call | solution.py:283
  71.6 3.2 %collective-permute-done.24.refs_1_ = bf16[128,1024]{1,0:T(8,128)(2,1)S(1)} collective-permute-done((bf16[128,1024]{1,0:T(8,128)(2,1)S(1)}, bf16[128,1024]{1,0:T(8,128)(2,1)S(1)}, u32[]{:S(2)}, u32[]{:S(2)}) %collective-permute-start.24) | collective-permute-done | bytes 262176 | tf_op jit(solution)/shard_map/ppermute | solution.py:421
  75.2 7.1 %collective-permute-done.28.refs_1_ = bf16[128,1024]{1,0:T(8,128)(2,1)S(1)} collective-permute-done((bf16[128,1024]{1,0:T(8,128)(2,1)S(1)}, bf16[128,1024]{1,0:T(8,128)(2,1)S(1)}, u32[]{:S(2)}, u32[]{:S(2)}) %collective-permute-start.28) | collective-permute-done | bytes 262176 | tf_op jit(solution)/shard_map/ppermute | solution.py:421
  82.9 4.3 %shard_map.111 = (bf16[1024,128]{1,0:T(8,128)(2,1)S(1)}, bf16[1024,128]{1,0:T(8,128)(2,1)S(1)}) custom-call(s32[6]{0:T(128)S(1)} %stack.42.place_ref.refs_0_, bf16[128,1024]{1,0:T(8,128)(2,1)S(1)} %collective-permute-done.24.refs_1_, bf16[128,1024]{1,0:T(8,128)(2,1)S(1)} %collective-permute-done.25.refs_2_, ...), custom_call_target="tpu_custom_call" | custom-call | flops 2214592512 | bytes 9699328 | tf_op jit(solution)/shard_map/pallas_call | solution.py:283
  87.1 1.7 %collective-permute-start.26 = (bf16[1024,128]{1,0:T(8,128)(2,1)S(1)}, bf16[1024,128]{1,0:T(8,128)(2,1)S(1)}, u32[]{:S(2)}, u32[]{:S(2)}) collective-permute-start(bf16[1024,128]{1,0:T(8,128)(2,1)S(1)} %get-tuple-element.117.refs_10_), channel_id=1, source_target_pairs={{0,2},{1,3},{2,0},{3,1},{4,6},{5,7},{6,4},{7,5},{8,10},{9,11},{10,... | collective-permute-start | bytes 786440 | tf_op jit(solution)/shard_map/ppermute | solution.py:421
  89.2 0.9 collective-permute-done.29.refs_2_
  90.2 4.3 %shard_map.113 = (bf16[1024,128]{1,0:T(8,128)(2,1)S(1)}, bf16[1024,128]{1,0:T(8,128)(2,1)S(1)}) custom-call(s32[6]{0:T(128)S(1)} %stack.42.place_ref.refs_0_, bf16[128,1024]{1,0:T(8,128)(2,1)S(1)} %collective-permute-done.28.refs_1_, bf16[128,1024]{1,0:T(8,128)(2,1)S(1)} %collective-permute-done.29.refs_2_, ...), custom_call_target="tpu_custom_call" | custom-call | flops 2214592512 | bytes 9699328 | tf_op jit(solution)/shard_map/pallas_call | solution.py:283
  94.4 0.8 collective-permute-start.30
  95.2 1.2 collective-permute-done.26.refs_1_
  96.5 2.0 %collective-permute-start.27 = (bf16[1024,128]{1,0:T(8,128)(2,1)S(1)}, bf16[1024,128]{1,0:T(8,128)(2,1)S(1)}, u32[]{:S(2)}, u32[]{:S(2)}) collective-permute-start(bf16[1024,128]{1,0:T(8,128)(2,1)S(1)} %shard_map.112.refs_10_), channel_id=1, source_target_pairs={{0,8},{1,9},{2,10},{3,11},{4,12},{5,13},{6,14},{7,15},{8,0},{9,1},... | collective-permute-start | bytes 786440 | tf_op jit(solution)/shard_map/ppermute | solution.py:421
  98.5 3.5 %collective-permute-done.33.refs_2_ = bf16[128,1024]{1,0:T(8,128)(2,1)S(1)} collective-permute-done((bf16[128,1024]{1,0:T(8,128)(2,1)S(1)}, bf16[128,1024]{1,0:T(8,128)(2,1)S(1)}, u32[]{:S(2)}, u32[]{:S(2)}) %collective-permute-start.33) | collective-permute-done | bytes 262176 | tf_op jit(solution)/shard_map/ppermute | solution.py:421
  102.1 4.3 %shard_map.115 = (bf16[1024,128]{1,0:T(8,128)(2,1)S(1)}, bf16[1024,128]{1,0:T(8,128)(2,1)S(1)}) custom-call(s32[6]{0:T(128)S(1)} %stack.42.place_ref.refs_0_, bf16[128,1024]{1,0:T(8,128)(2,1)S(1)} %collective-permute-done.32.refs_1_, bf16[128,1024]{1,0:T(8,128)(2,1)S(1)} %collective-permute-done.33.refs_2_, ...), custom_call_target="tpu_custom_call" | custom-call | flops 2214592512 | bytes 9699328 | tf_op jit(solution)/shard_map/pallas_call | solution.py:283
  106.3 1.5 %collective-permute-start.34 = (bf16[1024,128]{1,0:T(8,128)(2,1)S(1)}, bf16[1024,128]{1,0:T(8,128)(2,1)S(1)}, u32[]{:S(2)}, u32[]{:S(2)}) collective-permute-start(bf16[1024,128]{1,0:T(8,128)(2,1)S(1)} %get-tuple-element.123), channel_id=1, source_target_pairs={{0,2},{1,3},{2,0},{3,1},{4,6},{5,7},{6,4},{7,5},{8,10},{9,11},{10,... | collective-permute-start | bytes 786440 | tf_op jit(solution)/shard_map/ppermute | solution.py:421
  107.9 0.6 collective-permute-start.36
  108.5 1.7 %collective-permute-start.31 = (bf16[1024,128]{1,0:T(8,128)(2,1)S(1)}, bf16[1024,128]{1,0:T(8,128)(2,1)S(1)}, u32[]{:S(2)}, u32[]{:S(2)}) collective-permute-start(bf16[1024,128]{1,0:T(8,128)(2,1)S(1)} %shard_map.114), channel_id=1, source_target_pairs={{0,12},{1,13},{2,14},{3,15},{4,8},{5,9},{6,10},{7,11},{8,4},{9,5},... | collective-permute-start | bytes 786440 | tf_op jit(solution)/shard_map/ppermute | solution.py:421
  110.2 4.1 %collective-permute-done.34.refs_1_ = bf16[1024,128]{1,0:T(8,128)(2,1)S(1)} collective-permute-done((bf16[1024,128]{1,0:T(8,128)(2,1)S(1)}, bf16[1024,128]{1,0:T(8,128)(2,1)S(1)}, u32[]{:S(2)}, u32[]{:S(2)}) %collective-permute-start.34) | collective-permute-done | bytes 262176 | tf_op jit(solution)/shard_map/ppermute | solution.py:421
  114.4 1.7 %collective-permute-start.35 = (bf16[1024,128]{1,0:T(8,128)(2,1)S(1)}, bf16[1024,128]{1,0:T(8,128)(2,1)S(1)}, u32[]{:S(2)}, u32[]{:S(2)}) collective-permute-start(bf16[1024,128]{1,0:T(8,128)(2,1)S(1)} %shard_map.116), channel_id=1, source_target_pairs={{0,4},{1,5},{2,6},{3,7},{4,0},{5,1},{6,2},{7,3},{8,12},{9,13},{10,... | collective-permute-start | bytes 786440 | tf_op jit(solution)/shard_map/ppermute | solution.py:421
  116.0 1.1 collective-permute-done.36.refs_4_
  117.1 2.1 %collective-permute-done.31.refs_2_ = bf16[1024,128]{1,0:T(8,128)(2,1)S(1)} collective-permute-done((bf16[1024,128]{1,0:T(8,128)(2,1)S(1)}, bf16[1024,128]{1,0:T(8,128)(2,1)S(1)}, u32[]{:S(2)}, u32[]{:S(2)}) %collective-permute-start.31) | collective-permute-done | bytes 262176 | tf_op jit(solution)/shard_map/ppermute | solution.py:421
  119.2 2.8 %collective-permute-done.35.refs_3_ = bf16[1024,128]{1,0:T(8,128)(2,1)S(1)} collective-permute-done((bf16[1024,128]{1,0:T(8,128)(2,1)S(1)}, bf16[1024,128]{1,0:T(8,128)(2,1)S(1)}, u32[]{:S(2)}, u32[]{:S(2)}) %collective-permute-start.35) | collective-permute-done | bytes 262176 | tf_op jit(solution)/shard_map/ppermute | solution.py:421
  122.0 1.0 shard_map.117
  (52 shorter events, 2.4 us)
Async XLA Ops:
  0.0 13.8 %collective-permute-start.3 = (bf16[128,1024]{1,0:T(8,128)(2,1)}, bf16[128,1024]{1,0:T(8,128)(2,1)S(1)}, u32[]{:S(2)}, u32[]{:S(2)}) collective-permute-start(bf16[128,1024]{1,0:T(8,128)(2,1)} %tokens_ref.2), channel_id=1, source_target_pairs={{0,16},{16,0},{1,17},{17,1},{2,18},{18,2},{3,19},{19,3},{4,20},{20... | collective-permute-start | bytes 786440 | tf_op jit(solution)/shard_map/ppermute | solution.py:418
  2.9 10.9 %collective-permute-start.4 = (bf16[128,1024]{1,0:T(8,128)(2,1)}, bf16[128,1024]{1,0:T(8,128)(2,1)S(1)}, u32[]{:S(2)}, u32[]{:S(2)}) collective-permute-start(bf16[128,1024]{1,0:T(8,128)(2,1)} %tokens_ref.2), channel_id=1, source_target_pairs={{0,2},{1,3},{2,0},{3,1},{4,6},{5,7},{6,4},{7,5},{8,10},{9,11},{10,... | collective-permute-start | bytes 786440 | tf_op jit(solution)/shard_map/ppermute | solution.py:421
  4.5 0.9 copy-start.5
  5.5 0.8 copy-start.6
  7.3 6.5 %collective-permute-start.1 = (bf16[32,1024]{1,0:T(8,128)(2,1)S(1)}, bf16[32,1024]{1,0:T(8,128)(2,1)S(1)}, u32[]{:S(2)}, u32[]{:S(2)}) collective-permute-start(bf16[32,1024]{1,0:T(8,128)(2,1)S(1)} %get-tuple-element.67), channel_id=1, source_target_pairs={{0,2},{1,3},{2,0},{3,1},{4,6},{5,7},{6,4},{7,5},{8,10},{9,11},{10,... | collective-permute-start | bytes 196616 | tf_op jit(solution)/shard_map/ppermute | solution.py:421
  7.8 5.9 %collective-permute-start.2 = (bf16[32,1024]{1,0:T(8,128)(2,1)S(1)}, bf16[32,1024]{1,0:T(8,128)(2,1)S(1)}, u32[]{:S(2)}, u32[]{:S(2)}) collective-permute-start(bf16[32,1024]{1,0:T(8,128)(2,1)S(1)} %get-tuple-element.68), channel_id=1, source_target_pairs={{0,18},{1,19},{2,16},{3,17},{4,22},{5,23},{6,20},{7,21},{8,26},{9,... | collective-permute-start | bytes 196616 | tf_op jit(solution)/shard_map/ppermute | solution.py:451
  9.3 4.4 %collective-permute-start = (bf16[32,1024]{1,0:T(8,128)(2,1)S(1)}, bf16[32,1024]{1,0:T(8,128)(2,1)S(1)}, u32[]{:S(2)}, u32[]{:S(2)}) collective-permute-start(bf16[32,1024]{1,0:T(8,128)(2,1)S(1)} %get-tuple-element.66), channel_id=1, source_target_pairs={{0,16},{16,0},{1,17},{17,1},{2,18},{18,2},{3,19},{19,3},{4,20},{20... | collective-permute-start | bytes 196616 | tf_op jit(solution)/shard_map/ppermute | solution.py:418
  13.8 15.7 %collective-permute-start.7 = (bf16[704,1024]{1,0:T(8,128)(2,1)}, bf16[704,1024]{1,0:T(8,128)(2,1)S(1)}, u32[]{:S(2)}, u32[]{:S(2)}) collective-permute-start(bf16[704,1024]{1,0:T(8,128)(2,1)} %bitcast.23), channel_id=1, source_target_pairs={{0,1},{1,0},{2,3},{3,2},{4,5},{5,4},{6,7},{7,6},{8,9},{9,8},{10,11... | collective-permute-start | bytes 4325384 | tf_op jit(solution)/shard_map/ppermute | solution.py:421
  13.9 15.6 %collective-permute-start.8 = (bf16[704,1024]{1,0:T(8,128)(2,1)}, bf16[704,1024]{1,0:T(8,128)(2,1)S(1)}, u32[]{:S(2)}, u32[]{:S(2)}) collective-permute-start(bf16[704,1024]{1,0:T(8,128)(2,1)} %bitcast.25), channel_id=1, source_target_pairs={{0,1},{1,0},{2,3},{3,2},{4,5},{5,4},{6,7},{7,6},{8,9},{9,8},{10,11... | collective-permute-start | bytes 4325384 | tf_op jit(solution)/shard_map/ppermute | solution.py:421
  14.4 14.9 %collective-permute-start.5 = (bf16[4,32,1024]{2,1,0:T(8,128)(2,1)S(1)}, bf16[4,32,1024]{2,1,0:T(8,128)(2,1)S(1)}, u32[]{:S(2)}, u32[]{:S(2)}) collective-permute-start(bf16[4,32,1024]{2,1,0:T(8,128)(2,1)S(1)} %pad_maximum_fusion.refs_6_), channel_id=1, source_target_pairs={{0,8},{1,9},{2,10},{3,11},{4,12},{5,13},{6,14},{7,15},{8,0},{9,1},... | collective-permute-start | bytes 786440 | tf_op jit(solution)/shard_map/ppermute | solution.py:421
  17.0 12.5 %collective-permute-start.6 = (bf16[4,32,1024]{2,1,0:T(8,128)(2,1)S(1)}, bf16[4,32,1024]{2,1,0:T(8,128)(2,1)S(1)}, u32[]{:S(2)}, u32[]{:S(2)}) collective-permute-start(bf16[4,32,1024]{2,1,0:T(8,128)(2,1)S(1)} %pad_maximum_fusion.refs_6_), channel_id=1, source_target_pairs={{0,4},{1,5},{2,6},{3,7},{4,0},{5,1},{6,2},{7,3},{8,12},{9,13},{10,... | collective-permute-start | bytes 786440 | tf_op jit(solution)/shard_map/ppermute | solution.py:421
  18.6 10.9 %collective-permute-start.9 = (bf16[128,1024]{1,0:T(8,128)(2,1)S(1)}, bf16[128,1024]{1,0:T(8,128)(2,1)S(1)}, u32[]{:S(2)}, u32[]{:S(2)}) collective-permute-start(bf16[128,1024]{1,0:T(8,128)(2,1)S(1)} %collective-permute-done.3.refs_3_), channel_id=1, source_target_pairs={{0,2},{1,3},{2,0},{3,1},{4,6},{5,7},{6,4},{7,5},{8,10},{9,11},{10,... | collective-permute-start | bytes 786440 | tf_op jit(solution)/shard_map/ppermute | solution.py:421
  20.1 0.9 copy-start.3
  21.0 0.7 copy-start.7
  21.7 0.7 copy-start.8
  22.4 0.7 copy-start.9
  29.5 11.8 %collective-permute-start.17 = (bf16[704,1024]{1,0:T(8,128)(2,1)}, bf16[704,1024]{1,0:T(8,128)(2,1)S(1)}, u32[]{:S(2)}, u32[]{:S(2)}) collective-permute-start(bf16[704,1024]{1,0:T(8,128)(2,1)} %bitcast.21), channel_id=1, source_target_pairs={{0,1},{1,0},{2,3},{3,2},{4,5},{5,4},{6,7},{7,6},{8,9},{9,8},{10,11... | collective-permute-start | bytes 4325384 | tf_op jit(solution)/shard_map/ppermute | solution.py:421
  29.6 9.8 %collective-permute-start.13 = (bf16[4,32,1024]{2,1,0:T(8,128)(2,1)S(1)}, bf16[4,32,1024]{2,1,0:T(8,128)(2,1)S(1)}, u32[]{:S(2)}, u32[]{:S(2)}) collective-permute-start(bf16[4,32,1024]{2,1,0:T(8,128)(2,1)S(1)} %collective-permute-done.5.refs_10_), channel_id=1, source_target_pairs={{0,4},{1,5},{2,6},{3,7},{4,0},{5,1},{6,2},{7,3},{8,12},{9,13},{10,... | collective-permute-start | bytes 786440 | tf_op jit(solution)/shard_map/ppermute | solution.py:421
  31.1 3.7 %collective-permute-start.15 = (f32[16,128]{1,0:T(8,128)S(1)}, f32[16,128]{1,0:T(8,128)S(1)}, u32[]{:S(2)}, u32[]{:S(2)}) collective-permute-start(f32[16,128]{1,0:T(8,128)S(1)} %get-tuple-element.85.first_ref), channel_id=1, source_target_pairs={{0,2},{1,3},{2,0},{3,1},{4,6},{5,7},{6,4},{7,5},{8,10},{9,11},{10,... | collective-permute-start | bytes 24584 | tf_op jit(solution)/shard_map/ppermute | solution.py:421
  34.7 4.6 %collective-permute-start.16 = (f32[2,16,128]{2,1,0:T(8,128)S(1)}, f32[2,16,128]{2,1,0:T(8,128)S(1)}, u32[]{:S(2)}, u32[]{:S(2)}) collective-permute-start(f32[2,16,128]{2,1,0:T(8,128)S(1)} %shard_map.102.first_ref), channel_id=1, source_target_pairs={{0,8},{1,9},{2,10},{3,11},{4,12},{5,13},{6,14},{7,15},{8,0},{9,1},... | collective-permute-start | bytes 49160 | tf_op jit(solution)/shard_map/ppermute | solution.py:421
  37.1 2.8 %collective-permute-start.10 = (bf16[4,32,1024]{2,1,0:T(8,128)(2,1)S(1)}, bf16[4,32,1024]{2,1,0:T(8,128)(2,1)S(1)}, u32[]{:S(2)}, u32[]{:S(2)}) collective-permute-start(bf16[4,32,1024]{2,1,0:T(8,128)(2,1)S(1)} %pad_maximum_fusion.refs_6_), channel_id=1, source_target_pairs={{0,1},{1,0},{2,3},{3,2},{4,5},{5,4},{6,7},{7,6},{8,9},{9,8},{10,11... | collective-permute-start | bytes 786440 | tf_op jit(solution)/shard_map/ppermute | solution.py:421
  37.1 3.8 %collective-permute-start.12 = (bf16[4,32,1024]{2,1,0:T(8,128)(2,1)S(1)}, bf16[4,32,1024]{2,1,0:T(8,128)(2,1)S(1)}, u32[]{:S(2)}, u32[]{:S(2)}) collective-permute-start(bf16[4,32,1024]{2,1,0:T(8,128)(2,1)S(1)} %collective-permute-done.5.refs_10_), channel_id=1, source_target_pairs={{0,1},{1,0},{2,3},{3,2},{4,5},{5,4},{6,7},{7,6},{8,9},{9,8},{10,11... | collective-permute-start | bytes 786440 | tf_op jit(solution)/shard_map/ppermute | solution.py:421
  39.4 1.5 %collective-permute-start.11 = (bf16[4,32,1024]{2,1,0:T(8,128)(2,1)S(1)}, bf16[4,32,1024]{2,1,0:T(8,128)(2,1)S(1)}, u32[]{:S(2)}, u32[]{:S(2)}) collective-permute-start(bf16[4,32,1024]{2,1,0:T(8,128)(2,1)S(1)} %collective-permute-done.6.refs_8_), channel_id=1, source_target_pairs={{0,1},{1,0},{2,3},{3,2},{4,5},{5,4},{6,7},{7,6},{8,9},{9,8},{10,11... | collective-permute-start | bytes 786440 | tf_op jit(solution)/shard_map/ppermute | solution.py:421
  39.4 1.9 %collective-permute-start.14 = (bf16[4,32,1024]{2,1,0:T(8,128)(2,1)S(1)}, bf16[4,32,1024]{2,1,0:T(8,128)(2,1)S(1)}, u32[]{:S(2)}, u32[]{:S(2)}) collective-permute-start(bf16[4,32,1024]{2,1,0:T(8,128)(2,1)S(1)} %collective-permute-done.13.refs_12_), channel_id=1, source_target_pairs={{0,1},{1,0},{2,3},{3,2},{4,5},{5,4},{6,7},{7,6},{8,9},{9,8},{10,11... | collective-permute-start | bytes 786440 | tf_op jit(solution)/shard_map/ppermute | solution.py:421
  41.3 7.4 %copy-start = (bf16[1,704,1024]{2,1,0:T(8,128)(2,1)S(1)}, bf16[1,704,1024]{2,1,0:T(8,128)(2,1)}, u32[]{:S(2)}) copy-start(bf16[1,704,1024]{2,1,0:T(8,128)(2,1)} %param.19) | copy-start | bytes 4325380
  41.3 7.4 %copy-start.1 = (bf16[1,1024,704]{1,2,0:T(8,128)(2,1)S(1)}, bf16[1,1024,704]{1,2,0:T(8,128)(2,1)}, u32[]{:S(2)}) copy-start(bf16[1,1024,704]{1,2,0:T(8,128)(2,1)} %param.17) | copy-start | bytes 4325380
  41.3 7.4 %copy-start.2 = (bf16[1,1024,704]{1,2,0:T(8,128)(2,1)S(1)}, bf16[1,1024,704]{1,2,0:T(8,128)(2,1)}, u32[]{:S(2)}) copy-start(bf16[1,1024,704]{1,2,0:T(8,128)(2,1)} %param.18) | copy-start | bytes 4325380
  45.3 8.4 %collective-permute-start.18 = (bf16[2,64,1024]{2,1,0:T(8,128)(2,1)S(1)}, bf16[2,64,1024]{2,1,0:T(8,128)(2,1)S(1)}, u32[]{:S(2)}, u32[]{:S(2)}) collective-permute-start(bf16[2,64,1024]{2,1,0:T(8,128)(2,1)S(1)} %get-tuple-element.88), channel_id=1, source_target_pairs={{0,2},{1,3},{2,0},{3,1},{4,6},{5,7},{6,4},{7,5},{8,10},{9,11},{10,... | collective-permute-start | bytes 786440 | tf_op jit(solution)/shard_map/ppermute | solution.py:421
  46.9 8.1 %collective-permute-start.19 = (bf16[2,64,1024]{2,1,0:T(8,128)(2,1)S(1)}, bf16[2,64,1024]{2,1,0:T(8,128)(2,1)S(1)}, u32[]{:S(2)}, u32[]{:S(2)}) collective-permute-start(bf16[2,64,1024]{2,1,0:T(8,128)(2,1)S(1)} %get-tuple-element.89), channel_id=1, source_target_pairs={{0,16},{16,0},{1,17},{17,1},{2,18},{18,2},{3,19},{19,3},{4,20},{20... | collective-permute-start | bytes 786440 | tf_op jit(solution)/shard_map/ppermute | solution.py:418
  47.4 3.9 %collective-permute-start.20 = (f32[2,2,16,128]{3,2,1,0:T(8,128)S(1)}, f32[2,2,16,128]{3,2,1,0:T(8,128)S(1)}, u32[]{:S(2)}, u32[]{:S(2)}) collective-permute-start(f32[2,2,16,128]{3,2,1,0:T(8,128)S(1)} %shard_map.103.refs_14_.refs_3_), channel_id=1, source_target_pairs={{0,4},{1,5},{2,6},{3,7},{4,0},{5,1},{6,2},{7,3},{8,12},{9,13},{10,... | collective-permute-start | bytes 98312 | tf_op jit(solution)/shard_map/ppermute | solution.py:421
  55.0 5.0 %collective-permute-start.22 = (bf16[64,1024]{1,0:T(8,128)(2,1)S(1)}, bf16[64,1024]{1,0:T(8,128)(2,1)S(1)}, u32[]{:S(2)}, u32[]{:S(2)}) collective-permute-start(bf16[64,1024]{1,0:T(8,128)(2,1)S(1)} %shard_map.107), channel_id=1, source_target_pairs={{0,2},{1,3},{2,0},{3,1},{4,6},{5,7},{6,4},{7,5},{8,10},{9,11},{10,... | collective-permute-start | bytes 393224 | tf_op jit(solution)/shard_map/ppermute | solution.py:421
  55.6 5.1 %copy-start.4 = (bf16[128,1024]{1,0:T(8,128)(2,1)S(1)}, bf16[128,1024]{1,0:T(8,128)(2,1)}, u32[]{:S(2)}) copy-start(bf16[128,1024]{1,0:T(8,128)(2,1)} %tokens_ref.2) | copy-start | bytes 786436
  55.6 5.1 %copy-start.10 = (f32[1024]{0:T(1024)S(1)}, f32[1024]{0:T(1024)}, u32[]{:S(2)}) copy-start(f32[1024]{0:T(1024)} %param.14) | copy-start | bytes 12292
  55.6 5.0 %collective-permute-start.21 = (bf16[64,1024]{1,0:T(8,128)(2,1)S(1)}, bf16[64,1024]{1,0:T(8,128)(2,1)S(1)}, u32[]{:S(2)}, u32[]{:S(2)}) collective-permute-start(bf16[64,1024]{1,0:T(8,128)(2,1)S(1)} %shard_map.106), channel_id=1, source_target_pairs={{0,16},{16,0},{1,17},{17,1},{2,18},{18,2},{3,19},{19,3},{4,20},{20... | collective-permute-start | bytes 393224 | tf_op jit(solution)/shard_map/ppermute | solution.py:418
  60.9 6.4 %collective-permute-start.23 = (bf16[128,1024]{1,0:T(8,128)(2,1)S(1)}, bf16[128,1024]{1,0:T(8,128)(2,1)S(1)}, u32[]{:S(2)}, u32[]{:S(2)}) collective-permute-start(bf16[128,1024]{1,0:T(8,128)(2,1)S(1)} %get-tuple-element.121.refs_1_), channel_id=1, source_target_pairs={{0,2},{1,3},{2,0},{3,1},{4,6},{5,7},{6,4},{7,5},{8,10},{9,11},{10,... | collective-permute-start | bytes 786440 | tf_op jit(solution)/shard_map/ppermute | solution.py:421
  62.5 12.3 %collective-permute-start.24 = (bf16[128,1024]{1,0:T(8,128)(2,1)S(1)}, bf16[128,1024]{1,0:T(8,128)(2,1)S(1)}, u32[]{:S(2)}, u32[]{:S(2)}) collective-permute-start(bf16[128,1024]{1,0:T(8,128)(2,1)S(1)} %get-tuple-element.121.refs_1_), channel_id=1, source_target_pairs={{0,8},{1,9},{2,10},{3,11},{4,12},{5,13},{6,14},{7,15},{8,0},{9,1},... | collective-permute-start | bytes 786440 | tf_op jit(solution)/shard_map/ppermute | solution.py:421
  74.8 7.4 %collective-permute-start.28 = (bf16[128,1024]{1,0:T(8,128)(2,1)S(1)}, bf16[128,1024]{1,0:T(8,128)(2,1)S(1)}, u32[]{:S(2)}, u32[]{:S(2)}) collective-permute-start(bf16[128,1024]{1,0:T(8,128)(2,1)S(1)} %collective-permute-done.24.refs_1_), channel_id=1, source_target_pairs={{0,4},{1,5},{2,6},{3,7},{4,0},{5,1},{6,2},{7,3},{8,12},{9,13},{10,... | collective-permute-start | bytes 786440 | tf_op jit(solution)/shard_map/ppermute | solution.py:421
  74.8 8.1 %collective-permute-start.25 = (bf16[128,1024]{1,0:T(8,128)(2,1)S(1)}, bf16[128,1024]{1,0:T(8,128)(2,1)S(1)}, u32[]{:S(2)}, u32[]{:S(2)}) collective-permute-start(bf16[128,1024]{1,0:T(8,128)(2,1)S(1)} %collective-permute-done.24.refs_1_), channel_id=1, source_target_pairs={{0,2},{1,3},{2,0},{3,1},{4,6},{5,7},{6,4},{7,5},{8,10},{9,11},{10,... | collective-permute-start | bytes 786440 | tf_op jit(solution)/shard_map/ppermute | solution.py:421
  82.2 6.6 %collective-permute-start.32 = (bf16[128,1024]{1,0:T(8,128)(2,1)S(1)}, bf16[128,1024]{1,0:T(8,128)(2,1)S(1)}, u32[]{:S(2)}, u32[]{:S(2)}) collective-permute-start(bf16[128,1024]{1,0:T(8,128)(2,1)S(1)} %get-tuple-element.121.refs_1_), channel_id=1, source_target_pairs={{0,4},{1,5},{2,6},{3,7},{4,0},{5,1},{6,2},{7,3},{8,12},{9,13},{10,... | collective-permute-start | bytes 786440 | tf_op jit(solution)/shard_map/ppermute | solution.py:421
  82.5 7.6 %collective-permute-start.29 = (bf16[128,1024]{1,0:T(8,128)(2,1)S(1)}, bf16[128,1024]{1,0:T(8,128)(2,1)S(1)}, u32[]{:S(2)}, u32[]{:S(2)}) collective-permute-start(bf16[128,1024]{1,0:T(8,128)(2,1)S(1)} %collective-permute-done.28.refs_1_), channel_id=1, source_target_pairs={{0,2},{1,3},{2,0},{3,1},{4,6},{5,7},{6,4},{7,5},{8,10},{9,11},{10,... | collective-permute-start | bytes 786440 | tf_op jit(solution)/shard_map/ppermute | solution.py:421
  87.1 9.3 %collective-permute-start.26 = (bf16[1024,128]{1,0:T(8,128)(2,1)S(1)}, bf16[1024,128]{1,0:T(8,128)(2,1)S(1)}, u32[]{:S(2)}, u32[]{:S(2)}) collective-permute-start(bf16[1024,128]{1,0:T(8,128)(2,1)S(1)} %get-tuple-element.117.refs_10_), channel_id=1, source_target_pairs={{0,2},{1,3},{2,0},{3,1},{4,6},{5,7},{6,4},{7,5},{8,10},{9,11},{10,... | collective-permute-start | bytes 786440 | tf_op jit(solution)/shard_map/ppermute | solution.py:421
  88.9 13.2 %collective-permute-start.33 = (bf16[128,1024]{1,0:T(8,128)(2,1)S(1)}, bf16[128,1024]{1,0:T(8,128)(2,1)S(1)}, u32[]{:S(2)}, u32[]{:S(2)}) collective-permute-start(bf16[128,1024]{1,0:T(8,128)(2,1)S(1)} %collective-permute-done.32.refs_1_), channel_id=1, source_target_pairs={{0,2},{1,3},{2,0},{3,1},{4,6},{5,7},{6,4},{7,5},{8,10},{9,11},{10,... | collective-permute-start | bytes 786440 | tf_op jit(solution)/shard_map/ppermute | solution.py:421
  94.4 14.0 %collective-permute-start.30 = (bf16[1024,128]{1,0:T(8,128)(2,1)S(1)}, bf16[1024,128]{1,0:T(8,128)(2,1)S(1)}, u32[]{:S(2)}, u32[]{:S(2)}) collective-permute-start(bf16[1024,128]{1,0:T(8,128)(2,1)S(1)} %get-tuple-element.120.refs_11_), channel_id=1, source_target_pairs={{0,2},{1,3},{2,0},{3,1},{4,6},{5,7},{6,4},{7,5},{8,10},{9,11},{10,... | collective-permute-start | bytes 786440 | tf_op jit(solution)/shard_map/ppermute | solution.py:421
  96.5 11.9 %collective-permute-start.27 = (bf16[1024,128]{1,0:T(8,128)(2,1)S(1)}, bf16[1024,128]{1,0:T(8,128)(2,1)S(1)}, u32[]{:S(2)}, u32[]{:S(2)}) collective-permute-start(bf16[1024,128]{1,0:T(8,128)(2,1)S(1)} %shard_map.112.refs_10_), channel_id=1, source_target_pairs={{0,8},{1,9},{2,10},{3,11},{4,12},{5,13},{6,14},{7,15},{8,0},{9,1},... | collective-permute-start | bytes 786440 | tf_op jit(solution)/shard_map/ppermute | solution.py:421
  106.3 8.0 %collective-permute-start.34 = (bf16[1024,128]{1,0:T(8,128)(2,1)S(1)}, bf16[1024,128]{1,0:T(8,128)(2,1)S(1)}, u32[]{:S(2)}, u32[]{:S(2)}) collective-permute-start(bf16[1024,128]{1,0:T(8,128)(2,1)S(1)} %get-tuple-element.123), channel_id=1, source_target_pairs={{0,2},{1,3},{2,0},{3,1},{4,6},{5,7},{6,4},{7,5},{8,10},{9,11},{10,... | collective-permute-start | bytes 786440 | tf_op jit(solution)/shard_map/ppermute | solution.py:421
  107.9 9.2 %collective-permute-start.36 = (bf16[1024,128]{1,0:T(8,128)(2,1)S(1)}, bf16[1024,128]{1,0:T(8,128)(2,1)S(1)}, u32[]{:S(2)}, u32[]{:S(2)}) collective-permute-start(bf16[1024,128]{1,0:T(8,128)(2,1)S(1)} %get-tuple-element.124.refs_10_), channel_id=1, source_target_pairs={{0,2},{1,3},{2,0},{3,1},{4,6},{5,7},{6,4},{7,5},{8,10},{9,11},{10,... | collective-permute-start | bytes 786440 | tf_op jit(solution)/shard_map/ppermute | solution.py:421
  108.5 10.7 %collective-permute-start.31 = (bf16[1024,128]{1,0:T(8,128)(2,1)S(1)}, bf16[1024,128]{1,0:T(8,128)(2,1)S(1)}, u32[]{:S(2)}, u32[]{:S(2)}) collective-permute-start(bf16[1024,128]{1,0:T(8,128)(2,1)S(1)} %shard_map.114), channel_id=1, source_target_pairs={{0,12},{1,13},{2,14},{3,15},{4,8},{5,9},{6,10},{7,11},{8,4},{9,5},... | collective-permute-start | bytes 786440 | tf_op jit(solution)/shard_map/ppermute | solution.py:421
  114.4 7.7 %collective-permute-start.35 = (bf16[1024,128]{1,0:T(8,128)(2,1)S(1)}, bf16[1024,128]{1,0:T(8,128)(2,1)S(1)}, u32[]{:S(2)}, u32[]{:S(2)}) collective-permute-start(bf16[1024,128]{1,0:T(8,128)(2,1)S(1)} %shard_map.116), channel_id=1, source_target_pairs={{0,4},{1,5},{2,6},{3,7},{4,0},{5,1},{6,2},{7,3},{8,12},{9,13},{10,... | collective-permute-start | bytes 786440 | tf_op jit(solution)/shard_map/ppermute | solution.py:421
where the time goes:
time: 123 us
  waiting for transfers between devices  50.4 us (41%)
  starting transfers between devices  41.3 us (34%)
  Pallas kernels  26.2 us (21%)
  local copies, waits for them, and re-layouts  4.88 us (4%)
    ppermute x32, waiting for transfers between devices, swap_expert(): lax.ppermute(value, 'expert', [(e, e ^ mask) for e in range(expert_size)])  48.5 us
    ppermute x32, starting transfers between devices, swap_expert(): lax.ppermute(value, 'expert', [(e, e ^ mask) for e in range(expert_size)])  33.5 us
    pallas_call x4, Pallas kernels, expert_call(): pl.pallas_call(functools.partial(expert_kernel, tiles, pick), out_shape=(...  17 us
    ppermute x4, starting transfers between devices, swap_pair(): return lax.ppermute(value, 'fsdp', [(f, f ^ 1) for f in range(fsdp_size)])  6.37 us
    unnamed x22, local copies, waits for them, and re-layouts  4.8 us
    pallas_call x1, Pallas kernels, attention_call(): pl.pallas_call(functools.partial(attention_kernel, count, len(pieces)), o...  4.01 us
    pallas_call x2, Pallas kernels, load_call(): pl.pallas_call(load_kernel, out_shape=(jax.ShapeDtypeStruct(gate.shape, g...  2.71 us
  transfers between devices with their start and end apart: 37, of which 22 were waited for; matrix products, arithmetic and copies ran while one was open for 0% of the time, Pallas kernels for 17%

commit v1 on v0

--- a/solution.py
+++ b/solution.py
@@ -512,27 +512,34 @@
     for step, mask in enumerate(order):
         low = mask & -mask
         source = arrivals[mask ^ low]
-        if mask == 1 and step >= 2:
-            source, _ = hold((source, block))
-        block = swap_layer(source, low)
-        if step == 1:
-            block, _ = hold((block, crossings[0]))
+        if mask == 1:
+            source, across, _ = hold((source, own_across, block))
+            block, across = swap_layer(source, 1), swap_layer(across, 1)
+        else:
+            block = swap_layer(source, low)
+            if step == 1:
+                block, _ = hold((block, crossings[0]))
+            across = swap_side(block)
+        if step == 0:
+            own_across = across
         arrivals[mask] = block
         own, crossing = expert_call(
             place,
-            [block, swap_side(block)],
+            [block, across],
             (scale_maps[mask % 2], [mask >> bit & 1 for bit in range(1, layers.bit_length() - 1)]),
             [*own_expert, *other_expert],
             (sums[step - 3 : step - 2] if step >= 3 else []) + crossings[-1:],
         )
         crossings.append(crossing)
         if step == 0:
-            first = own
+            finals.append(own)
+        elif mask == 1:
+            finals.append(swap_layer(own, 1))
         else:
-            sums.append(sum_call([own, swap_side(crossing)], finals[:1] if step == 2 else []))
+            sums.append(sum_call([own, swap_side(crossing)], finals[1:2] if step == 2 else []))
             finals.append(swap_layer(sums[-1], mask))
-    crossing, _ = hold((crossings[0], crossings[-1]))
-    return mix_call(hidden_stream, [first, *finals, swap_side(crossing)])
+    crossing = sum_call([crossings[0], swap_layer(crossings[-1], 1)])
+    return mix_call(hidden_stream, [*finals, swap_side(crossing)])
 
 
 def solution(mesh):

time: 123 us -> 131 us (1.065)
  waiting for transfers between devices: 50.4 us -> 61.7 us
  starting transfers between devices: 41.3 us -> 37.9 us
    ppermute x32, waiting for transfers between devices: 48.5 us -> 59.8 us  [swap_expert(): lax.ppermute(value, 'expert', [(e, e ^ mask) for e in range(expert_size)])]
    ppermute x32, starting transfers between devices: 33.5 us -> 30.1 us  [swap_expert(): lax.ppermute(value, 'expert', [(e, e ^ mask) for e in range(expert_size)])]
  transfers between devices with their start and end apart: 37 -> 37, of which waited for: 22 -> 21; matrix products, arithmetic and copies ran while one was open for 0% -> 0% of each run, Pallas kernels for 17% -> 13%
where the time goes in v1:
time: 131 us
  waiting for transfers between devices  61.7 us (47%)
  starting transfers between devices  37.9 us (29%)
  Pallas kernels  26.2 us (20%)
  local copies, waits for them, and re-layouts  4.88 us (4%)
    ppermute x32, waiting for transfers between devices, swap_expert(): lax.ppermute(value, 'expert', [(e, e ^ mask) for e in range(expert_size)])  59.8 us
    ppermute x32, starting transfers between devices, swap_expert(): lax.ppermute(value, 'expert', [(e, e ^ mask) for e in range(expert_size)])  30.1 us
    pallas_call x4, Pallas kernels, expert_call(): pl.pallas_call(functools.partial(expert_kernel, tiles, pick), out_shape=(...  17 us
    ppermute x4, starting transfers between devices, swap_pair(): return lax.ppermute(value, 'fsdp', [(f, f ^ 1) for f in range(fsdp_size)])  6.37 us
    unnamed x22, local copies, waits for them, and re-layouts  4.8 us
    pallas_call x1, Pallas kernels, attention_call(): pl.pallas_call(functools.partial(attention_kernel, count, len(pieces)), o...  4.01 us
    pallas_call x2, Pallas kernels, load_call(): pl.pallas_call(load_kernel, out_shape=(jax.ShapeDtypeStruct(gate.shape, g...  2.71 us
  transfers between devices with their start and end apart: 37, of which 21 were waited for; matrix products, arithmetic and copies ran while one was open for 0% of the time, Pallas kernels for 13%

profile of v1, /device:TPU:0, one launch (start us, length us, event | category | flops | bytes accessed | tf_op | source)
XLA Modules:
  0.0 130.9 jit_solution(3838335931545015375)
XLA Ops:
  0.0 2.9 %collective-permute-start.3 = (bf16[128,1024]{1,0:T(8,128)(2,1)}, bf16[128,1024]{1,0:T(8,128)(2,1)S(1)}, u32[]{:S(2)}, u32[]{:S(2)}) collective-permute-start(bf16[128,1024]{1,0:T(8,128)(2,1)} %tokens_ref.2), channel_id=1, source_target_pairs={{0,16},{16,0},{1,17},{17,1},{2,18},{18,2},{3,19},{19,3},{4,20},{20... | collective-permute-start | bytes 786440 | tf_op jit(solution)/shard_map/ppermute | solution.py:418
  2.9 1.5 %collective-permute-start.4 = (bf16[128,1024]{1,0:T(8,128)(2,1)}, bf16[128,1024]{1,0:T(8,128)(2,1)S(1)}, u32[]{:S(2)}, u32[]{:S(2)}) collective-permute-start(bf16[128,1024]{1,0:T(8,128)(2,1)} %tokens_ref.2), channel_id=1, source_target_pairs={{0,2},{1,3},{2,0},{3,1},{4,6},{5,7},{6,4},{7,5},{8,10},{9,11},{10,... | collective-permute-start | bytes 786440 | tf_op jit(solution)/shard_map/ppermute | solution.py:421
  4.5 0.9 copy-done.5
  5.5 0.8 copy-done.6
  6.3 0.9 shard_map.100
  7.3 0.6 collective-permute-start.1
  7.8 1.5 %collective-permute-start.2 = (bf16[32,1024]{1,0:T(8,128)(2,1)S(1)}, bf16[32,1024]{1,0:T(8,128)(2,1)S(1)}, u32[]{:S(2)}, u32[]{:S(2)}) collective-permute-start(bf16[32,1024]{1,0:T(8,128)(2,1)S(1)} %get-tuple-element.68), channel_id=1, source_target_pairs={{0,18},{1,19},{2,16},{3,17},{4,22},{5,23},{6,20},{7,21},{8,26},{9,... | collective-permute-start | bytes 196616 | tf_op jit(solution)/shard_map/ppermute | solution.py:451
  9.3 1.5 %collective-permute-start = (bf16[32,1024]{1,0:T(8,128)(2,1)S(1)}, bf16[32,1024]{1,0:T(8,128)(2,1)S(1)}, u32[]{:S(2)}, u32[]{:S(2)}) collective-permute-start(bf16[32,1024]{1,0:T(8,128)(2,1)S(1)} %get-tuple-element.66), channel_id=1, source_target_pairs={{0,16},{16,0},{1,17},{17,1},{2,18},{18,2},{3,19},{19,3},{4,20},{20... | collective-permute-start | bytes 196616 | tf_op jit(solution)/shard_map/ppermute | solution.py:418
  10.8 2.9 %collective-permute-done.1 = bf16[32,1024]{1,0:T(8,128)(2,1)S(1)} collective-permute-done((bf16[32,1024]{1,0:T(8,128)(2,1)S(1)}, bf16[32,1024]{1,0:T(8,128)(2,1)S(1)}, u32[]{:S(2)}, u32[]{:S(2)}) %collective-permute-start.1) | collective-permute-done | bytes 65568 | tf_op jit(solution)/shard_map/ppermute | solution.py:421
  13.9 0.5 collective-permute-start.8
  14.4 2.6 %collective-permute-start.5 = (bf16[4,32,1024]{2,1,0:T(8,128)(2,1)S(1)}, bf16[4,32,1024]{2,1,0:T(8,128)(2,1)S(1)}, u32[]{:S(2)}, u32[]{:S(2)}) collective-permute-start(bf16[4,32,1024]{2,1,0:T(8,128)(2,1)S(1)} %pad_maximum_fusion.refs_6_), channel_id=1, source_target_pairs={{0,8},{1,9},{2,10},{3,11},{4,12},{5,13},{6,14},{7,15},{8,0},{9,1},... | collective-permute-start | bytes 786440 | tf_op jit(solution)/shard_map/ppermute | solution.py:421
  17.0 1.6 %collective-permute-start.6 = (bf16[4,32,1024]{2,1,0:T(8,128)(2,1)S(1)}, bf16[4,32,1024]{2,1,0:T(8,128)(2,1)S(1)}, u32[]{:S(2)}, u32[]{:S(2)}) collective-permute-start(bf16[4,32,1024]{2,1,0:T(8,128)(2,1)S(1)} %pad_maximum_fusion.refs_6_), channel_id=1, source_target_pairs={{0,4},{1,5},{2,6},{3,7},{4,0},{5,1},{6,2},{7,3},{8,12},{9,13},{10,... | collective-permute-start | bytes 786440 | tf_op jit(solution)/shard_map/ppermute | solution.py:421
  18.6 1.5 %collective-permute-start.9 = (bf16[128,1024]{1,0:T(8,128)(2,1)S(1)}, bf16[128,1024]{1,0:T(8,128)(2,1)S(1)}, u32[]{:S(2)}, u32[]{:S(2)}) collective-permute-start(bf16[128,1024]{1,0:T(8,128)(2,1)S(1)} %collective-permute-done.3.refs_3_), channel_id=1, source_target_pairs={{0,2},{1,3},{2,0},{3,1},{4,6},{5,7},{6,4},{7,5},{8,10},{9,11},{10,... | collective-permute-start | bytes 786440 | tf_op jit(solution)/shard_map/ppermute | solution.py:421
  20.1 0.9 copy-done.3
  21.0 0.7 copy-done.7
  21.7 0.7 copy-done.8
  22.4 0.7 copy-done.9
  23.1 6.2 %collective-permute-done.5.refs_10_ = bf16[4,32,1024]{2,1,0:T(8,128)(2,1)S(1)} collective-permute-done((bf16[4,32,1024]{2,1,0:T(8,128)(2,1)S(1)}, bf16[4,32,1024]{2,1,0:T(8,128)(2,1)S(1)}, u32[]{:S(2)}, u32[]{:S(2)}) %collective-permute-start.5) | collective-permute-done | bytes 262176 | tf_op jit(solution)/shard_map/ppermute | solution.py:421
  29.6 1.5 %collective-permute-start.13 = (bf16[4,32,1024]{2,1,0:T(8,128)(2,1)S(1)}, bf16[4,32,1024]{2,1,0:T(8,128)(2,1)S(1)}, u32[]{:S(2)}, u32[]{:S(2)}) collective-permute-start(bf16[4,32,1024]{2,1,0:T(8,128)(2,1)S(1)} %collective-permute-done.5.refs_10_), channel_id=1, source_target_pairs={{0,4},{1,5},{2,6},{3,7},{4,0},{5,1},{6,2},{7,3},{8,12},{9,13},{10,... | collective-permute-start | bytes 786440 | tf_op jit(solution)/shard_map/ppermute | solution.py:421
  31.1 1.5 %collective-permute-start.15 = (f32[16,128]{1,0:T(8,128)S(1)}, f32[16,128]{1,0:T(8,128)S(1)}, u32[]{:S(2)}, u32[]{:S(2)}) collective-permute-start(f32[16,128]{1,0:T(8,128)S(1)} %get-tuple-element.85.first_ref), channel_id=1, source_target_pairs={{0,2},{1,3},{2,0},{3,1},{4,6},{5,7},{6,4},{7,5},{8,10},{9,11},{10,... | collective-permute-start | bytes 24584 | tf_op jit(solution)/shard_map/ppermute | solution.py:421
  32.6 2.2 %collective-permute-done.15.second_ref = f32[16,128]{1,0:T(8,128)S(1)} collective-permute-done((f32[16,128]{1,0:T(8,128)S(1)}, f32[16,128]{1,0:T(8,128)S(1)}, u32[]{:S(2)}, u32[]{:S(2)}) %collective-permute-start.15) | collective-permute-done | bytes 8224 | tf_op jit(solution)/shard_map/ppermute | solution.py:421
  34.7 2.3 %collective-permute-start.16 = (f32[2,16,128]{2,1,0:T(8,128)S(1)}, f32[2,16,128]{2,1,0:T(8,128)S(1)}, u32[]{:S(2)}, u32[]{:S(2)}) collective-permute-start(f32[2,16,128]{2,1,0:T(8,128)S(1)} %shard_map.102.first_ref), channel_id=1, source_target_pairs={{0,8},{1,9},{2,10},{3,11},{4,12},{5,13},{6,14},{7,15},{8,0},{9,1},... | collective-permute-start | bytes 49160 | tf_op jit(solution)/shard_map/ppermute | solution.py:421
  37.1 0.5 collective-permute-start.12
  37.6 1.8 %collective-permute-done.16.second_ref = f32[2,16,128]{2,1,0:T(8,128)S(1)} collective-permute-done((f32[2,16,128]{2,1,0:T(8,128)S(1)}, f32[2,16,128]{2,1,0:T(8,128)S(1)}, u32[]{:S(2)}, u32[]{:S(2)}) %collective-permute-start.16) | collective-permute-done | bytes 16416 | tf_op jit(solution)/shard_map/ppermute | solution.py:421
  39.4 0.5 collective-permute-start.14
  39.9 1.0 collective-permute-done.11.refs_9_
  40.9 0.4 collective-permute-done.14.refs_13_
  41.3 4.0 %shard_map.104 = (bf16[2,64,1024]{2,1,0:T(8,128)(2,1)S(1)}, bf16[2,64,1024]{2,1,0:T(8,128)(2,1)S(1)}, bf16[2,64,1024]{2,1,0:T(8,128)(2,1)S(1)}, bf16[2,64,1024]{2,1,0:T(8,128)(2,1)S(1)}) custom-call(s32[6]{0:T(128)S(1)} %stack.42.place_ref.refs_0_, f32[1,1024]{1,0:T(1,128)S(1)} %get-tuple-element.71.refs_1_, ...), custom_call_target="tpu_custom_call" | custom-call | flops 1140850688 | bytes 4194304 | tf_op jit(solution)/shard_map/pallas_call | solution.py:171
  45.3 1.6 %collective-permute-start.18 = (bf16[2,64,1024]{2,1,0:T(8,128)(2,1)S(1)}, bf16[2,64,1024]{2,1,0:T(8,128)(2,1)S(1)}, u32[]{:S(2)}, u32[]{:S(2)}) collective-permute-start(bf16[2,64,1024]{2,1,0:T(8,128)(2,1)S(1)} %get-tuple-element.88), channel_id=1, source_target_pairs={{0,2},{1,3},{2,0},{3,1},{4,6},{5,7},{6,4},{7,5},{8,10},{9,11},{10,... | collective-permute-start | bytes 786440 | tf_op jit(solution)/shard_map/ppermute | solution.py:421
  46.9 0.5 collective-permute-start.19
  47.4 1.3 collective-permute-start.20
  48.7 1.3 shard_map.105
  50.0 1.4 %collective-permute-done.20.refs_3_ = f32[2,2,16,128]{3,2,1,0:T(8,128)S(1)} collective-permute-done((f32[2,2,16,128]{3,2,1,0:T(8,128)S(1)}, f32[2,2,16,128]{3,2,1,0:T(8,128)S(1)}, u32[]{:S(2)}, u32[]{:S(2)}) %collective-permute-start.20) | collective-permute-done | bytes 32800 | tf_op jit(solution)/shard_map/ppermute | solution.py:421
  51.3 2.4 %collective-permute-done.18.refs_1_ = bf16[2,64,1024]{2,1,0:T(8,128)(2,1)S(1)} collective-permute-done((bf16[2,64,1024]{2,1,0:T(8,128)(2,1)S(1)}, bf16[2,64,1024]{2,1,0:T(8,128)(2,1)S(1)}, u32[]{:S(2)}, u32[]{:S(2)}) %collective-permute-start.18) | collective-permute-done | bytes 262176 | tf_op jit(solution)/shard_map/ppermute | solution.py:421
  53.7 1.2 collective-permute-done.19.refs_1_.after_ref.refs_4_
  55.0 0.6 collective-permute-start.22
  55.6 1.4 %collective-permute-start.21 = (bf16[64,1024]{1,0:T(8,128)(2,1)S(1)}, bf16[64,1024]{1,0:T(8,128)(2,1)S(1)}, u32[]{:S(2)}, u32[]{:S(2)}) collective-permute-start(bf16[64,1024]{1,0:T(8,128)(2,1)S(1)} %shard_map.106), channel_id=1, source_target_pairs={{0,16},{16,0},{1,17},{17,1},{2,18},{18,2},{3,19},{19,3},{4,20},{20... | collective-permute-start | bytes 393224 | tf_op jit(solution)/shard_map/ppermute | solution.py:418
  57.0 1.4 %shard_map.108 = (bf16[704,1024]{1,0:T(8,128)(2,1)S(1)}, bf16[704,1024]{1,0:T(8,128)(2,1)S(1)}, bf16[1024,768]{1,0:T(8,128)(2,1)S(1)}) custom-call(bf16[704,1024]{1,0:T(8,128)(2,1)S(1)} %collective-permute-done.7.gate_hbm, bf16[704,1024]{1,0:T(8,128)(2,1)S(1)} %collective-permute-done.8.up_hbm, ...), custom_call_target="tpu_custom_call" | custom-call | bytes 8650752 | tf_op jit(solution)/shard_map/pallas_call | solution.py:360
  58.5 1.5 %collective-permute-done.22.refs_5_ = bf16[64,1024]{1,0:T(8,128)(2,1)S(1)} collective-permute-done((bf16[64,1024]{1,0:T(8,128)(2,1)S(1)}, bf16[64,1024]{1,0:T(8,128)(2,1)S(1)}, u32[]{:S(2)}, u32[]{:S(2)}) %collective-permute-start.22) | collective-permute-done | bytes 131104 | tf_op jit(solution)/shard_map/ppermute | solution.py:421
  60.0 0.7 collective-permute-done.21.refs_2_
  60.7 0.2 shard_map.109
  60.9 1.6 %collective-permute-start.23 = (bf16[128,1024]{1,0:T(8,128)(2,1)S(1)}, bf16[128,1024]{1,0:T(8,128)(2,1)S(1)}, u32[]{:S(2)}, u32[]{:S(2)}) collective-permute-start(bf16[128,1024]{1,0:T(8,128)(2,1)S(1)} %get-tuple-element.121.refs_1_), channel_id=1, source_target_pairs={{0,2},{1,3},{2,0},{3,1},{4,6},{5,7},{6,4},{7,5},{8,10},{9,11},{10,... | collective-permute-start | bytes 786440 | tf_op jit(solution)/shard_map/ppermute | solution.py:421
  62.5 2.3 %collective-permute-start.24 = (bf16[128,1024]{1,0:T(8,128)(2,1)S(1)}, bf16[128,1024]{1,0:T(8,128)(2,1)S(1)}, u32[]{:S(2)}, u32[]{:S(2)}) collective-permute-start(bf16[128,1024]{1,0:T(8,128)(2,1)S(1)} %get-tuple-element.121.refs_1_), channel_id=1, source_target_pairs={{0,8},{1,9},{2,10},{3,11},{4,12},{5,13},{6,14},{7,15},{8,0},{9,1},... | collective-permute-start | bytes 786440 | tf_op jit(solution)/shard_map/ppermute | solution.py:421
  64.8 2.6 %collective-permute-done.23.refs_2_ = bf16[128,1024]{1,0:T(8,128)(2,1)S(1)} collective-permute-done((bf16[128,1024]{1,0:T(8,128)(2,1)S(1)}, bf16[128,1024]{1,0:T(8,128)(2,1)S(1)}, u32[]{:S(2)}, u32[]{:S(2)}) %collective-permute-start.23) | collective-permute-done | bytes 262176 | tf_op jit(solution)/shard_map/ppermute | solution.py:421
  67.4 4.3 %shard_map.110 = (bf16[1024,128]{1,0:T(8,128)(2,1)S(1)}, bf16[1024,128]{1,0:T(8,128)(2,1)S(1)}) custom-call(s32[6]{0:T(128)S(1)} %stack.42.place_ref.refs_0_, bf16[128,1024]{1,0:T(8,128)(2,1)S(1)} %get-tuple-element.121.refs_1_, bf16[128,1024]{1,0:T(8,128)(2,1)S(1)} %collective-permute-done.23.refs_2_, f32[2,2,16,128]{3,2,1,0:T(8,128)S(1)} %shard_map.103.refs_14_.refs_3_, ...), custom_call_target="tpu_custom_call" | custom-call | flops 2214592512 | bytes 9699328 | tf_op jit(solution)/shard_map/pallas_call | solution.py:283
  71.6 3.2 %collective-permute-done.24.refs_1_ = bf16[128,1024]{1,0:T(8,128)(2,1)S(1)} collective-permute-done((bf16[128,1024]{1,0:T(8,128)(2,1)S(1)}, bf16[128,1024]{1,0:T(8,128)(2,1)S(1)}, u32[]{:S(2)}, u32[]{:S(2)}) %collective-permute-start.24) | collective-permute-done | bytes 262176 | tf_op jit(solution)/shard_map/ppermute | solution.py:421
  74.8 0.4 collective-permute-start.25
  75.2 7.1 %collective-permute-done.25.refs_2_ = bf16[128,1024]{1,0:T(8,128)(2,1)S(1)} collective-permute-done((bf16[128,1024]{1,0:T(8,128)(2,1)S(1)}, bf16[128,1024]{1,0:T(8,128)(2,1)S(1)}, u32[]{:S(2)}, u32[]{:S(2)}) %collective-permute-start.25) | collective-permute-done | bytes 262176 | tf_op jit(solution)/shard_map/ppermute | solution.py:421
  82.2 4.3 %shard_map.111 = (bf16[1024,128]{1,0:T(8,128)(2,1)S(1)}, bf16[1024,128]{1,0:T(8,128)(2,1)S(1)}) custom-call(s32[6]{0:T(128)S(1)} %stack.42.place_ref.refs_0_, bf16[128,1024]{1,0:T(8,128)(2,1)S(1)} %collective-permute-done.24.refs_1_, bf16[128,1024]{1,0:T(8,128)(2,1)S(1)} %collective-permute-done.25.refs_2_, ...), custom_call_target="tpu_custom_call" | custom-call | flops 2214592512 | bytes 9699328 | tf_op jit(solution)/shard_map/pallas_call | solution.py:283
  86.5 0.4 collective-permute-start.26
  86.9 1.7 %collective-permute-start.29 = (bf16[128,1024]{1,0:T(8,128)(2,1)S(1)}, bf16[128,1024]{1,0:T(8,128)(2,1)S(1)}, u32[]{:S(2)}, u32[]{:S(2)}) collective-permute-start(bf16[128,1024]{1,0:T(8,128)(2,1)S(1)} %collective-permute-done.28.refs_1_), channel_id=1, source_target_pairs={{0,2},{1,3},{2,0},{3,1},{4,6},{5,7},{6,4},{7,5},{8,10},{9,11},{10,... | collective-permute-start | bytes 786440 | tf_op jit(solution)/shard_map/ppermute | solution.py:421
  88.6 2.0 %collective-permute-start.33 = (bf16[128,1024]{1,0:T(8,128)(2,1)S(1)}, bf16[128,1024]{1,0:T(8,128)(2,1)S(1)}, u32[]{:S(2)}, u32[]{:S(2)}) collective-permute-start(bf16[128,1024]{1,0:T(8,128)(2,1)S(1)} %collective-permute-done.23.refs_2_), channel_id=1, source_target_pairs={{0,4},{1,5},{2,6},{3,7},{4,0},{5,1},{6,2},{7,3},{8,12},{9,13},{10,... | collective-permute-start | bytes 786440 | tf_op jit(solution)/shard_map/ppermute | solution.py:421
  90.6 5.2 %collective-permute-done.26.refs_1_ = bf16[1024,128]{1,0:T(8,128)(2,1)S(1)} collective-permute-done((bf16[1024,128]{1,0:T(8,128)(2,1)S(1)}, bf16[1024,128]{1,0:T(8,128)(2,1)S(1)}, u32[]{:S(2)}, u32[]{:S(2)}) %collective-permute-start.26) | collective-permute-done | bytes 262176 | tf_op jit(solution)/shard_map/ppermute | solution.py:421
  95.9 2.8 %collective-permute-done.29.refs_2_ = bf16[128,1024]{1,0:T(8,128)(2,1)S(1)} collective-permute-done((bf16[128,1024]{1,0:T(8,128)(2,1)S(1)}, bf16[128,1024]{1,0:T(8,128)(2,1)S(1)}, u32[]{:S(2)}, u32[]{:S(2)}) %collective-permute-start.29) | collective-permute-done | bytes 262176 | tf_op jit(solution)/shard_map/ppermute | solution.py:421
  98.7 4.3 %shard_map.113 = (bf16[1024,128]{1,0:T(8,128)(2,1)S(1)}, bf16[1024,128]{1,0:T(8,128)(2,1)S(1)}) custom-call(s32[6]{0:T(128)S(1)} %stack.42.place_ref.refs_0_, bf16[128,1024]{1,0:T(8,128)(2,1)S(1)} %collective-permute-done.28.refs_1_, bf16[128,1024]{1,0:T(8,128)(2,1)S(1)} %collective-permute-done.29.refs_2_, ...), custom_call_target="tpu_custom_call" | custom-call | flops 2214592512 | bytes 9699328 | tf_op jit(solution)/shard_map/pallas_call | solution.py:283
  103.0 4.3 %shard_map.115 = (bf16[1024,128]{1,0:T(8,128)(2,1)S(1)}, bf16[1024,128]{1,0:T(8,128)(2,1)S(1)}) custom-call(s32[6]{0:T(128)S(1)} %stack.42.place_ref.refs_0_, bf16[128,1024]{1,0:T(8,128)(2,1)S(1)} %collective-permute-done.32.refs_1_, bf16[128,1024]{1,0:T(8,128)(2,1)S(1)} %collective-permute-done.33.refs_2_, ...), custom_call_target="tpu_custom_call" | custom-call | flops 2214592512 | bytes 9699328 | tf_op jit(solution)/shard_map/pallas_call | solution.py:283
  107.3 0.4 collective-permute-start.30
  107.7 1.7 %collective-permute-start.27 = (bf16[1024,128]{1,0:T(8,128)(2,1)S(1)}, bf16[1024,128]{1,0:T(8,128)(2,1)S(1)}, u32[]{:S(2)}, u32[]{:S(2)}) collective-permute-start(bf16[1024,128]{1,0:T(8,128)(2,1)S(1)} %shard_map.112.refs_10_), channel_id=1, source_target_pairs={{0,8},{1,9},{2,10},{3,11},{4,12},{5,13},{6,14},{7,15},{8,0},{9,1},... | collective-permute-start | bytes 786440 | tf_op jit(solution)/shard_map/ppermute | solution.py:421
  109.7 11.7 %collective-permute-done.35.refs_1_ = bf16[1024,128]{1,0:T(8,128)(2,1)S(1)} collective-permute-done((bf16[1024,128]{1,0:T(8,128)(2,1)S(1)}, bf16[1024,128]{1,0:T(8,128)(2,1)S(1)}, u32[]{:S(2)}, u32[]{:S(2)}) %collective-permute-start.35) | collective-permute-done | bytes 262176 | tf_op jit(solution)/shard_map/ppermute | solution.py:421
  121.6 1.0 collective-permute-start.31
  122.7 4.3 %collective-permute-done.34.refs_3_ = bf16[1024,128]{1,0:T(8,128)(2,1)S(1)} collective-permute-done((bf16[1024,128]{1,0:T(8,128)(2,1)S(1)}, bf16[1024,128]{1,0:T(8,128)(2,1)S(1)}, u32[]{:S(2)}, u32[]{:S(2)}) %collective-permute-start.34) | collective-permute-done | bytes 262176 | tf_op jit(solution)/shard_map/ppermute | solution.py:421
  126.9 1.0 collective-permute-done.36.refs_4_
  127.9 2.1 %collective-permute-done.31.refs_2_ = bf16[1024,128]{1,0:T(8,128)(2,1)S(1)} collective-permute-done((bf16[1024,128]{1,0:T(8,128)(2,1)S(1)}, bf16[1024,128]{1,0:T(8,128)(2,1)S(1)}, u32[]{:S(2)}, u32[]{:S(2)}) %collective-permute-start.31) | collective-permute-done | bytes 262176 | tf_op jit(solution)/shard_map/ppermute | solution.py:421
  130.0 0.9 shard_map.117
  (52 shorter events, 1.2 us)
Async XLA Ops:
  0.0 13.8 %collective-permute-start.3 = (bf16[128,1024]{1,0:T(8,128)(2,1)}, bf16[128,1024]{1,0:T(8,128)(2,1)S(1)}, u32[]{:S(2)}, u32[]{:S(2)}) collective-permute-start(bf16[128,1024]{1,0:T(8,128)(2,1)} %tokens_ref.2), channel_id=1, source_target_pairs={{0,16},{16,0},{1,17},{17,1},{2,18},{18,2},{3,19},{19,3},{4,20},{20... | collective-permute-start | bytes 786440 | tf_op jit(solution)/shard_map/ppermute | solution.py:418
  2.9 10.9 %collective-permute-start.4 = (bf16[128,1024]{1,0:T(8,128)(2,1)}, bf16[128,1024]{1,0:T(8,128)(2,1)S(1)}, u32[]{:S(2)}, u32[]{:S(2)}) collective-permute-start(bf16[128,1024]{1,0:T(8,128)(2,1)} %tokens_ref.2), channel_id=1, source_target_pairs={{0,2},{1,3},{2,0},{3,1},{4,6},{5,7},{6,4},{7,5},{8,10},{9,11},{10,... | collective-permute-start | bytes 786440 | tf_op jit(solution)/shard_map/ppermute | solution.py:421
  4.5 0.9 copy-start.5
  5.5 0.8 copy-start.6
  7.3 6.5 %collective-permute-start.1 = (bf16[32,1024]{1,0:T(8,128)(2,1)S(1)}, bf16[32,1024]{1,0:T(8,128)(2,1)S(1)}, u32[]{:S(2)}, u32[]{:S(2)}) collective-permute-start(bf16[32,1024]{1,0:T(8,128)(2,1)S(1)} %get-tuple-element.67), channel_id=1, source_target_pairs={{0,2},{1,3},{2,0},{3,1},{4,6},{5,7},{6,4},{7,5},{8,10},{9,11},{10,... | collective-permute-start | bytes 196616 | tf_op jit(solution)/shard_map/ppermute | solution.py:421
  7.8 5.9 %collective-permute-start.2 = (bf16[32,1024]{1,0:T(8,128)(2,1)S(1)}, bf16[32,1024]{1,0:T(8,128)(2,1)S(1)}, u32[]{:S(2)}, u32[]{:S(2)}) collective-permute-start(bf16[32,1024]{1,0:T(8,128)(2,1)S(1)} %get-tuple-element.68), channel_id=1, source_target_pairs={{0,18},{1,19},{2,16},{3,17},{4,22},{5,23},{6,20},{7,21},{8,26},{9,... | collective-permute-start | bytes 196616 | tf_op jit(solution)/shard_map/ppermute | solution.py:451
  9.3 4.4 %collective-permute-start = (bf16[32,1024]{1,0:T(8,128)(2,1)S(1)}, bf16[32,1024]{1,0:T(8,128)(2,1)S(1)}, u32[]{:S(2)}, u32[]{:S(2)}) collective-permute-start(bf16[32,1024]{1,0:T(8,128)(2,1)S(1)} %get-tuple-element.66), channel_id=1, source_target_pairs={{0,16},{16,0},{1,17},{17,1},{2,18},{18,2},{3,19},{19,3},{4,20},{20... | collective-permute-start | bytes 196616 | tf_op jit(solution)/shard_map/ppermute | solution.py:418
  13.8 15.7 %collective-permute-start.7 = (bf16[704,1024]{1,0:T(8,128)(2,1)}, bf16[704,1024]{1,0:T(8,128)(2,1)S(1)}, u32[]{:S(2)}, u32[]{:S(2)}) collective-permute-start(bf16[704,1024]{1,0:T(8,128)(2,1)} %bitcast.23), channel_id=1, source_target_pairs={{0,1},{1,0},{2,3},{3,2},{4,5},{5,4},{6,7},{7,6},{8,9},{9,8},{10,11... | collective-permute-start | bytes 4325384 | tf_op jit(solution)/shard_map/ppermute | solution.py:421
  13.9 15.6 %collective-permute-start.8 = (bf16[704,1024]{1,0:T(8,128)(2,1)}, bf16[704,1024]{1,0:T(8,128)(2,1)S(1)}, u32[]{:S(2)}, u32[]{:S(2)}) collective-permute-start(bf16[704,1024]{1,0:T(8,128)(2,1)} %bitcast.25), channel_id=1, source_target_pairs={{0,1},{1,0},{2,3},{3,2},{4,5},{5,4},{6,7},{7,6},{8,9},{9,8},{10,11... | collective-permute-start | bytes 4325384 | tf_op jit(solution)/shard_map/ppermute | solution.py:421
  14.4 14.9 %collective-permute-start.5 = (bf16[4,32,1024]{2,1,0:T(8,128)(2,1)S(1)}, bf16[4,32,1024]{2,1,0:T(8,128)(2,1)S(1)}, u32[]{:S(2)}, u32[]{:S(2)}) collective-permute-start(bf16[4,32,1024]{2,1,0:T(8,128)(2,1)S(1)} %pad_maximum_fusion.refs_6_), channel_id=1, source_target_pairs={{0,8},{1,9},{2,10},{3,11},{4,12},{5,13},{6,14},{7,15},{8,0},{9,1},... | collective-permute-start | bytes 786440 | tf_op jit(solution)/shard_map/ppermute | solution.py:421
  17.0 12.5 %collective-permute-start.6 = (bf16[4,32,1024]{2,1,0:T(8,128)(2,1)S(1)}, bf16[4,32,1024]{2,1,0:T(8,128)(2,1)S(1)}, u32[]{:S(2)}, u32[]{:S(2)}) collective-permute-start(bf16[4,32,1024]{2,1,0:T(8,128)(2,1)S(1)} %pad_maximum_fusion.refs_6_), channel_id=1, source_target_pairs={{0,4},{1,5},{2,6},{3,7},{4,0},{5,1},{6,2},{7,3},{8,12},{9,13},{10,... | collective-permute-start | bytes 786440 | tf_op jit(solution)/shard_map/ppermute | solution.py:421
  18.6 10.9 %collective-permute-start.9 = (bf16[128,1024]{1,0:T(8,128)(2,1)S(1)}, bf16[128,1024]{1,0:T(8,128)(2,1)S(1)}, u32[]{:S(2)}, u32[]{:S(2)}) collective-permute-start(bf16[128,1024]{1,0:T(8,128)(2,1)S(1)} %collective-permute-done.3.refs_3_), channel_id=1, source_target_pairs={{0,2},{1,3},{2,0},{3,1},{4,6},{5,7},{6,4},{7,5},{8,10},{9,11},{10,... | collective-permute-start | bytes 786440 | tf_op jit(solution)/shard_map/ppermute | solution.py:421
  20.1 0.9 copy-start.3
  21.0 0.7 copy-start.7
  21.7 0.7 copy-start.8
  22.4 0.7 copy-start.9
  29.5 11.8 %collective-permute-start.17 = (bf16[704,1024]{1,0:T(8,128)(2,1)}, bf16[704,1024]{1,0:T(8,128)(2,1)S(1)}, u32[]{:S(2)}, u32[]{:S(2)}) collective-permute-start(bf16[704,1024]{1,0:T(8,128)(2,1)} %bitcast.21), channel_id=1, source_target_pairs={{0,1},{1,0},{2,3},{3,2},{4,5},{5,4},{6,7},{7,6},{8,9},{9,8},{10,11... | collective-permute-start | bytes 4325384 | tf_op jit(solution)/shard_map/ppermute | solution.py:421
  29.6 9.8 %collective-permute-start.13 = (bf16[4,32,1024]{2,1,0:T(8,128)(2,1)S(1)}, bf16[4,32,1024]{2,1,0:T(8,128)(2,1)S(1)}, u32[]{:S(2)}, u32[]{:S(2)}) collective-permute-start(bf16[4,32,1024]{2,1,0:T(8,128)(2,1)S(1)} %collective-permute-done.5.refs_10_), channel_id=1, source_target_pairs={{0,4},{1,5},{2,6},{3,7},{4,0},{5,1},{6,2},{7,3},{8,12},{9,13},{10,... | collective-permute-start | bytes 786440 | tf_op jit(solution)/shard_map/ppermute | solution.py:421
  31.1 3.7 %collective-permute-start.15 = (f32[16,128]{1,0:T(8,128)S(1)}, f32[16,128]{1,0:T(8,128)S(1)}, u32[]{:S(2)}, u32[]{:S(2)}) collective-permute-start(f32[16,128]{1,0:T(8,128)S(1)} %get-tuple-element.85.first_ref), channel_id=1, source_target_pairs={{0,2},{1,3},{2,0},{3,1},{4,6},{5,7},{6,4},{7,5},{8,10},{9,11},{10,... | collective-permute-start | bytes 24584 | tf_op jit(solution)/shard_map/ppermute | solution.py:421
  34.7 4.6 %collective-permute-start.16 = (f32[2,16,128]{2,1,0:T(8,128)S(1)}, f32[2,16,128]{2,1,0:T(8,128)S(1)}, u32[]{:S(2)}, u32[]{:S(2)}) collective-permute-start(f32[2,16,128]{2,1,0:T(8,128)S(1)} %shard_map.102.first_ref), channel_id=1, source_target_pairs={{0,8},{1,9},{2,10},{3,11},{4,12},{5,13},{6,14},{7,15},{8,0},{9,1},... | collective-permute-start | bytes 49160 | tf_op jit(solution)/shard_map/ppermute | solution.py:421
  37.1 2.8 %collective-permute-start.10 = (bf16[4,32,1024]{2,1,0:T(8,128)(2,1)S(1)}, bf16[4,32,1024]{2,1,0:T(8,128)(2,1)S(1)}, u32[]{:S(2)}, u32[]{:S(2)}) collective-permute-start(bf16[4,32,1024]{2,1,0:T(8,128)(2,1)S(1)} %pad_maximum_fusion.refs_6_), channel_id=1, source_target_pairs={{0,1},{1,0},{2,3},{3,2},{4,5},{5,4},{6,7},{7,6},{8,9},{9,8},{10,11... | collective-permute-start | bytes 786440 | tf_op jit(solution)/shard_map/ppermute | solution.py:421
  37.1 3.8 %collective-permute-start.12 = (bf16[4,32,1024]{2,1,0:T(8,128)(2,1)S(1)}, bf16[4,32,1024]{2,1,0:T(8,128)(2,1)S(1)}, u32[]{:S(2)}, u32[]{:S(2)}) collective-permute-start(bf16[4,32,1024]{2,1,0:T(8,128)(2,1)S(1)} %collective-permute-done.5.refs_10_), channel_id=1, source_target_pairs={{0,1},{1,0},{2,3},{3,2},{4,5},{5,4},{6,7},{7,6},{8,9},{9,8},{10,11... | collective-permute-start | bytes 786440 | tf_op jit(solution)/shard_map/ppermute | solution.py:421
  39.4 1.5 %collective-permute-start.11 = (bf16[4,32,1024]{2,1,0:T(8,128)(2,1)S(1)}, bf16[4,32,1024]{2,1,0:T(8,128)(2,1)S(1)}, u32[]{:S(2)}, u32[]{:S(2)}) collective-permute-start(bf16[4,32,1024]{2,1,0:T(8,128)(2,1)S(1)} %collective-permute-done.6.refs_8_), channel_id=1, source_target_pairs={{0,1},{1,0},{2,3},{3,2},{4,5},{5,4},{6,7},{7,6},{8,9},{9,8},{10,11... | collective-permute-start | bytes 786440 | tf_op jit(solution)/shard_map/ppermute | solution.py:421
  39.4 1.9 %collective-permute-start.14 = (bf16[4,32,1024]{2,1,0:T(8,128)(2,1)S(1)}, bf16[4,32,1024]{2,1,0:T(8,128)(2,1)S(1)}, u32[]{:S(2)}, u32[]{:S(2)}) collective-permute-start(bf16[4,32,1024]{2,1,0:T(8,128)(2,1)S(1)} %collective-permute-done.13.refs_12_), channel_id=1, source_target_pairs={{0,1},{1,0},{2,3},{3,2},{4,5},{5,4},{6,7},{7,6},{8,9},{9,8},{10,11... | collective-permute-start | bytes 786440 | tf_op jit(solution)/shard_map/ppermute | solution.py:421
  41.3 7.4 %copy-start = (bf16[1,704,1024]{2,1,0:T(8,128)(2,1)S(1)}, bf16[1,704,1024]{2,1,0:T(8,128)(2,1)}, u32[]{:S(2)}) copy-start(bf16[1,704,1024]{2,1,0:T(8,128)(2,1)} %param.19) | copy-start | bytes 4325380
  41.3 7.4 %copy-start.1 = (bf16[1,1024,704]{1,2,0:T(8,128)(2,1)S(1)}, bf16[1,1024,704]{1,2,0:T(8,128)(2,1)}, u32[]{:S(2)}) copy-start(bf16[1,1024,704]{1,2,0:T(8,128)(2,1)} %param.17) | copy-start | bytes 4325380
  41.3 7.4 %copy-start.2 = (bf16[1,1024,704]{1,2,0:T(8,128)(2,1)S(1)}, bf16[1,1024,704]{1,2,0:T(8,128)(2,1)}, u32[]{:S(2)}) copy-start(bf16[1,1024,704]{1,2,0:T(8,128)(2,1)} %param.18) | copy-start | bytes 4325380
  45.3 8.4 %collective-permute-start.18 = (bf16[2,64,1024]{2,1,0:T(8,128)(2,1)S(1)}, bf16[2,64,1024]{2,1,0:T(8,128)(2,1)S(1)}, u32[]{:S(2)}, u32[]{:S(2)}) collective-permute-start(bf16[2,64,1024]{2,1,0:T(8,128)(2,1)S(1)} %get-tuple-element.88), channel_id=1, source_target_pairs={{0,2},{1,3},{2,0},{3,1},{4,6},{5,7},{6,4},{7,5},{8,10},{9,11},{10,... | collective-permute-start | bytes 786440 | tf_op jit(solution)/shard_map/ppermute | solution.py:421
  46.9 8.1 %collective-permute-start.19 = (bf16[2,64,1024]{2,1,0:T(8,128)(2,1)S(1)}, bf16[2,64,1024]{2,1,0:T(8,128)(2,1)S(1)}, u32[]{:S(2)}, u32[]{:S(2)}) collective-permute-start(bf16[2,64,1024]{2,1,0:T(8,128)(2,1)S(1)} %get-tuple-element.89), channel_id=1, source_target_pairs={{0,16},{16,0},{1,17},{17,1},{2,18},{18,2},{3,19},{19,3},{4,20},{20... | collective-permute-start | bytes 786440 | tf_op jit(solution)/shard_map/ppermute | solution.py:418
  47.4 3.9 %collective-permute-start.20 = (f32[2,2,16,128]{3,2,1,0:T(8,128)S(1)}, f32[2,2,16,128]{3,2,1,0:T(8,128)S(1)}, u32[]{:S(2)}, u32[]{:S(2)}) collective-permute-start(f32[2,2,16,128]{3,2,1,0:T(8,128)S(1)} %shard_map.103.refs_14_.refs_3_), channel_id=1, source_target_pairs={{0,4},{1,5},{2,6},{3,7},{4,0},{5,1},{6,2},{7,3},{8,12},{9,13},{10,... | collective-permute-start | bytes 98312 | tf_op jit(solution)/shard_map/ppermute | solution.py:421
  55.0 5.0 %collective-permute-start.22 = (bf16[64,1024]{1,0:T(8,128)(2,1)S(1)}, bf16[64,1024]{1,0:T(8,128)(2,1)S(1)}, u32[]{:S(2)}, u32[]{:S(2)}) collective-permute-start(bf16[64,1024]{1,0:T(8,128)(2,1)S(1)} %shard_map.107), channel_id=1, source_target_pairs={{0,2},{1,3},{2,0},{3,1},{4,6},{5,7},{6,4},{7,5},{8,10},{9,11},{10,... | collective-permute-start | bytes 393224 | tf_op jit(solution)/shard_map/ppermute | solution.py:421
  55.6 5.1 %copy-start.4 = (bf16[128,1024]{1,0:T(8,128)(2,1)S(1)}, bf16[128,1024]{1,0:T(8,128)(2,1)}, u32[]{:S(2)}) copy-start(bf16[128,1024]{1,0:T(8,128)(2,1)} %tokens_ref.2) | copy-start | bytes 786436
  55.6 5.1 %copy-start.10 = (f32[1024]{0:T(1024)S(1)}, f32[1024]{0:T(1024)}, u32[]{:S(2)}) copy-start(f32[1024]{0:T(1024)} %param.14) | copy-start | bytes 12292
  55.6 5.0 %collective-permute-start.21 = (bf16[64,1024]{1,0:T(8,128)(2,1)S(1)}, bf16[64,1024]{1,0:T(8,128)(2,1)S(1)}, u32[]{:S(2)}, u32[]{:S(2)}) collective-permute-start(bf16[64,1024]{1,0:T(8,128)(2,1)S(1)} %shard_map.106), channel_id=1, source_target_pairs={{0,16},{16,0},{1,17},{17,1},{2,18},{18,2},{3,19},{19,3},{4,20},{20... | collective-permute-start | bytes 393224 | tf_op jit(solution)/shard_map/ppermute | solution.py:418
  60.9 6.4 %collective-permute-start.23 = (bf16[128,1024]{1,0:T(8,128)(2,1)S(1)}, bf16[128,1024]{1,0:T(8,128)(2,1)S(1)}, u32[]{:S(2)}, u32[]{:S(2)}) collective-permute-start(bf16[128,1024]{1,0:T(8,128)(2,1)S(1)} %get-tuple-element.121.refs_1_), channel_id=1, source_target_pairs={{0,2},{1,3},{2,0},{3,1},{4,6},{5,7},{6,4},{7,5},{8,10},{9,11},{10,... | collective-permute-start | bytes 786440 | tf_op jit(solution)/shard_map/ppermute | solution.py:421
  62.5 12.3 %collective-permute-start.24 = (bf16[128,1024]{1,0:T(8,128)(2,1)S(1)}, bf16[128,1024]{1,0:T(8,128)(2,1)S(1)}, u32[]{:S(2)}, u32[]{:S(2)}) collective-permute-start(bf16[128,1024]{1,0:T(8,128)(2,1)S(1)} %get-tuple-element.121.refs_1_), channel_id=1, source_target_pairs={{0,8},{1,9},{2,10},{3,11},{4,12},{5,13},{6,14},{7,15},{8,0},{9,1},... | collective-permute-start | bytes 786440 | tf_op jit(solution)/shard_map/ppermute | solution.py:421
  74.8 7.4 %collective-permute-start.25 = (bf16[128,1024]{1,0:T(8,128)(2,1)S(1)}, bf16[128,1024]{1,0:T(8,128)(2,1)S(1)}, u32[]{:S(2)}, u32[]{:S(2)}) collective-permute-start(bf16[128,1024]{1,0:T(8,128)(2,1)S(1)} %collective-permute-done.24.refs_1_), channel_id=1, source_target_pairs={{0,2},{1,3},{2,0},{3,1},{4,6},{5,7},{6,4},{7,5},{8,10},{9,11},{10,... | collective-permute-start | bytes 786440 | tf_op jit(solution)/shard_map/ppermute | solution.py:421
  75.2 11.8 %collective-permute-start.28 = (bf16[128,1024]{1,0:T(8,128)(2,1)S(1)}, bf16[128,1024]{1,0:T(8,128)(2,1)S(1)}, u32[]{:S(2)}, u32[]{:S(2)}) collective-permute-start(bf16[128,1024]{1,0:T(8,128)(2,1)S(1)} %collective-permute-done.24.refs_1_), channel_id=1, source_target_pairs={{0,4},{1,5},{2,6},{3,7},{4,0},{5,1},{6,2},{7,3},{8,12},{9,13},{10,... | collective-permute-start | bytes 786440 | tf_op jit(solution)/shard_map/ppermute | solution.py:421
  86.5 9.3 %collective-permute-start.26 = (bf16[1024,128]{1,0:T(8,128)(2,1)S(1)}, bf16[1024,128]{1,0:T(8,128)(2,1)S(1)}, u32[]{:S(2)}, u32[]{:S(2)}) collective-permute-start(bf16[1024,128]{1,0:T(8,128)(2,1)S(1)} %get-tuple-element.117.refs_10_), channel_id=1, source_target_pairs={{0,2},{1,3},{2,0},{3,1},{4,6},{5,7},{6,4},{7,5},{8,10},{9,11},{10,... | collective-permute-start | bytes 786440 | tf_op jit(solution)/shard_map/ppermute | solution.py:421
  86.9 11.8 %collective-permute-start.29 = (bf16[128,1024]{1,0:T(8,128)(2,1)S(1)}, bf16[128,1024]{1,0:T(8,128)(2,1)S(1)}, u32[]{:S(2)}, u32[]{:S(2)}) collective-permute-start(bf16[128,1024]{1,0:T(8,128)(2,1)S(1)} %collective-permute-done.28.refs_1_), channel_id=1, source_target_pairs={{0,2},{1,3},{2,0},{3,1},{4,6},{5,7},{6,4},{7,5},{8,10},{9,11},{10,... | collective-permute-start | bytes 786440 | tf_op jit(solution)/shard_map/ppermute | solution.py:421
  88.6 14.4 %collective-permute-start.32 = (bf16[128,1024]{1,0:T(8,128)(2,1)S(1)}, bf16[128,1024]{1,0:T(8,128)(2,1)S(1)}, u32[]{:S(2)}, u32[]{:S(2)}) collective-permute-start(bf16[128,1024]{1,0:T(8,128)(2,1)S(1)} %get-tuple-element.121.refs_1_), channel_id=1, source_target_pairs={{0,4},{1,5},{2,6},{3,7},{4,0},{5,1},{6,2},{7,3},{8,12},{9,13},{10,... | collective-permute-start | bytes 786440 | tf_op jit(solution)/shard_map/ppermute | solution.py:421
  88.6 14.4 %collective-permute-start.33 = (bf16[128,1024]{1,0:T(8,128)(2,1)S(1)}, bf16[128,1024]{1,0:T(8,128)(2,1)S(1)}, u32[]{:S(2)}, u32[]{:S(2)}) collective-permute-start(bf16[128,1024]{1,0:T(8,128)(2,1)S(1)} %collective-permute-done.23.refs_2_), channel_id=1, source_target_pairs={{0,4},{1,5},{2,6},{3,7},{4,0},{5,1},{6,2},{7,3},{8,12},{9,13},{10,... | collective-permute-start | bytes 786440 | tf_op jit(solution)/shard_map/ppermute | solution.py:421
  107.2 14.2 %collective-permute-start.35 = (bf16[1024,128]{1,0:T(8,128)(2,1)S(1)}, bf16[1024,128]{1,0:T(8,128)(2,1)S(1)}, u32[]{:S(2)}, u32[]{:S(2)}) collective-permute-start(bf16[1024,128]{1,0:T(8,128)(2,1)S(1)} %get-tuple-element.124), channel_id=1, source_target_pairs={{0,4},{1,5},{2,6},{3,7},{4,0},{5,1},{6,2},{7,3},{8,12},{9,13},{10,... | collective-permute-start | bytes 786440 | tf_op jit(solution)/shard_map/ppermute | solution.py:421
  107.3 14.2 %collective-permute-start.30 = (bf16[1024,128]{1,0:T(8,128)(2,1)S(1)}, bf16[1024,128]{1,0:T(8,128)(2,1)S(1)}, u32[]{:S(2)}, u32[]{:S(2)}) collective-permute-start(bf16[1024,128]{1,0:T(8,128)(2,1)S(1)} %get-tuple-element.120.refs_11_), channel_id=1, source_target_pairs={{0,2},{1,3},{2,0},{3,1},{4,6},{5,7},{6,4},{7,5},{8,10},{9,11},{10,... | collective-permute-start | bytes 786440 | tf_op jit(solution)/shard_map/ppermute | solution.py:421
  107.7 13.8 %collective-permute-start.27 = (bf16[1024,128]{1,0:T(8,128)(2,1)S(1)}, bf16[1024,128]{1,0:T(8,128)(2,1)S(1)}, u32[]{:S(2)}, u32[]{:S(2)}) collective-permute-start(bf16[1024,128]{1,0:T(8,128)(2,1)S(1)} %shard_map.112.refs_10_), channel_id=1, source_target_pairs={{0,8},{1,9},{2,10},{3,11},{4,12},{5,13},{6,14},{7,15},{8,0},{9,1},... | collective-permute-start | bytes 786440 | tf_op jit(solution)/shard_map/ppermute | solution.py:421
  109.5 17.5 %collective-permute-start.34 = (bf16[1024,128]{1,0:T(8,128)(2,1)S(1)}, bf16[1024,128]{1,0:T(8,128)(2,1)S(1)}, u32[]{:S(2)}, u32[]{:S(2)}) collective-permute-start(bf16[1024,128]{1,0:T(8,128)(2,1)S(1)} %get-tuple-element.123), channel_id=1, source_target_pairs={{0,4},{1,5},{2,6},{3,7},{4,0},{5,1},{6,2},{7,3},{8,12},{9,13},{10,... | collective-permute-start | bytes 786440 | tf_op jit(solution)/shard_map/ppermute | solution.py:421
  121.5 6.4 %collective-permute-start.36 = (bf16[1024,128]{1,0:T(8,128)(2,1)S(1)}, bf16[1024,128]{1,0:T(8,128)(2,1)S(1)}, u32[]{:S(2)}, u32[]{:S(2)}) collective-permute-start(bf16[1024,128]{1,0:T(8,128)(2,1)S(1)} %shard_map.116), channel_id=1, source_target_pairs={{0,2},{1,3},{2,0},{3,1},{4,6},{5,7},{6,4},{7,5},{8,10},{9,11},{10,... | collective-permute-start | bytes 786440 | tf_op jit(solution)/shard_map/ppermute | solution.py:421
  121.6 8.3 %collective-permute-start.31 = (bf16[1024,128]{1,0:T(8,128)(2,1)S(1)}, bf16[1024,128]{1,0:T(8,128)(2,1)S(1)}, u32[]{:S(2)}, u32[]{:S(2)}) collective-permute-start(bf16[1024,128]{1,0:T(8,128)(2,1)S(1)} %shard_map.114), channel_id=1, source_target_pairs={{0,12},{1,13},{2,14},{3,15},{4,8},{5,9},{6,10},{7,11},{8,4},{9,5},... | collective-permute-start | bytes 786440 | tf_op jit(solution)/shard_map/ppermute | solution.py:421

commit v2 on v0

--- a/solution.py
+++ b/solution.py
@@ -147,7 +147,7 @@
             values = own[:, 2 * HEAD_DIM :]
             scores = dot_nt(queries, keys) * (1.0 / math.sqrt(HEAD_DIM))
             raised = jnp.where(causal, jnp.exp(jnp.where(causal, scores, 0.0)), 0.0)
-            probs = raised / jnp.sum(raised, axis=-1, keepdims=True)
+            probs = raised * (1.0 / jnp.sum(raised, axis=-1, keepdims=True))
             outs.append(
                 jnp.dot(
                     probs.astype(jnp.bfloat16), values, preferred_element_type=jnp.float32
@@ -258,16 +258,17 @@
             [scale_ref[*pick, block, pl.ds(place_ref[4 + expert], 1), :] for block in range(2)],
             axis=1,
         )
+        inner = []
         for start, size in tiles:
             gate_value = dot_nt(gate_ref[start : start + size, :], inputs)
             up_value = dot_nt(up_ref[start : start + size, :], inputs)
-            inner = gate_value / (1.0 + jnp.exp(-gate_value)) * (up_value * scale)
-            term = jnp.dot(
-                down_ref[:, start : start + size],
-                inner.astype(jnp.bfloat16),
-                preferred_element_type=jnp.float32,
-            )
-            result = term if result is None else result + term
+            half = 0.5 * gate_value
+            inner.append(((half + half * jnp.tanh(half)) * (up_value * scale)).astype(jnp.bfloat16))
+        inner = jnp.concatenate(inner, axis=0)
+        term = jnp.dot(
+            down_ref[:, : inner.shape[0]], inner, preferred_element_type=jnp.float32
+        )
+        result = term if result is None else result + term
     result = result.astype(jnp.bfloat16)
     rows = block_refs[0].shape[0]
     own_ref[...] = result[:, :rows]

time: 123 us -> 122 us (level)
  Pallas kernels: 26.2 us -> 22.6 us
  waiting for transfers between devices: 50.4 us -> 53 us
    pallas_call x4, Pallas kernels: 17 us -> 13.4 us  [expert_call(): pl.pallas_call(functools.partial(expert_kernel, tiles, pick), out_shape=(...]
    ppermute x32, waiting for transfers between devices: 48.5 us -> 51.1 us  [swap_expert(): lax.ppermute(value, 'expert', [(e, e ^ mask) for e in range(expert_size)])]
  transfers between devices with their start and end apart: 37 -> 37, of which waited for: 22 -> 23; matrix products, arithmetic and copies ran while one was open for 0% -> 0% of each run, Pallas kernels for 17% -> 14%
where the time goes in v2:
time: 122 us
  waiting for transfers between devices  53 us (43%)
  starting transfers between devices  41.2 us (34%)
  Pallas kernels  22.6 us (19%)
  local copies, waits for them, and re-layouts  4.88 us (4%)
    ppermute x32, waiting for transfers between devices, swap_expert(): lax.ppermute(value, 'expert', [(e, e ^ mask) for e in range(expert_size)])  51.1 us
    ppermute x32, starting transfers between devices, swap_expert(): lax.ppermute(value, 'expert', [(e, e ^ mask) for e in range(expert_size)])  33.3 us
    pallas_call x4, Pallas kernels, expert_call(): pl.pallas_call(functools.partial(expert_kernel, tiles, pick), out_shape=(...  13.4 us
    ppermute x4, starting transfers between devices, swap_pair(): return lax.ppermute(value, 'fsdp', [(f, f ^ 1) for f in range(fsdp_size)])  6.37 us
    unnamed x22, local copies, waits for them, and re-layouts  4.8 us
    pallas_call x1, Pallas kernels, attention_call(): pl.pallas_call(functools.partial(attention_kernel, count, len(pieces)), o...  4.01 us
    pallas_call x2, Pallas kernels, load_call(): pl.pallas_call(load_kernel, out_shape=(jax.ShapeDtypeStruct(gate.shape, g...  2.71 us
  transfers between devices with their start and end apart: 37, of which 23 were waited for; matrix products, arithmetic and copies ran while one was open for 0% of the time, Pallas kernels for 14%

profile of v2, /device:TPU:0, one launch (start us, length us, event | category | flops | bytes accessed | tf_op | source)
XLA Modules:
  0.0 121.9 jit_solution(6340463784603425664)
XLA Ops:
  0.0 2.9 %collective-permute-start.3 = (bf16[128,1024]{1,0:T(8,128)(2,1)}, bf16[128,1024]{1,0:T(8,128)(2,1)S(1)}, u32[]{:S(2)}, u32[]{:S(2)}) collective-permute-start(bf16[128,1024]{1,0:T(8,128)(2,1)} %tokens_ref.2), channel_id=1, source_target_pairs={{0,16},{16,0},{1,17},{17,1},{2,18},{18,2},{3,19},{19,3},{4,20},{20... | collective-permute-start | bytes 786440 | tf_op jit(solution)/shard_map/ppermute | solution.py:419
  2.9 1.5 %collective-permute-start.4 = (bf16[128,1024]{1,0:T(8,128)(2,1)}, bf16[128,1024]{1,0:T(8,128)(2,1)S(1)}, u32[]{:S(2)}, u32[]{:S(2)}) collective-permute-start(bf16[128,1024]{1,0:T(8,128)(2,1)} %tokens_ref.2), channel_id=1, source_target_pairs={{0,2},{1,3},{2,0},{3,1},{4,6},{5,7},{6,4},{7,5},{8,10},{9,11},{10,... | collective-permute-start | bytes 786440 | tf_op jit(solution)/shard_map/ppermute | solution.py:422
  4.5 0.9 copy-done.5
  5.5 0.8 copy-done.6
  6.3 0.9 shard_map.100
  7.3 0.6 collective-permute-start.1
  7.8 1.5 %collective-permute-start.2 = (bf16[32,1024]{1,0:T(8,128)(2,1)S(1)}, bf16[32,1024]{1,0:T(8,128)(2,1)S(1)}, u32[]{:S(2)}, u32[]{:S(2)}) collective-permute-start(bf16[32,1024]{1,0:T(8,128)(2,1)S(1)} %get-tuple-element.68), channel_id=1, source_target_pairs={{0,18},{1,19},{2,16},{3,17},{4,22},{5,23},{6,20},{7,21},{8,26},{9,... | collective-permute-start | bytes 196616 | tf_op jit(solution)/shard_map/ppermute | solution.py:452
  9.3 1.5 %collective-permute-start = (bf16[32,1024]{1,0:T(8,128)(2,1)S(1)}, bf16[32,1024]{1,0:T(8,128)(2,1)S(1)}, u32[]{:S(2)}, u32[]{:S(2)}) collective-permute-start(bf16[32,1024]{1,0:T(8,128)(2,1)S(1)} %get-tuple-element.66), channel_id=1, source_target_pairs={{0,16},{16,0},{1,17},{17,1},{2,18},{18,2},{3,19},{19,3},{4,20},{20... | collective-permute-start | bytes 196616 | tf_op jit(solution)/shard_map/ppermute | solution.py:419
  10.8 2.9 %collective-permute-done.1 = bf16[32,1024]{1,0:T(8,128)(2,1)S(1)} collective-permute-done((bf16[32,1024]{1,0:T(8,128)(2,1)S(1)}, bf16[32,1024]{1,0:T(8,128)(2,1)S(1)}, u32[]{:S(2)}, u32[]{:S(2)}) %collective-permute-start.1) | collective-permute-done | bytes 65568 | tf_op jit(solution)/shard_map/ppermute | solution.py:422
  13.9 0.5 collective-permute-start.8
  14.4 2.6 %collective-permute-start.5 = (bf16[4,32,1024]{2,1,0:T(8,128)(2,1)S(1)}, bf16[4,32,1024]{2,1,0:T(8,128)(2,1)S(1)}, u32[]{:S(2)}, u32[]{:S(2)}) collective-permute-start(bf16[4,32,1024]{2,1,0:T(8,128)(2,1)S(1)} %pad_maximum_fusion.refs_6_), channel_id=1, source_target_pairs={{0,8},{1,9},{2,10},{3,11},{4,12},{5,13},{6,14},{7,15},{8,0},{9,1},... | collective-permute-start | bytes 786440 | tf_op jit(solution)/shard_map/ppermute | solution.py:422
  17.0 1.6 %collective-permute-start.6 = (bf16[4,32,1024]{2,1,0:T(8,128)(2,1)S(1)}, bf16[4,32,1024]{2,1,0:T(8,128)(2,1)S(1)}, u32[]{:S(2)}, u32[]{:S(2)}) collective-permute-start(bf16[4,32,1024]{2,1,0:T(8,128)(2,1)S(1)} %pad_maximum_fusion.refs_6_), channel_id=1, source_target_pairs={{0,4},{1,5},{2,6},{3,7},{4,0},{5,1},{6,2},{7,3},{8,12},{9,13},{10,... | collective-permute-start | bytes 786440 | tf_op jit(solution)/shard_map/ppermute | solution.py:422
  18.6 1.5 %collective-permute-start.9 = (bf16[128,1024]{1,0:T(8,128)(2,1)S(1)}, bf16[128,1024]{1,0:T(8,128)(2,1)S(1)}, u32[]{:S(2)}, u32[]{:S(2)}) collective-permute-start(bf16[128,1024]{1,0:T(8,128)(2,1)S(1)} %collective-permute-done.3.refs_3_), channel_id=1, source_target_pairs={{0,2},{1,3},{2,0},{3,1},{4,6},{5,7},{6,4},{7,5},{8,10},{9,11},{10,... | collective-permute-start | bytes 786440 | tf_op jit(solution)/shard_map/ppermute | solution.py:422
  20.1 0.9 copy-done.3
  21.0 0.7 copy-done.7
  21.7 0.7 copy-done.8
  22.4 0.7 copy-done.9
  23.1 6.2 %collective-permute-done.5.refs_10_ = bf16[4,32,1024]{2,1,0:T(8,128)(2,1)S(1)} collective-permute-done((bf16[4,32,1024]{2,1,0:T(8,128)(2,1)S(1)}, bf16[4,32,1024]{2,1,0:T(8,128)(2,1)S(1)}, u32[]{:S(2)}, u32[]{:S(2)}) %collective-permute-start.5) | collective-permute-done | bytes 262176 | tf_op jit(solution)/shard_map/ppermute | solution.py:422
  29.6 1.5 %collective-permute-start.13 = (bf16[4,32,1024]{2,1,0:T(8,128)(2,1)S(1)}, bf16[4,32,1024]{2,1,0:T(8,128)(2,1)S(1)}, u32[]{:S(2)}, u32[]{:S(2)}) collective-permute-start(bf16[4,32,1024]{2,1,0:T(8,128)(2,1)S(1)} %collective-permute-done.5.refs_10_), channel_id=1, source_target_pairs={{0,4},{1,5},{2,6},{3,7},{4,0},{5,1},{6,2},{7,3},{8,12},{9,13},{10,... | collective-permute-start | bytes 786440 | tf_op jit(solution)/shard_map/ppermute | solution.py:422
  31.1 1.5 %collective-permute-start.15 = (f32[16,128]{1,0:T(8,128)S(1)}, f32[16,128]{1,0:T(8,128)S(1)}, u32[]{:S(2)}, u32[]{:S(2)}) collective-permute-start(f32[16,128]{1,0:T(8,128)S(1)} %get-tuple-element.85.first_ref), channel_id=1, source_target_pairs={{0,2},{1,3},{2,0},{3,1},{4,6},{5,7},{6,4},{7,5},{8,10},{9,11},{10,... | collective-permute-start | bytes 24584 | tf_op jit(solution)/shard_map/ppermute | solution.py:422
  32.6 2.2 %collective-permute-done.15.second_ref = f32[16,128]{1,0:T(8,128)S(1)} collective-permute-done((f32[16,128]{1,0:T(8,128)S(1)}, f32[16,128]{1,0:T(8,128)S(1)}, u32[]{:S(2)}, u32[]{:S(2)}) %collective-permute-start.15) | collective-permute-done | bytes 8224 | tf_op jit(solution)/shard_map/ppermute | solution.py:422
  34.7 2.3 %collective-permute-start.16 = (f32[2,16,128]{2,1,0:T(8,128)S(1)}, f32[2,16,128]{2,1,0:T(8,128)S(1)}, u32[]{:S(2)}, u32[]{:S(2)}) collective-permute-start(f32[2,16,128]{2,1,0:T(8,128)S(1)} %shard_map.102.first_ref), channel_id=1, source_target_pairs={{0,8},{1,9},{2,10},{3,11},{4,12},{5,13},{6,14},{7,15},{8,0},{9,1},... | collective-permute-start | bytes 49160 | tf_op jit(solution)/shard_map/ppermute | solution.py:422
  37.1 0.5 collective-permute-start.12
  37.6 1.8 %collective-permute-done.16.second_ref = f32[2,16,128]{2,1,0:T(8,128)S(1)} collective-permute-done((f32[2,16,128]{2,1,0:T(8,128)S(1)}, f32[2,16,128]{2,1,0:T(8,128)S(1)}, u32[]{:S(2)}, u32[]{:S(2)}) %collective-permute-start.16) | collective-permute-done | bytes 16416 | tf_op jit(solution)/shard_map/ppermute | solution.py:422
  39.4 0.5 collective-permute-start.14
  39.9 1.0 collective-permute-done.11.refs_9_
  40.9 0.4 collective-permute-done.14.refs_13_
  41.3 4.0 %shard_map.104 = (bf16[2,64,1024]{2,1,0:T(8,128)(2,1)S(1)}, bf16[2,64,1024]{2,1,0:T(8,128)(2,1)S(1)}, bf16[2,64,1024]{2,1,0:T(8,128)(2,1)S(1)}, bf16[2,64,1024]{2,1,0:T(8,128)(2,1)S(1)}) custom-call(s32[6]{0:T(128)S(1)} %stack.42.place_ref.refs_0_, f32[1,1024]{1,0:T(1,128)S(1)} %get-tuple-element.71.refs_1_, ...), custom_call_target="tpu_custom_call" | custom-call | flops 1140850688 | bytes 4194304 | tf_op jit(solution)/shard_map/pallas_call | solution.py:171
  45.3 1.6 %collective-permute-start.18 = (bf16[2,64,1024]{2,1,0:T(8,128)(2,1)S(1)}, bf16[2,64,1024]{2,1,0:T(8,128)(2,1)S(1)}, u32[]{:S(2)}, u32[]{:S(2)}) collective-permute-start(bf16[2,64,1024]{2,1,0:T(8,128)(2,1)S(1)} %get-tuple-element.88), channel_id=1, source_target_pairs={{0,2},{1,3},{2,0},{3,1},{4,6},{5,7},{6,4},{7,5},{8,10},{9,11},{10,... | collective-permute-start | bytes 786440 | tf_op jit(solution)/shard_map/ppermute | solution.py:422
  46.9 0.5 collective-permute-start.19
  47.4 1.3 %collective-permute-start.20 = (f32[2,2,16,128]{3,2,1,0:T(8,128)S(1)}, f32[2,2,16,128]{3,2,1,0:T(8,128)S(1)}, u32[]{:S(2)}, u32[]{:S(2)}) collective-permute-start(f32[2,2,16,128]{3,2,1,0:T(8,128)S(1)} %shard_map.103.refs_14_.refs_3_), channel_id=1, source_target_pairs={{0,4},{1,5},{2,6},{3,7},{4,0},{5,1},{6,2},{7,3},{8,12},{9,13},{10,... | collective-permute-start | bytes 98312 | tf_op jit(solution)/shard_map/ppermute | solution.py:422
  48.7 1.3 %shard_map.105 = (bf16[704,1024]{1,0:T(8,128)(2,1)S(1)}, bf16[704,1024]{1,0:T(8,128)(2,1)S(1)}, bf16[1024,768]{1,0:T(8,128)(2,1)S(1)}) custom-call(bf16[704,1024]{1,0:T(8,128)(2,1)S(1)} %bitcast.24, bf16[704,1024]{1,0:T(8,128)(2,1)S(1)} %bitcast.26, bf16[704,1024]{1,0:T(8,128)(2,1)S(1)} %bitcast.22, bf16[2,64,1024]{2,1,0:T(8,128)(2,1)S(1)} %get-tuple-element.87.after_ref.refs_0_), custom_call_target="tpu_custom_call" | custom-call | bytes 8650752 | tf_op jit(solution)/shard_map/pallas_call | solution.py:361
  50.0 1.4 %collective-permute-done.20.refs_3_ = f32[2,2,16,128]{3,2,1,0:T(8,128)S(1)} collective-permute-done((f32[2,2,16,128]{3,2,1,0:T(8,128)S(1)}, f32[2,2,16,128]{3,2,1,0:T(8,128)S(1)}, u32[]{:S(2)}, u32[]{:S(2)}) %collective-permute-start.20) | collective-permute-done | bytes 32800 | tf_op jit(solution)/shard_map/ppermute | solution.py:422
  51.3 2.4 %collective-permute-done.18.refs_1_ = bf16[2,64,1024]{2,1,0:T(8,128)(2,1)S(1)} collective-permute-done((bf16[2,64,1024]{2,1,0:T(8,128)(2,1)S(1)}, bf16[2,64,1024]{2,1,0:T(8,128)(2,1)S(1)}, u32[]{:S(2)}, u32[]{:S(2)}) %collective-permute-start.18) | collective-permute-done | bytes 262176 | tf_op jit(solution)/shard_map/ppermute | solution.py:422
  53.7 1.2 collective-permute-done.19.refs_1_.after_ref.refs_4_
  55.0 0.6 collective-permute-start.22
  55.6 1.4 %collective-permute-start.21 = (bf16[64,1024]{1,0:T(8,128)(2,1)S(1)}, bf16[64,1024]{1,0:T(8,128)(2,1)S(1)}, u32[]{:S(2)}, u32[]{:S(2)}) collective-permute-start(bf16[64,1024]{1,0:T(8,128)(2,1)S(1)} %shard_map.106), channel_id=1, source_target_pairs={{0,16},{16,0},{1,17},{17,1},{2,18},{18,2},{3,19},{19,3},{4,20},{20... | collective-permute-start | bytes 393224 | tf_op jit(solution)/shard_map/ppermute | solution.py:419
  57.0 1.4 %shard_map.108 = (bf16[704,1024]{1,0:T(8,128)(2,1)S(1)}, bf16[704,1024]{1,0:T(8,128)(2,1)S(1)}, bf16[1024,768]{1,0:T(8,128)(2,1)S(1)}) custom-call(bf16[704,1024]{1,0:T(8,128)(2,1)S(1)} %collective-permute-done.7.gate_hbm, bf16[704,1024]{1,0:T(8,128)(2,1)S(1)} %collective-permute-done.8.up_hbm, ...), custom_call_target="tpu_custom_call" | custom-call | bytes 8650752 | tf_op jit(solution)/shard_map/pallas_call | solution.py:361
  58.5 1.5 %collective-permute-done.22.refs_5_ = bf16[64,1024]{1,0:T(8,128)(2,1)S(1)} collective-permute-done((bf16[64,1024]{1,0:T(8,128)(2,1)S(1)}, bf16[64,1024]{1,0:T(8,128)(2,1)S(1)}, u32[]{:S(2)}, u32[]{:S(2)}) %collective-permute-start.22) | collective-permute-done | bytes 131104 | tf_op jit(solution)/shard_map/ppermute | solution.py:422
  60.0 0.7 collective-permute-done.21.refs_2_
  60.9 1.6 %collective-permute-start.23 = (bf16[128,1024]{1,0:T(8,128)(2,1)S(1)}, bf16[128,1024]{1,0:T(8,128)(2,1)S(1)}, u32[]{:S(2)}, u32[]{:S(2)}) collective-permute-start(bf16[128,1024]{1,0:T(8,128)(2,1)S(1)} %get-tuple-element.121.refs_1_), channel_id=1, source_target_pairs={{0,2},{1,3},{2,0},{3,1},{4,6},{5,7},{6,4},{7,5},{8,10},{9,11},{10,... | collective-permute-start | bytes 786440 | tf_op jit(solution)/shard_map/ppermute | solution.py:422
  62.5 2.3 %collective-permute-start.24 = (bf16[128,1024]{1,0:T(8,128)(2,1)S(1)}, bf16[128,1024]{1,0:T(8,128)(2,1)S(1)}, u32[]{:S(2)}, u32[]{:S(2)}) collective-permute-start(bf16[128,1024]{1,0:T(8,128)(2,1)S(1)} %get-tuple-element.121.refs_1_), channel_id=1, source_target_pairs={{0,8},{1,9},{2,10},{3,11},{4,12},{5,13},{6,14},{7,15},{8,0},{9,1},... | collective-permute-start | bytes 786440 | tf_op jit(solution)/shard_map/ppermute | solution.py:422
  64.8 2.6 %collective-permute-done.23.refs_2_ = bf16[128,1024]{1,0:T(8,128)(2,1)S(1)} collective-permute-done((bf16[128,1024]{1,0:T(8,128)(2,1)S(1)}, bf16[128,1024]{1,0:T(8,128)(2,1)S(1)}, u32[]{:S(2)}, u32[]{:S(2)}) %collective-permute-start.23) | collective-permute-done | bytes 262176 | tf_op jit(solution)/shard_map/ppermute | solution.py:422
  67.4 3.4 %shard_map.110 = (bf16[1024,128]{1,0:T(8,128)(2,1)S(1)}, bf16[1024,128]{1,0:T(8,128)(2,1)S(1)}) custom-call(s32[6]{0:T(128)S(1)} %stack.42.place_ref.refs_0_, bf16[128,1024]{1,0:T(8,128)(2,1)S(1)} %get-tuple-element.121.refs_1_, bf16[128,1024]{1,0:T(8,128)(2,1)S(1)} %collective-permute-done.23.refs_2_, f32[2,2,16,128]{3,2,1,0:T(8,128)S(1)} %shard_map.103.refs_14_.refs_3_, ...), custom_call_target="tpu_custom_call" | custom-call | flops 2214592512 | bytes 9699328 | tf_op jit(solution)/shard_map/pallas_call | solution.py:284
  70.7 4.1 %collective-permute-done.24.refs_1_ = bf16[128,1024]{1,0:T(8,128)(2,1)S(1)} collective-permute-done((bf16[128,1024]{1,0:T(8,128)(2,1)S(1)}, bf16[128,1024]{1,0:T(8,128)(2,1)S(1)}, u32[]{:S(2)}, u32[]{:S(2)}) %collective-permute-start.24) | collective-permute-done | bytes 262176 | tf_op jit(solution)/shard_map/ppermute | solution.py:422
  75.2 7.1 %collective-permute-done.28.refs_1_ = bf16[128,1024]{1,0:T(8,128)(2,1)S(1)} collective-permute-done((bf16[128,1024]{1,0:T(8,128)(2,1)S(1)}, bf16[128,1024]{1,0:T(8,128)(2,1)S(1)}, u32[]{:S(2)}, u32[]{:S(2)}) %collective-permute-start.28) | collective-permute-done | bytes 262176 | tf_op jit(solution)/shard_map/ppermute | solution.py:422
  82.9 3.4 %shard_map.111 = (bf16[1024,128]{1,0:T(8,128)(2,1)S(1)}, bf16[1024,128]{1,0:T(8,128)(2,1)S(1)}) custom-call(s32[6]{0:T(128)S(1)} %stack.42.place_ref.refs_0_, bf16[128,1024]{1,0:T(8,128)(2,1)S(1)} %collective-permute-done.24.refs_1_, bf16[128,1024]{1,0:T(8,128)(2,1)S(1)} %collective-permute-done.25.refs_2_, ...), custom_call_target="tpu_custom_call" | custom-call | flops 2214592512 | bytes 9699328 | tf_op jit(solution)/shard_map/pallas_call | solution.py:284
  86.2 1.7 %collective-permute-start.26 = (bf16[1024,128]{1,0:T(8,128)(2,1)S(1)}, bf16[1024,128]{1,0:T(8,128)(2,1)S(1)}, u32[]{:S(2)}, u32[]{:S(2)}) collective-permute-start(bf16[1024,128]{1,0:T(8,128)(2,1)S(1)} %get-tuple-element.117.refs_10_), channel_id=1, source_target_pairs={{0,2},{1,3},{2,0},{3,1},{4,6},{5,7},{6,4},{7,5},{8,10},{9,11},{10,... | collective-permute-start | bytes 786440 | tf_op jit(solution)/shard_map/ppermute | solution.py:422
  88.0 0.8 collective-permute-done.32.refs_1_
  89.1 2.0 %collective-permute-done.29.refs_2_ = bf16[128,1024]{1,0:T(8,128)(2,1)S(1)} collective-permute-done((bf16[128,1024]{1,0:T(8,128)(2,1)S(1)}, bf16[128,1024]{1,0:T(8,128)(2,1)S(1)}, u32[]{:S(2)}, u32[]{:S(2)}) %collective-permute-start.29) | collective-permute-done | bytes 262176 | tf_op jit(solution)/shard_map/ppermute | solution.py:422
  91.1 3.4 %shard_map.113 = (bf16[1024,128]{1,0:T(8,128)(2,1)S(1)}, bf16[1024,128]{1,0:T(8,128)(2,1)S(1)}) custom-call(s32[6]{0:T(128)S(1)} %stack.42.place_ref.refs_0_, bf16[128,1024]{1,0:T(8,128)(2,1)S(1)} %collective-permute-done.28.refs_1_, bf16[128,1024]{1,0:T(8,128)(2,1)S(1)} %collective-permute-done.29.refs_2_, ...), custom_call_target="tpu_custom_call" | custom-call | flops 2214592512 | bytes 9699328 | tf_op jit(solution)/shard_map/pallas_call | solution.py:284
  94.6 2.2 %collective-permute-done.26.refs_1_ = bf16[1024,128]{1,0:T(8,128)(2,1)S(1)} collective-permute-done((bf16[1024,128]{1,0:T(8,128)(2,1)S(1)}, bf16[1024,128]{1,0:T(8,128)(2,1)S(1)}, u32[]{:S(2)}, u32[]{:S(2)}) %collective-permute-start.26) | collective-permute-done | bytes 262176 | tf_op jit(solution)/shard_map/ppermute | solution.py:422
  96.8 2.4 %collective-permute-start.27 = (bf16[1024,128]{1,0:T(8,128)(2,1)S(1)}, bf16[1024,128]{1,0:T(8,128)(2,1)S(1)}, u32[]{:S(2)}, u32[]{:S(2)}) collective-permute-start(bf16[1024,128]{1,0:T(8,128)(2,1)S(1)} %shard_map.112.refs_10_), channel_id=1, source_target_pairs={{0,8},{1,9},{2,10},{3,11},{4,12},{5,13},{6,14},{7,15},{8,0},{9,1},... | collective-permute-start | bytes 786440 | tf_op jit(solution)/shard_map/ppermute | solution.py:422
  99.2 3.1 %collective-permute-done.33.refs_2_ = bf16[128,1024]{1,0:T(8,128)(2,1)S(1)} collective-permute-done((bf16[128,1024]{1,0:T(8,128)(2,1)S(1)}, bf16[128,1024]{1,0:T(8,128)(2,1)S(1)}, u32[]{:S(2)}, u32[]{:S(2)}) %collective-permute-start.33) | collective-permute-done | bytes 262176 | tf_op jit(solution)/shard_map/ppermute | solution.py:422
  102.4 3.4 %shard_map.115 = (bf16[1024,128]{1,0:T(8,128)(2,1)S(1)}, bf16[1024,128]{1,0:T(8,128)(2,1)S(1)}) custom-call(s32[6]{0:T(128)S(1)} %stack.42.place_ref.refs_0_, bf16[128,1024]{1,0:T(8,128)(2,1)S(1)} %collective-permute-done.32.refs_1_, bf16[128,1024]{1,0:T(8,128)(2,1)S(1)} %collective-permute-done.33.refs_2_, ...), custom_call_target="tpu_custom_call" | custom-call | flops 2214592512 | bytes 9699328 | tf_op jit(solution)/shard_map/pallas_call | solution.py:284
  105.7 0.5 collective-permute-start.34
  106.3 1.6 %collective-permute-start.36 = (bf16[1024,128]{1,0:T(8,128)(2,1)S(1)}, bf16[1024,128]{1,0:T(8,128)(2,1)S(1)}, u32[]{:S(2)}, u32[]{:S(2)}) collective-permute-start(bf16[1024,128]{1,0:T(8,128)(2,1)S(1)} %get-tuple-element.124.refs_10_), channel_id=1, source_target_pairs={{0,2},{1,3},{2,0},{3,1},{4,6},{5,7},{6,4},{7,5},{8,10},{9,11},{10,... | collective-permute-start | bytes 786440 | tf_op jit(solution)/shard_map/ppermute | solution.py:422
  107.9 1.9 %collective-permute-start.31 = (bf16[1024,128]{1,0:T(8,128)(2,1)S(1)}, bf16[1024,128]{1,0:T(8,128)(2,1)S(1)}, u32[]{:S(2)}, u32[]{:S(2)}) collective-permute-start(bf16[1024,128]{1,0:T(8,128)(2,1)S(1)} %shard_map.114), channel_id=1, source_target_pairs={{0,12},{1,13},{2,14},{3,15},{4,8},{5,9},{6,10},{7,11},{8,4},{9,5},... | collective-permute-start | bytes 786440 | tf_op jit(solution)/shard_map/ppermute | solution.py:422
  109.8 4.5 %collective-permute-done.34.refs_1_ = bf16[1024,128]{1,0:T(8,128)(2,1)S(1)} collective-permute-done((bf16[1024,128]{1,0:T(8,128)(2,1)S(1)}, bf16[1024,128]{1,0:T(8,128)(2,1)S(1)}, u32[]{:S(2)}, u32[]{:S(2)}) %collective-permute-start.34) | collective-permute-done | bytes 262176 | tf_op jit(solution)/shard_map/ppermute | solution.py:422
  114.4 1.7 %collective-permute-start.35 = (bf16[1024,128]{1,0:T(8,128)(2,1)S(1)}, bf16[1024,128]{1,0:T(8,128)(2,1)S(1)}, u32[]{:S(2)}, u32[]{:S(2)}) collective-permute-start(bf16[1024,128]{1,0:T(8,128)(2,1)S(1)} %shard_map.116), channel_id=1, source_target_pairs={{0,4},{1,5},{2,6},{3,7},{4,0},{5,1},{6,2},{7,3},{8,12},{9,13},{10,... | collective-permute-start | bytes 786440 | tf_op jit(solution)/shard_map/ppermute | solution.py:422
  116.0 1.1 collective-permute-done.36.refs_4_
  117.1 1.1 collective-permute-done.31.refs_2_
  118.2 2.8 %collective-permute-done.35.refs_3_ = bf16[1024,128]{1,0:T(8,128)(2,1)S(1)} collective-permute-done((bf16[1024,128]{1,0:T(8,128)(2,1)S(1)}, bf16[1024,128]{1,0:T(8,128)(2,1)S(1)}, u32[]{:S(2)}, u32[]{:S(2)}) %collective-permute-start.35) | collective-permute-done | bytes 262176 | tf_op jit(solution)/shard_map/ppermute | solution.py:422
  121.0 1.0 shard_map.117
  (52 shorter events, 2.5 us)
Async XLA Ops:
  0.0 13.8 %collective-permute-start.3 = (bf16[128,1024]{1,0:T(8,128)(2,1)}, bf16[128,1024]{1,0:T(8,128)(2,1)S(1)}, u32[]{:S(2)}, u32[]{:S(2)}) collective-permute-start(bf16[128,1024]{1,0:T(8,128)(2,1)} %tokens_ref.2), channel_id=1, source_target_pairs={{0,16},{16,0},{1,17},{17,1},{2,18},{18,2},{3,19},{19,3},{4,20},{20... | collective-permute-start | bytes 786440 | tf_op jit(solution)/shard_map/ppermute | solution.py:419
  2.9 10.9 %collective-permute-start.4 = (bf16[128,1024]{1,0:T(8,128)(2,1)}, bf16[128,1024]{1,0:T(8,128)(2,1)S(1)}, u32[]{:S(2)}, u32[]{:S(2)}) collective-permute-start(bf16[128,1024]{1,0:T(8,128)(2,1)} %tokens_ref.2), channel_id=1, source_target_pairs={{0,2},{1,3},{2,0},{3,1},{4,6},{5,7},{6,4},{7,5},{8,10},{9,11},{10,... | collective-permute-start | bytes 786440 | tf_op jit(solution)/shard_map/ppermute | solution.py:422
  4.5 0.9 copy-start.5
  5.5 0.8 copy-start.6
  7.3 6.5 %collective-permute-start.1 = (bf16[32,1024]{1,0:T(8,128)(2,1)S(1)}, bf16[32,1024]{1,0:T(8,128)(2,1)S(1)}, u32[]{:S(2)}, u32[]{:S(2)}) collective-permute-start(bf16[32,1024]{1,0:T(8,128)(2,1)S(1)} %get-tuple-element.67), channel_id=1, source_target_pairs={{0,2},{1,3},{2,0},{3,1},{4,6},{5,7},{6,4},{7,5},{8,10},{9,11},{10,... | collective-permute-start | bytes 196616 | tf_op jit(solution)/shard_map/ppermute | solution.py:422
  7.8 5.9 %collective-permute-start.2 = (bf16[32,1024]{1,0:T(8,128)(2,1)S(1)}, bf16[32,1024]{1,0:T(8,128)(2,1)S(1)}, u32[]{:S(2)}, u32[]{:S(2)}) collective-permute-start(bf16[32,1024]{1,0:T(8,128)(2,1)S(1)} %get-tuple-element.68), channel_id=1, source_target_pairs={{0,18},{1,19},{2,16},{3,17},{4,22},{5,23},{6,20},{7,21},{8,26},{9,... | collective-permute-start | bytes 196616 | tf_op jit(solution)/shard_map/ppermute | solution.py:452
  9.3 4.4 %collective-permute-start = (bf16[32,1024]{1,0:T(8,128)(2,1)S(1)}, bf16[32,1024]{1,0:T(8,128)(2,1)S(1)}, u32[]{:S(2)}, u32[]{:S(2)}) collective-permute-start(bf16[32,1024]{1,0:T(8,128)(2,1)S(1)} %get-tuple-element.66), channel_id=1, source_target_pairs={{0,16},{16,0},{1,17},{17,1},{2,18},{18,2},{3,19},{19,3},{4,20},{20... | collective-permute-start | bytes 196616 | tf_op jit(solution)/shard_map/ppermute | solution.py:419
  13.8 15.7 %collective-permute-start.7 = (bf16[704,1024]{1,0:T(8,128)(2,1)}, bf16[704,1024]{1,0:T(8,128)(2,1)S(1)}, u32[]{:S(2)}, u32[]{:S(2)}) collective-permute-start(bf16[704,1024]{1,0:T(8,128)(2,1)} %bitcast.23), channel_id=1, source_target_pairs={{0,1},{1,0},{2,3},{3,2},{4,5},{5,4},{6,7},{7,6},{8,9},{9,8},{10,11... | collective-permute-start | bytes 4325384 | tf_op jit(solution)/shard_map/ppermute | solution.py:422
  13.9 15.6 %collective-permute-start.8 = (bf16[704,1024]{1,0:T(8,128)(2,1)}, bf16[704,1024]{1,0:T(8,128)(2,1)S(1)}, u32[]{:S(2)}, u32[]{:S(2)}) collective-permute-start(bf16[704,1024]{1,0:T(8,128)(2,1)} %bitcast.25), channel_id=1, source_target_pairs={{0,1},{1,0},{2,3},{3,2},{4,5},{5,4},{6,7},{7,6},{8,9},{9,8},{10,11... | collective-permute-start | bytes 4325384 | tf_op jit(solution)/shard_map/ppermute | solution.py:422
  14.4 14.9 %collective-permute-start.5 = (bf16[4,32,1024]{2,1,0:T(8,128)(2,1)S(1)}, bf16[4,32,1024]{2,1,0:T(8,128)(2,1)S(1)}, u32[]{:S(2)}, u32[]{:S(2)}) collective-permute-start(bf16[4,32,1024]{2,1,0:T(8,128)(2,1)S(1)} %pad_maximum_fusion.refs_6_), channel_id=1, source_target_pairs={{0,8},{1,9},{2,10},{3,11},{4,12},{5,13},{6,14},{7,15},{8,0},{9,1},... | collective-permute-start | bytes 786440 | tf_op jit(solution)/shard_map/ppermute | solution.py:422
  17.0 12.5 %collective-permute-start.6 = (bf16[4,32,1024]{2,1,0:T(8,128)(2,1)S(1)}, bf16[4,32,1024]{2,1,0:T(8,128)(2,1)S(1)}, u32[]{:S(2)}, u32[]{:S(2)}) collective-permute-start(bf16[4,32,1024]{2,1,0:T(8,128)(2,1)S(1)} %pad_maximum_fusion.refs_6_), channel_id=1, source_target_pairs={{0,4},{1,5},{2,6},{3,7},{4,0},{5,1},{6,2},{7,3},{8,12},{9,13},{10,... | collective-permute-start | bytes 786440 | tf_op jit(solution)/shard_map/ppermute | solution.py:422
  18.6 10.9 %collective-permute-start.9 = (bf16[128,1024]{1,0:T(8,128)(2,1)S(1)}, bf16[128,1024]{1,0:T(8,128)(2,1)S(1)}, u32[]{:S(2)}, u32[]{:S(2)}) collective-permute-start(bf16[128,1024]{1,0:T(8,128)(2,1)S(1)} %collective-permute-done.3.refs_3_), channel_id=1, source_target_pairs={{0,2},{1,3},{2,0},{3,1},{4,6},{5,7},{6,4},{7,5},{8,10},{9,11},{10,... | collective-permute-start | bytes 786440 | tf_op jit(solution)/shard_map/ppermute | solution.py:422
  20.1 0.9 copy-start.3
  21.0 0.7 copy-start.7
  21.7 0.7 copy-start.8
  22.4 0.7 copy-start.9
  29.5 11.8 %collective-permute-start.17 = (bf16[704,1024]{1,0:T(8,128)(2,1)}, bf16[704,1024]{1,0:T(8,128)(2,1)S(1)}, u32[]{:S(2)}, u32[]{:S(2)}) collective-permute-start(bf16[704,1024]{1,0:T(8,128)(2,1)} %bitcast.21), channel_id=1, source_target_pairs={{0,1},{1,0},{2,3},{3,2},{4,5},{5,4},{6,7},{7,6},{8,9},{9,8},{10,11... | collective-permute-start | bytes 4325384 | tf_op jit(solution)/shard_map/ppermute | solution.py:422
  29.6 9.8 %collective-permute-start.13 = (bf16[4,32,1024]{2,1,0:T(8,128)(2,1)S(1)}, bf16[4,32,1024]{2,1,0:T(8,128)(2,1)S(1)}, u32[]{:S(2)}, u32[]{:S(2)}) collective-permute-start(bf16[4,32,1024]{2,1,0:T(8,128)(2,1)S(1)} %collective-permute-done.5.refs_10_), channel_id=1, source_target_pairs={{0,4},{1,5},{2,6},{3,7},{4,0},{5,1},{6,2},{7,3},{8,12},{9,13},{10,... | collective-permute-start | bytes 786440 | tf_op jit(solution)/shard_map/ppermute | solution.py:422
  31.1 3.7 %collective-permute-start.15 = (f32[16,128]{1,0:T(8,128)S(1)}, f32[16,128]{1,0:T(8,128)S(1)}, u32[]{:S(2)}, u32[]{:S(2)}) collective-permute-start(f32[16,128]{1,0:T(8,128)S(1)} %get-tuple-element.85.first_ref), channel_id=1, source_target_pairs={{0,2},{1,3},{2,0},{3,1},{4,6},{5,7},{6,4},{7,5},{8,10},{9,11},{10,... | collective-permute-start | bytes 24584 | tf_op jit(solution)/shard_map/ppermute | solution.py:422
  34.7 4.6 %collective-permute-start.16 = (f32[2,16,128]{2,1,0:T(8,128)S(1)}, f32[2,16,128]{2,1,0:T(8,128)S(1)}, u32[]{:S(2)}, u32[]{:S(2)}) collective-permute-start(f32[2,16,128]{2,1,0:T(8,128)S(1)} %shard_map.102.first_ref), channel_id=1, source_target_pairs={{0,8},{1,9},{2,10},{3,11},{4,12},{5,13},{6,14},{7,15},{8,0},{9,1},... | collective-permute-start | bytes 49160 | tf_op jit(solution)/shard_map/ppermute | solution.py:422
  37.1 2.8 %collective-permute-start.10 = (bf16[4,32,1024]{2,1,0:T(8,128)(2,1)S(1)}, bf16[4,32,1024]{2,1,0:T(8,128)(2,1)S(1)}, u32[]{:S(2)}, u32[]{:S(2)}) collective-permute-start(bf16[4,32,1024]{2,1,0:T(8,128)(2,1)S(1)} %pad_maximum_fusion.refs_6_), channel_id=1, source_target_pairs={{0,1},{1,0},{2,3},{3,2},{4,5},{5,4},{6,7},{7,6},{8,9},{9,8},{10,11... | collective-permute-start | bytes 786440 | tf_op jit(solution)/shard_map/ppermute | solution.py:422
  37.1 3.8 %collective-permute-start.12 = (bf16[4,32,1024]{2,1,0:T(8,128)(2,1)S(1)}, bf16[4,32,1024]{2,1,0:T(8,128)(2,1)S(1)}, u32[]{:S(2)}, u32[]{:S(2)}) collective-permute-start(bf16[4,32,1024]{2,1,0:T(8,128)(2,1)S(1)} %collective-permute-done.5.refs_10_), channel_id=1, source_target_pairs={{0,1},{1,0},{2,3},{3,2},{4,5},{5,4},{6,7},{7,6},{8,9},{9,8},{10,11... | collective-permute-start | bytes 786440 | tf_op jit(solution)/shard_map/ppermute | solution.py:422
  39.4 1.5 %collective-permute-start.11 = (bf16[4,32,1024]{2,1,0:T(8,128)(2,1)S(1)}, bf16[4,32,1024]{2,1,0:T(8,128)(2,1)S(1)}, u32[]{:S(2)}, u32[]{:S(2)}) collective-permute-start(bf16[4,32,1024]{2,1,0:T(8,128)(2,1)S(1)} %collective-permute-done.6.refs_8_), channel_id=1, source_target_pairs={{0,1},{1,0},{2,3},{3,2},{4,5},{5,4},{6,7},{7,6},{8,9},{9,8},{10,11... | collective-permute-start | bytes 786440 | tf_op jit(solution)/shard_map/ppermute | solution.py:422
  39.4 1.9 %collective-permute-start.14 = (bf16[4,32,1024]{2,1,0:T(8,128)(2,1)S(1)}, bf16[4,32,1024]{2,1,0:T(8,128)(2,1)S(1)}, u32[]{:S(2)}, u32[]{:S(2)}) collective-permute-start(bf16[4,32,1024]{2,1,0:T(8,128)(2,1)S(1)} %collective-permute-done.13.refs_12_), channel_id=1, source_target_pairs={{0,1},{1,0},{2,3},{3,2},{4,5},{5,4},{6,7},{7,6},{8,9},{9,8},{10,11... | collective-permute-start | bytes 786440 | tf_op jit(solution)/shard_map/ppermute | solution.py:422
  41.3 7.4 %copy-start = (bf16[1,704,1024]{2,1,0:T(8,128)(2,1)S(1)}, bf16[1,704,1024]{2,1,0:T(8,128)(2,1)}, u32[]{:S(2)}) copy-start(bf16[1,704,1024]{2,1,0:T(8,128)(2,1)} %param.19) | copy-start | bytes 4325380
  41.3 7.4 %copy-start.1 = (bf16[1,1024,704]{1,2,0:T(8,128)(2,1)S(1)}, bf16[1,1024,704]{1,2,0:T(8,128)(2,1)}, u32[]{:S(2)}) copy-start(bf16[1,1024,704]{1,2,0:T(8,128)(2,1)} %param.17) | copy-start | bytes 4325380
  41.3 7.4 %copy-start.2 = (bf16[1,1024,704]{1,2,0:T(8,128)(2,1)S(1)}, bf16[1,1024,704]{1,2,0:T(8,128)(2,1)}, u32[]{:S(2)}) copy-start(bf16[1,1024,704]{1,2,0:T(8,128)(2,1)} %param.18) | copy-start | bytes 4325380
  45.3 8.4 %collective-permute-start.18 = (bf16[2,64,1024]{2,1,0:T(8,128)(2,1)S(1)}, bf16[2,64,1024]{2,1,0:T(8,128)(2,1)S(1)}, u32[]{:S(2)}, u32[]{:S(2)}) collective-permute-start(bf16[2,64,1024]{2,1,0:T(8,128)(2,1)S(1)} %get-tuple-element.88), channel_id=1, source_target_pairs={{0,2},{1,3},{2,0},{3,1},{4,6},{5,7},{6,4},{7,5},{8,10},{9,11},{10,... | collective-permute-start | bytes 786440 | tf_op jit(solution)/shard_map/ppermute | solution.py:422
  46.9 8.1 %collective-permute-start.19 = (bf16[2,64,1024]{2,1,0:T(8,128)(2,1)S(1)}, bf16[2,64,1024]{2,1,0:T(8,128)(2,1)S(1)}, u32[]{:S(2)}, u32[]{:S(2)}) collective-permute-start(bf16[2,64,1024]{2,1,0:T(8,128)(2,1)S(1)} %get-tuple-element.89), channel_id=1, source_target_pairs={{0,16},{16,0},{1,17},{17,1},{2,18},{18,2},{3,19},{19,3},{4,20},{20... | collective-permute-start | bytes 786440 | tf_op jit(solution)/shard_map/ppermute | solution.py:419
  47.4 3.9 %collective-permute-start.20 = (f32[2,2,16,128]{3,2,1,0:T(8,128)S(1)}, f32[2,2,16,128]{3,2,1,0:T(8,128)S(1)}, u32[]{:S(2)}, u32[]{:S(2)}) collective-permute-start(f32[2,2,16,128]{3,2,1,0:T(8,128)S(1)} %shard_map.103.refs_14_.refs_3_), channel_id=1, source_target_pairs={{0,4},{1,5},{2,6},{3,7},{4,0},{5,1},{6,2},{7,3},{8,12},{9,13},{10,... | collective-permute-start | bytes 98312 | tf_op jit(solution)/shard_map/ppermute | solution.py:422
  55.0 5.0 %collective-permute-start.22 = (bf16[64,1024]{1,0:T(8,128)(2,1)S(1)}, bf16[64,1024]{1,0:T(8,128)(2,1)S(1)}, u32[]{:S(2)}, u32[]{:S(2)}) collective-permute-start(bf16[64,1024]{1,0:T(8,128)(2,1)S(1)} %shard_map.107), channel_id=1, source_target_pairs={{0,2},{1,3},{2,0},{3,1},{4,6},{5,7},{6,4},{7,5},{8,10},{9,11},{10,... | collective-permute-start | bytes 393224 | tf_op jit(solution)/shard_map/ppermute | solution.py:422
  55.6 5.1 %copy-start.4 = (bf16[128,1024]{1,0:T(8,128)(2,1)S(1)}, bf16[128,1024]{1,0:T(8,128)(2,1)}, u32[]{:S(2)}) copy-start(bf16[128,1024]{1,0:T(8,128)(2,1)} %tokens_ref.2) | copy-start | bytes 786436
  55.6 5.1 %copy-start.10 = (f32[1024]{0:T(1024)S(1)}, f32[1024]{0:T(1024)}, u32[]{:S(2)}) copy-start(f32[1024]{0:T(1024)} %param.14) | copy-start | bytes 12292
  55.6 5.0 %collective-permute-start.21 = (bf16[64,1024]{1,0:T(8,128)(2,1)S(1)}, bf16[64,1024]{1,0:T(8,128)(2,1)S(1)}, u32[]{:S(2)}, u32[]{:S(2)}) collective-permute-start(bf16[64,1024]{1,0:T(8,128)(2,1)S(1)} %shard_map.106), channel_id=1, source_target_pairs={{0,16},{16,0},{1,17},{17,1},{2,18},{18,2},{3,19},{19,3},{4,20},{20... | collective-permute-start | bytes 393224 | tf_op jit(solution)/shard_map/ppermute | solution.py:419
  60.9 6.4 %collective-permute-start.23 = (bf16[128,1024]{1,0:T(8,128)(2,1)S(1)}, bf16[128,1024]{1,0:T(8,128)(2,1)S(1)}, u32[]{:S(2)}, u32[]{:S(2)}) collective-permute-start(bf16[128,1024]{1,0:T(8,128)(2,1)S(1)} %get-tuple-element.121.refs_1_), channel_id=1, source_target_pairs={{0,2},{1,3},{2,0},{3,1},{4,6},{5,7},{6,4},{7,5},{8,10},{9,11},{10,... | collective-permute-start | bytes 786440 | tf_op jit(solution)/shard_map/ppermute | solution.py:422
  62.5 12.3 %collective-permute-start.24 = (bf16[128,1024]{1,0:T(8,128)(2,1)S(1)}, bf16[128,1024]{1,0:T(8,128)(2,1)S(1)}, u32[]{:S(2)}, u32[]{:S(2)}) collective-permute-start(bf16[128,1024]{1,0:T(8,128)(2,1)S(1)} %get-tuple-element.121.refs_1_), channel_id=1, source_target_pairs={{0,8},{1,9},{2,10},{3,11},{4,12},{5,13},{6,14},{7,15},{8,0},{9,1},... | collective-permute-start | bytes 786440 | tf_op jit(solution)/shard_map/ppermute | solution.py:422
  74.8 7.4 %collective-permute-start.28 = (bf16[128,1024]{1,0:T(8,128)(2,1)S(1)}, bf16[128,1024]{1,0:T(8,128)(2,1)S(1)}, u32[]{:S(2)}, u32[]{:S(2)}) collective-permute-start(bf16[128,1024]{1,0:T(8,128)(2,1)S(1)} %collective-permute-done.24.refs_1_), channel_id=1, source_target_pairs={{0,4},{1,5},{2,6},{3,7},{4,0},{5,1},{6,2},{7,3},{8,12},{9,13},{10,... | collective-permute-start | bytes 786440 | tf_op jit(solution)/shard_map/ppermute | solution.py:422
  74.8 8.1 %collective-permute-start.25 = (bf16[128,1024]{1,0:T(8,128)(2,1)S(1)}, bf16[128,1024]{1,0:T(8,128)(2,1)S(1)}, u32[]{:S(2)}, u32[]{:S(2)}) collective-permute-start(bf16[128,1024]{1,0:T(8,128)(2,1)S(1)} %collective-permute-done.24.refs_1_), channel_id=1, source_target_pairs={{0,2},{1,3},{2,0},{3,1},{4,6},{5,7},{6,4},{7,5},{8,10},{9,11},{10,... | collective-permute-start | bytes 786440 | tf_op jit(solution)/shard_map/ppermute | solution.py:422
  82.2 6.5 %collective-permute-start.32 = (bf16[128,1024]{1,0:T(8,128)(2,1)S(1)}, bf16[128,1024]{1,0:T(8,128)(2,1)S(1)}, u32[]{:S(2)}, u32[]{:S(2)}) collective-permute-start(bf16[128,1024]{1,0:T(8,128)(2,1)S(1)} %get-tuple-element.121.refs_1_), channel_id=1, source_target_pairs={{0,4},{1,5},{2,6},{3,7},{4,0},{5,1},{6,2},{7,3},{8,12},{9,13},{10,... | collective-permute-start | bytes 786440 | tf_op jit(solution)/shard_map/ppermute | solution.py:422
  82.5 8.6 %collective-permute-start.29 = (bf16[128,1024]{1,0:T(8,128)(2,1)S(1)}, bf16[128,1024]{1,0:T(8,128)(2,1)S(1)}, u32[]{:S(2)}, u32[]{:S(2)}) collective-permute-start(bf16[128,1024]{1,0:T(8,128)(2,1)S(1)} %collective-permute-done.28.refs_1_), channel_id=1, source_target_pairs={{0,2},{1,3},{2,0},{3,1},{4,6},{5,7},{6,4},{7,5},{8,10},{9,11},{10,... | collective-permute-start | bytes 786440 | tf_op jit(solution)/shard_map/ppermute | solution.py:422
  86.2 10.5 %collective-permute-start.26 = (bf16[1024,128]{1,0:T(8,128)(2,1)S(1)}, bf16[1024,128]{1,0:T(8,128)(2,1)S(1)}, u32[]{:S(2)}, u32[]{:S(2)}) collective-permute-start(bf16[1024,128]{1,0:T(8,128)(2,1)S(1)} %get-tuple-element.117.refs_10_), channel_id=1, source_target_pairs={{0,2},{1,3},{2,0},{3,1},{4,6},{5,7},{6,4},{7,5},{8,10},{9,11},{10,... | collective-permute-start | bytes 786440 | tf_op jit(solution)/shard_map/ppermute | solution.py:422
  88.7 13.6 %collective-permute-start.33 = (bf16[128,1024]{1,0:T(8,128)(2,1)S(1)}, bf16[128,1024]{1,0:T(8,128)(2,1)S(1)}, u32[]{:S(2)}, u32[]{:S(2)}) collective-permute-start(bf16[128,1024]{1,0:T(8,128)(2,1)S(1)} %collective-permute-done.32.refs_1_), channel_id=1, source_target_pairs={{0,2},{1,3},{2,0},{3,1},{4,6},{5,7},{6,4},{7,5},{8,10},{9,11},{10,... | collective-permute-start | bytes 786440 | tf_op jit(solution)/shard_map/ppermute | solution.py:422
  94.5 13.3 %collective-permute-start.30 = (bf16[1024,128]{1,0:T(8,128)(2,1)S(1)}, bf16[1024,128]{1,0:T(8,128)(2,1)S(1)}, u32[]{:S(2)}, u32[]{:S(2)}) collective-permute-start(bf16[1024,128]{1,0:T(8,128)(2,1)S(1)} %get-tuple-element.120.refs_11_), channel_id=1, source_target_pairs={{0,2},{1,3},{2,0},{3,1},{4,6},{5,7},{6,4},{7,5},{8,10},{9,11},{10,... | collective-permute-start | bytes 786440 | tf_op jit(solution)/shard_map/ppermute | solution.py:422
  96.8 11.0 %collective-permute-start.27 = (bf16[1024,128]{1,0:T(8,128)(2,1)S(1)}, bf16[1024,128]{1,0:T(8,128)(2,1)S(1)}, u32[]{:S(2)}, u32[]{:S(2)}) collective-permute-start(bf16[1024,128]{1,0:T(8,128)(2,1)S(1)} %shard_map.112.refs_10_), channel_id=1, source_target_pairs={{0,8},{1,9},{2,10},{3,11},{4,12},{5,13},{6,14},{7,15},{8,0},{9,1},... | collective-permute-start | bytes 786440 | tf_op jit(solution)/shard_map/ppermute | solution.py:422
  105.7 8.6 %collective-permute-start.34 = (bf16[1024,128]{1,0:T(8,128)(2,1)S(1)}, bf16[1024,128]{1,0:T(8,128)(2,1)S(1)}, u32[]{:S(2)}, u32[]{:S(2)}) collective-permute-start(bf16[1024,128]{1,0:T(8,128)(2,1)S(1)} %get-tuple-element.123), channel_id=1, source_target_pairs={{0,2},{1,3},{2,0},{3,1},{4,6},{5,7},{6,4},{7,5},{8,10},{9,11},{10,... | collective-permute-start | bytes 786440 | tf_op jit(solution)/shard_map/ppermute | solution.py:422
  106.3 10.8 %collective-permute-start.36 = (bf16[1024,128]{1,0:T(8,128)(2,1)S(1)}, bf16[1024,128]{1,0:T(8,128)(2,1)S(1)}, u32[]{:S(2)}, u32[]{:S(2)}) collective-permute-start(bf16[1024,128]{1,0:T(8,128)(2,1)S(1)} %get-tuple-element.124.refs_10_), channel_id=1, source_target_pairs={{0,2},{1,3},{2,0},{3,1},{4,6},{5,7},{6,4},{7,5},{8,10},{9,11},{10,... | collective-permute-start | bytes 786440 | tf_op jit(solution)/shard_map/ppermute | solution.py:422
  107.9 10.2 %collective-permute-start.31 = (bf16[1024,128]{1,0:T(8,128)(2,1)S(1)}, bf16[1024,128]{1,0:T(8,128)(2,1)S(1)}, u32[]{:S(2)}, u32[]{:S(2)}) collective-permute-start(bf16[1024,128]{1,0:T(8,128)(2,1)S(1)} %shard_map.114), channel_id=1, source_target_pairs={{0,12},{1,13},{2,14},{3,15},{4,8},{5,9},{6,10},{7,11},{8,4},{9,5},... | collective-permute-start | bytes 786440 | tf_op jit(solution)/shard_map/ppermute | solution.py:422
  114.4 6.6 %collective-permute-start.35 = (bf16[1024,128]{1,0:T(8,128)(2,1)S(1)}, bf16[1024,128]{1,0:T(8,128)(2,1)S(1)}, u32[]{:S(2)}, u32[]{:S(2)}) collective-permute-start(bf16[1024,128]{1,0:T(8,128)(2,1)S(1)} %shard_map.116), channel_id=1, source_target_pairs={{0,4},{1,5},{2,6},{3,7},{4,0},{5,1},{6,2},{7,3},{8,12},{9,13},{10,... | collective-permute-start | bytes 786440 | tf_op jit(solution)/shard_map/ppermute | solution.py:422

commit v3 on v2

--- a/solution.py
+++ b/solution.py
@@ -147,7 +147,7 @@
             values = own[:, 2 * HEAD_DIM :]
             scores = dot_nt(queries, keys) * (1.0 / math.sqrt(HEAD_DIM))
             raised = jnp.where(causal, jnp.exp(jnp.where(causal, scores, 0.0)), 0.0)
-            probs = raised * (1.0 / jnp.sum(raised, axis=-1, keepdims=True))
+            probs = raised / jnp.sum(raised, axis=-1, keepdims=True)
             outs.append(
                 jnp.dot(
                     probs.astype(jnp.bfloat16), values, preferred_element_type=jnp.float32

time: 122 us -> 122 us (level)
  no operation moved by 1% of the time
where the time goes in v3:
time: 122 us
  waiting for transfers between devices  53 us (43%)
  starting transfers between devices  41.2 us (34%)
  Pallas kernels  22.6 us (19%)
  local copies, waits for them, and re-layouts  4.88 us (4%)
    ppermute x32, waiting for transfers between devices, swap_expert(): lax.ppermute(value, 'expert', [(e, e ^ mask) for e in range(expert_size)])  51.1 us
    ppermute x32, starting transfers between devices, swap_expert(): lax.ppermute(value, 'expert', [(e, e ^ mask) for e in range(expert_size)])  33.3 us
    pallas_call x4, Pallas kernels, expert_call(): pl.pallas_call(functools.partial(expert_kernel, tiles, pick), out_shape=(...  13.4 us
    ppermute x4, starting transfers between devices, swap_pair(): return lax.ppermute(value, 'fsdp', [(f, f ^ 1) for f in range(fsdp_size)])  6.37 us
    unnamed x22, local copies, waits for them, and re-layouts  4.8 us
    pallas_call x1, Pallas kernels, attention_call(): pl.pallas_call(functools.partial(attention_kernel, count, len(pieces)), o...  4.01 us
    pallas_call x2, Pallas kernels, load_call(): pl.pallas_call(load_kernel, out_shape=(jax.ShapeDtypeStruct(gate.shape, g...  2.71 us
  transfers between devices with their start and end apart: 37, of which 23 were waited for; matrix products, arithmetic and copies ran while one was open for 0% of the time, Pallas kernels for 14%

profile of v3, /device:TPU:0, one launch (start us, length us, event | category | flops | bytes accessed | tf_op | source)
XLA Modules:
  0.0 121.9 jit_solution(6340463784603425664)
XLA Ops:
  0.0 2.9 %collective-permute-start.3 = (bf16[128,1024]{1,0:T(8,128)(2,1)}, bf16[128,1024]{1,0:T(8,128)(2,1)S(1)}, u32[]{:S(2)}, u32[]{:S(2)}) collective-permute-start(bf16[128,1024]{1,0:T(8,128)(2,1)} %tokens_ref.2), channel_id=1, source_target_pairs={{0,16},{16,0},{1,17},{17,1},{2,18},{18,2},{3,19},{19,3},{4,20},{20... | collective-permute-start | bytes 786440 | tf_op jit(solution)/shard_map/ppermute | solution.py:419
  2.9 1.5 %collective-permute-start.4 = (bf16[128,1024]{1,0:T(8,128)(2,1)}, bf16[128,1024]{1,0:T(8,128)(2,1)S(1)}, u32[]{:S(2)}, u32[]{:S(2)}) collective-permute-start(bf16[128,1024]{1,0:T(8,128)(2,1)} %tokens_ref.2), channel_id=1, source_target_pairs={{0,2},{1,3},{2,0},{3,1},{4,6},{5,7},{6,4},{7,5},{8,10},{9,11},{10,... | collective-permute-start | bytes 786440 | tf_op jit(solution)/shard_map/ppermute | solution.py:422
  4.5 0.9 copy-done.5
  5.5 0.8 copy-done.6
  6.3 0.9 shard_map.100
  7.3 0.6 collective-permute-start.1
  7.8 1.5 %collective-permute-start.2 = (bf16[32,1024]{1,0:T(8,128)(2,1)S(1)}, bf16[32,1024]{1,0:T(8,128)(2,1)S(1)}, u32[]{:S(2)}, u32[]{:S(2)}) collective-permute-start(bf16[32,1024]{1,0:T(8,128)(2,1)S(1)} %get-tuple-element.68), channel_id=1, source_target_pairs={{0,18},{1,19},{2,16},{3,17},{4,22},{5,23},{6,20},{7,21},{8,26},{9,... | collective-permute-start | bytes 196616 | tf_op jit(solution)/shard_map/ppermute | solution.py:452
  9.3 1.5 %collective-permute-start = (bf16[32,1024]{1,0:T(8,128)(2,1)S(1)}, bf16[32,1024]{1,0:T(8,128)(2,1)S(1)}, u32[]{:S(2)}, u32[]{:S(2)}) collective-permute-start(bf16[32,1024]{1,0:T(8,128)(2,1)S(1)} %get-tuple-element.66), channel_id=1, source_target_pairs={{0,16},{16,0},{1,17},{17,1},{2,18},{18,2},{3,19},{19,3},{4,20},{20... | collective-permute-start | bytes 196616 | tf_op jit(solution)/shard_map/ppermute | solution.py:419
  10.8 2.9 %collective-permute-done.1 = bf16[32,1024]{1,0:T(8,128)(2,1)S(1)} collective-permute-done((bf16[32,1024]{1,0:T(8,128)(2,1)S(1)}, bf16[32,1024]{1,0:T(8,128)(2,1)S(1)}, u32[]{:S(2)}, u32[]{:S(2)}) %collective-permute-start.1) | collective-permute-done | bytes 65568 | tf_op jit(solution)/shard_map/ppermute | solution.py:422
  13.9 0.5 collective-permute-start.8
  14.4 2.6 %collective-permute-start.5 = (bf16[4,32,1024]{2,1,0:T(8,128)(2,1)S(1)}, bf16[4,32,1024]{2,1,0:T(8,128)(2,1)S(1)}, u32[]{:S(2)}, u32[]{:S(2)}) collective-permute-start(bf16[4,32,1024]{2,1,0:T(8,128)(2,1)S(1)} %pad_maximum_fusion.refs_6_), channel_id=1, source_target_pairs={{0,8},{1,9},{2,10},{3,11},{4,12},{5,13},{6,14},{7,15},{8,0},{9,1},... | collective-permute-start | bytes 786440 | tf_op jit(solution)/shard_map/ppermute | solution.py:422
  17.0 1.6 %collective-permute-start.6 = (bf16[4,32,1024]{2,1,0:T(8,128)(2,1)S(1)}, bf16[4,32,1024]{2,1,0:T(8,128)(2,1)S(1)}, u32[]{:S(2)}, u32[]{:S(2)}) collective-permute-start(bf16[4,32,1024]{2,1,0:T(8,128)(2,1)S(1)} %pad_maximum_fusion.refs_6_), channel_id=1, source_target_pairs={{0,4},{1,5},{2,6},{3,7},{4,0},{5,1},{6,2},{7,3},{8,12},{9,13},{10,... | collective-permute-start | bytes 786440 | tf_op jit(solution)/shard_map/ppermute | solution.py:422
  18.6 1.5 %collective-permute-start.9 = (bf16[128,1024]{1,0:T(8,128)(2,1)S(1)}, bf16[128,1024]{1,0:T(8,128)(2,1)S(1)}, u32[]{:S(2)}, u32[]{:S(2)}) collective-permute-start(bf16[128,1024]{1,0:T(8,128)(2,1)S(1)} %collective-permute-done.3.refs_3_), channel_id=1, source_target_pairs={{0,2},{1,3},{2,0},{3,1},{4,6},{5,7},{6,4},{7,5},{8,10},{9,11},{10,... | collective-permute-start | bytes 786440 | tf_op jit(solution)/shard_map/ppermute | solution.py:422
  20.1 0.9 copy-done.3
  21.0 0.7 copy-done.7
  21.7 0.7 copy-done.8
  22.4 0.7 copy-done.9
  23.1 6.2 %collective-permute-done.5.refs_10_ = bf16[4,32,1024]{2,1,0:T(8,128)(2,1)S(1)} collective-permute-done((bf16[4,32,1024]{2,1,0:T(8,128)(2,1)S(1)}, bf16[4,32,1024]{2,1,0:T(8,128)(2,1)S(1)}, u32[]{:S(2)}, u32[]{:S(2)}) %collective-permute-start.5) | collective-permute-done | bytes 262176 | tf_op jit(solution)/shard_map/ppermute | solution.py:422
  29.6 1.5 %collective-permute-start.13 = (bf16[4,32,1024]{2,1,0:T(8,128)(2,1)S(1)}, bf16[4,32,1024]{2,1,0:T(8,128)(2,1)S(1)}, u32[]{:S(2)}, u32[]{:S(2)}) collective-permute-start(bf16[4,32,1024]{2,1,0:T(8,128)(2,1)S(1)} %collective-permute-done.5.refs_10_), channel_id=1, source_target_pairs={{0,4},{1,5},{2,6},{3,7},{4,0},{5,1},{6,2},{7,3},{8,12},{9,13},{10,... | collective-permute-start | bytes 786440 | tf_op jit(solution)/shard_map/ppermute | solution.py:422
  31.1 1.5 %collective-permute-start.15 = (f32[16,128]{1,0:T(8,128)S(1)}, f32[16,128]{1,0:T(8,128)S(1)}, u32[]{:S(2)}, u32[]{:S(2)}) collective-permute-start(f32[16,128]{1,0:T(8,128)S(1)} %get-tuple-element.85.first_ref), channel_id=1, source_target_pairs={{0,2},{1,3},{2,0},{3,1},{4,6},{5,7},{6,4},{7,5},{8,10},{9,11},{10,... | collective-permute-start | bytes 24584 | tf_op jit(solution)/shard_map/ppermute | solution.py:422
  32.6 2.2 %collective-permute-done.15.second_ref = f32[16,128]{1,0:T(8,128)S(1)} collective-permute-done((f32[16,128]{1,0:T(8,128)S(1)}, f32[16,128]{1,0:T(8,128)S(1)}, u32[]{:S(2)}, u32[]{:S(2)}) %collective-permute-start.15) | collective-permute-done | bytes 8224 | tf_op jit(solution)/shard_map/ppermute | solution.py:422
  34.7 2.3 %collective-permute-start.16 = (f32[2,16,128]{2,1,0:T(8,128)S(1)}, f32[2,16,128]{2,1,0:T(8,128)S(1)}, u32[]{:S(2)}, u32[]{:S(2)}) collective-permute-start(f32[2,16,128]{2,1,0:T(8,128)S(1)} %shard_map.102.first_ref), channel_id=1, source_target_pairs={{0,8},{1,9},{2,10},{3,11},{4,12},{5,13},{6,14},{7,15},{8,0},{9,1},... | collective-permute-start | bytes 49160 | tf_op jit(solution)/shard_map/ppermute | solution.py:422
  37.1 0.5 collective-permute-start.12
  37.6 1.8 %collective-permute-done.16.second_ref = f32[2,16,128]{2,1,0:T(8,128)S(1)} collective-permute-done((f32[2,16,128]{2,1,0:T(8,128)S(1)}, f32[2,16,128]{2,1,0:T(8,128)S(1)}, u32[]{:S(2)}, u32[]{:S(2)}) %collective-permute-start.16) | collective-permute-done | bytes 16416 | tf_op jit(solution)/shard_map/ppermute | solution.py:422
  39.4 0.5 collective-permute-start.14
  39.9 1.0 collective-permute-done.11.refs_9_
  40.9 0.4 collective-permute-done.14.refs_13_
  41.3 4.0 %shard_map.104 = (bf16[2,64,1024]{2,1,0:T(8,128)(2,1)S(1)}, bf16[2,64,1024]{2,1,0:T(8,128)(2,1)S(1)}, bf16[2,64,1024]{2,1,0:T(8,128)(2,1)S(1)}, bf16[2,64,1024]{2,1,0:T(8,128)(2,1)S(1)}) custom-call(s32[6]{0:T(128)S(1)} %stack.42.place_ref.refs_0_, f32[1,1024]{1,0:T(1,128)S(1)} %get-tuple-element.71.refs_1_, ...), custom_call_target="tpu_custom_call" | custom-call | flops 1140850688 | bytes 4194304 | tf_op jit(solution)/shard_map/pallas_call | solution.py:171
  45.3 1.6 %collective-permute-start.18 = (bf16[2,64,1024]{2,1,0:T(8,128)(2,1)S(1)}, bf16[2,64,1024]{2,1,0:T(8,128)(2,1)S(1)}, u32[]{:S(2)}, u32[]{:S(2)}) collective-permute-start(bf16[2,64,1024]{2,1,0:T(8,128)(2,1)S(1)} %get-tuple-element.88), channel_id=1, source_target_pairs={{0,2},{1,3},{2,0},{3,1},{4,6},{5,7},{6,4},{7,5},{8,10},{9,11},{10,... | collective-permute-start | bytes 786440 | tf_op jit(solution)/shard_map/ppermute | solution.py:422
  46.9 0.5 collective-permute-start.19
  47.4 1.3 %collective-permute-start.20 = (f32[2,2,16,128]{3,2,1,0:T(8,128)S(1)}, f32[2,2,16,128]{3,2,1,0:T(8,128)S(1)}, u32[]{:S(2)}, u32[]{:S(2)}) collective-permute-start(f32[2,2,16,128]{3,2,1,0:T(8,128)S(1)} %shard_map.103.refs_14_.refs_3_), channel_id=1, source_target_pairs={{0,4},{1,5},{2,6},{3,7},{4,0},{5,1},{6,2},{7,3},{8,12},{9,13},{10,... | collective-permute-start | bytes 98312 | tf_op jit(solution)/shard_map/ppermute | solution.py:422
  48.7 1.3 %shard_map.105 = (bf16[704,1024]{1,0:T(8,128)(2,1)S(1)}, bf16[704,1024]{1,0:T(8,128)(2,1)S(1)}, bf16[1024,768]{1,0:T(8,128)(2,1)S(1)}) custom-call(bf16[704,1024]{1,0:T(8,128)(2,1)S(1)} %bitcast.24, bf16[704,1024]{1,0:T(8,128)(2,1)S(1)} %bitcast.26, bf16[704,1024]{1,0:T(8,128)(2,1)S(1)} %bitcast.22, bf16[2,64,1024]{2,1,0:T(8,128)(2,1)S(1)} %get-tuple-element.87.after_ref.refs_0_), custom_call_target="tpu_custom_call" | custom-call | bytes 8650752 | tf_op jit(solution)/shard_map/pallas_call | solution.py:361
  50.0 1.4 %collective-permute-done.20.refs_3_ = f32[2,2,16,128]{3,2,1,0:T(8,128)S(1)} collective-permute-done((f32[2,2,16,128]{3,2,1,0:T(8,128)S(1)}, f32[2,2,16,128]{3,2,1,0:T(8,128)S(1)}, u32[]{:S(2)}, u32[]{:S(2)}) %collective-permute-start.20) | collective-permute-done | bytes 32800 | tf_op jit(solution)/shard_map/ppermute | solution.py:422
  51.3 2.4 %collective-permute-done.18.refs_1_ = bf16[2,64,1024]{2,1,0:T(8,128)(2,1)S(1)} collective-permute-done((bf16[2,64,1024]{2,1,0:T(8,128)(2,1)S(1)}, bf16[2,64,1024]{2,1,0:T(8,128)(2,1)S(1)}, u32[]{:S(2)}, u32[]{:S(2)}) %collective-permute-start.18) | collective-permute-done | bytes 262176 | tf_op jit(solution)/shard_map/ppermute | solution.py:422
  53.7 1.2 collective-permute-done.19.refs_1_.after_ref.refs_4_
  55.0 0.6 collective-permute-start.22
  55.6 1.4 %collective-permute-start.21 = (bf16[64,1024]{1,0:T(8,128)(2,1)S(1)}, bf16[64,1024]{1,0:T(8,128)(2,1)S(1)}, u32[]{:S(2)}, u32[]{:S(2)}) collective-permute-start(bf16[64,1024]{1,0:T(8,128)(2,1)S(1)} %shard_map.106), channel_id=1, source_target_pairs={{0,16},{16,0},{1,17},{17,1},{2,18},{18,2},{3,19},{19,3},{4,20},{20... | collective-permute-start | bytes 393224 | tf_op jit(solution)/shard_map/ppermute | solution.py:419
  57.0 1.4 %shard_map.108 = (bf16[704,1024]{1,0:T(8,128)(2,1)S(1)}, bf16[704,1024]{1,0:T(8,128)(2,1)S(1)}, bf16[1024,768]{1,0:T(8,128)(2,1)S(1)}) custom-call(bf16[704,1024]{1,0:T(8,128)(2,1)S(1)} %collective-permute-done.7.gate_hbm, bf16[704,1024]{1,0:T(8,128)(2,1)S(1)} %collective-permute-done.8.up_hbm, ...), custom_call_target="tpu_custom_call" | custom-call | bytes 8650752 | tf_op jit(solution)/shard_map/pallas_call | solution.py:361
  58.5 1.5 %collective-permute-done.22.refs_5_ = bf16[64,1024]{1,0:T(8,128)(2,1)S(1)} collective-permute-done((bf16[64,1024]{1,0:T(8,128)(2,1)S(1)}, bf16[64,1024]{1,0:T(8,128)(2,1)S(1)}, u32[]{:S(2)}, u32[]{:S(2)}) %collective-permute-start.22) | collective-permute-done | bytes 131104 | tf_op jit(solution)/shard_map/ppermute | solution.py:422
  60.0 0.7 collective-permute-done.21.refs_2_
  60.9 1.6 %collective-permute-start.23 = (bf16[128,1024]{1,0:T(8,128)(2,1)S(1)}, bf16[128,1024]{1,0:T(8,128)(2,1)S(1)}, u32[]{:S(2)}, u32[]{:S(2)}) collective-permute-start(bf16[128,1024]{1,0:T(8,128)(2,1)S(1)} %get-tuple-element.121.refs_1_), channel_id=1, source_target_pairs={{0,2},{1,3},{2,0},{3,1},{4,6},{5,7},{6,4},{7,5},{8,10},{9,11},{10,... | collective-permute-start | bytes 786440 | tf_op jit(solution)/shard_map/ppermute | solution.py:422
  62.5 2.3 %collective-permute-start.24 = (bf16[128,1024]{1,0:T(8,128)(2,1)S(1)}, bf16[128,1024]{1,0:T(8,128)(2,1)S(1)}, u32[]{:S(2)}, u32[]{:S(2)}) collective-permute-start(bf16[128,1024]{1,0:T(8,128)(2,1)S(1)} %get-tuple-element.121.refs_1_), channel_id=1, source_target_pairs={{0,8},{1,9},{2,10},{3,11},{4,12},{5,13},{6,14},{7,15},{8,0},{9,1},... | collective-permute-start | bytes 786440 | tf_op jit(solution)/shard_map/ppermute | solution.py:422
  64.8 2.6 %collective-permute-done.23.refs_2_ = bf16[128,1024]{1,0:T(8,128)(2,1)S(1)} collective-permute-done((bf16[128,1024]{1,0:T(8,128)(2,1)S(1)}, bf16[128,1024]{1,0:T(8,128)(2,1)S(1)}, u32[]{:S(2)}, u32[]{:S(2)}) %collective-permute-start.23) | collective-permute-done | bytes 262176 | tf_op jit(solution)/shard_map/ppermute | solution.py:422
  67.4 3.4 %shard_map.110 = (bf16[1024,128]{1,0:T(8,128)(2,1)S(1)}, bf16[1024,128]{1,0:T(8,128)(2,1)S(1)}) custom-call(s32[6]{0:T(128)S(1)} %stack.42.place_ref.refs_0_, bf16[128,1024]{1,0:T(8,128)(2,1)S(1)} %get-tuple-element.121.refs_1_, bf16[128,1024]{1,0:T(8,128)(2,1)S(1)} %collective-permute-done.23.refs_2_, f32[2,2,16,128]{3,2,1,0:T(8,128)S(1)} %shard_map.103.refs_14_.refs_3_, ...), custom_call_target="tpu_custom_call" | custom-call | flops 2214592512 | bytes 9699328 | tf_op jit(solution)/shard_map/pallas_call | solution.py:284
  70.7 4.1 %collective-permute-done.24.refs_1_ = bf16[128,1024]{1,0:T(8,128)(2,1)S(1)} collective-permute-done((bf16[128,1024]{1,0:T(8,128)(2,1)S(1)}, bf16[128,1024]{1,0:T(8,128)(2,1)S(1)}, u32[]{:S(2)}, u32[]{:S(2)}) %collective-permute-start.24) | collective-permute-done | bytes 262176 | tf_op jit(solution)/shard_map/ppermute | solution.py:422
  75.2 7.1 %collective-permute-done.28.refs_1_ = bf16[128,1024]{1,0:T(8,128)(2,1)S(1)} collective-permute-done((bf16[128,1024]{1,0:T(8,128)(2,1)S(1)}, bf16[128,1024]{1,0:T(8,128)(2,1)S(1)}, u32[]{:S(2)}, u32[]{:S(2)}) %collective-permute-start.28) | collective-permute-done | bytes 262176 | tf_op jit(solution)/shard_map/ppermute | solution.py:422
  82.9 3.4 %shard_map.111 = (bf16[1024,128]{1,0:T(8,128)(2,1)S(1)}, bf16[1024,128]{1,0:T(8,128)(2,1)S(1)}) custom-call(s32[6]{0:T(128)S(1)} %stack.42.place_ref.refs_0_, bf16[128,1024]{1,0:T(8,128)(2,1)S(1)} %collective-permute-done.24.refs_1_, bf16[128,1024]{1,0:T(8,128)(2,1)S(1)} %collective-permute-done.25.refs_2_, ...), custom_call_target="tpu_custom_call" | custom-call | flops 2214592512 | bytes 9699328 | tf_op jit(solution)/shard_map/pallas_call | solution.py:284
  86.2 1.7 %collective-permute-start.26 = (bf16[1024,128]{1,0:T(8,128)(2,1)S(1)}, bf16[1024,128]{1,0:T(8,128)(2,1)S(1)}, u32[]{:S(2)}, u32[]{:S(2)}) collective-permute-start(bf16[1024,128]{1,0:T(8,128)(2,1)S(1)} %get-tuple-element.117.refs_10_), channel_id=1, source_target_pairs={{0,2},{1,3},{2,0},{3,1},{4,6},{5,7},{6,4},{7,5},{8,10},{9,11},{10,... | collective-permute-start | bytes 786440 | tf_op jit(solution)/shard_map/ppermute | solution.py:422
  88.0 0.8 collective-permute-done.32.refs_1_
  89.1 2.0 %collective-permute-done.29.refs_2_ = bf16[128,1024]{1,0:T(8,128)(2,1)S(1)} collective-permute-done((bf16[128,1024]{1,0:T(8,128)(2,1)S(1)}, bf16[128,1024]{1,0:T(8,128)(2,1)S(1)}, u32[]{:S(2)}, u32[]{:S(2)}) %collective-permute-start.29) | collective-permute-done | bytes 262176 | tf_op jit(solution)/shard_map/ppermute | solution.py:422
  91.1 3.4 %shard_map.113 = (bf16[1024,128]{1,0:T(8,128)(2,1)S(1)}, bf16[1024,128]{1,0:T(8,128)(2,1)S(1)}) custom-call(s32[6]{0:T(128)S(1)} %stack.42.place_ref.refs_0_, bf16[128,1024]{1,0:T(8,128)(2,1)S(1)} %collective-permute-done.28.refs_1_, bf16[128,1024]{1,0:T(8,128)(2,1)S(1)} %collective-permute-done.29.refs_2_, ...), custom_call_target="tpu_custom_call" | custom-call | flops 2214592512 | bytes 9699328 | tf_op jit(solution)/shard_map/pallas_call | solution.py:284
  94.6 2.2 %collective-permute-done.26.refs_1_ = bf16[1024,128]{1,0:T(8,128)(2,1)S(1)} collective-permute-done((bf16[1024,128]{1,0:T(8,128)(2,1)S(1)}, bf16[1024,128]{1,0:T(8,128)(2,1)S(1)}, u32[]{:S(2)}, u32[]{:S(2)}) %collective-permute-start.26) | collective-permute-done | bytes 262176 | tf_op jit(solution)/shard_map/ppermute | solution.py:422
  96.8 2.4 %collective-permute-start.27 = (bf16[1024,128]{1,0:T(8,128)(2,1)S(1)}, bf16[1024,128]{1,0:T(8,128)(2,1)S(1)}, u32[]{:S(2)}, u32[]{:S(2)}) collective-permute-start(bf16[1024,128]{1,0:T(8,128)(2,1)S(1)} %shard_map.112.refs_10_), channel_id=1, source_target_pairs={{0,8},{1,9},{2,10},{3,11},{4,12},{5,13},{6,14},{7,15},{8,0},{9,1},... | collective-permute-start | bytes 786440 | tf_op jit(solution)/shard_map/ppermute | solution.py:422
  99.2 3.1 %collective-permute-done.33.refs_2_ = bf16[128,1024]{1,0:T(8,128)(2,1)S(1)} collective-permute-done((bf16[128,1024]{1,0:T(8,128)(2,1)S(1)}, bf16[128,1024]{1,0:T(8,128)(2,1)S(1)}, u32[]{:S(2)}, u32[]{:S(2)}) %collective-permute-start.33) | collective-permute-done | bytes 262176 | tf_op jit(solution)/shard_map/ppermute | solution.py:422
  102.4 3.4 %shard_map.115 = (bf16[1024,128]{1,0:T(8,128)(2,1)S(1)}, bf16[1024,128]{1,0:T(8,128)(2,1)S(1)}) custom-call(s32[6]{0:T(128)S(1)} %stack.42.place_ref.refs_0_, bf16[128,1024]{1,0:T(8,128)(2,1)S(1)} %collective-permute-done.32.refs_1_, bf16[128,1024]{1,0:T(8,128)(2,1)S(1)} %collective-permute-done.33.refs_2_, ...), custom_call_target="tpu_custom_call" | custom-call | flops 2214592512 | bytes 9699328 | tf_op jit(solution)/shard_map/pallas_call | solution.py:284
  105.7 0.5 collective-permute-start.34
  106.3 1.6 %collective-permute-start.36 = (bf16[1024,128]{1,0:T(8,128)(2,1)S(1)}, bf16[1024,128]{1,0:T(8,128)(2,1)S(1)}, u32[]{:S(2)}, u32[]{:S(2)}) collective-permute-start(bf16[1024,128]{1,0:T(8,128)(2,1)S(1)} %get-tuple-element.124.refs_10_), channel_id=1, source_target_pairs={{0,2},{1,3},{2,0},{3,1},{4,6},{5,7},{6,4},{7,5},{8,10},{9,11},{10,... | collective-permute-start | bytes 786440 | tf_op jit(solution)/shard_map/ppermute | solution.py:422
  107.9 1.9 %collective-permute-start.31 = (bf16[1024,128]{1,0:T(8,128)(2,1)S(1)}, bf16[1024,128]{1,0:T(8,128)(2,1)S(1)}, u32[]{:S(2)}, u32[]{:S(2)}) collective-permute-start(bf16[1024,128]{1,0:T(8,128)(2,1)S(1)} %shard_map.114), channel_id=1, source_target_pairs={{0,12},{1,13},{2,14},{3,15},{4,8},{5,9},{6,10},{7,11},{8,4},{9,5},... | collective-permute-start | bytes 786440 | tf_op jit(solution)/shard_map/ppermute | solution.py:422
  109.8 4.5 %collective-permute-done.34.refs_1_ = bf16[1024,128]{1,0:T(8,128)(2,1)S(1)} collective-permute-done((bf16[1024,128]{1,0:T(8,128)(2,1)S(1)}, bf16[1024,128]{1,0:T(8,128)(2,1)S(1)}, u32[]{:S(2)}, u32[]{:S(2)}) %collective-permute-start.34) | collective-permute-done | bytes 262176 | tf_op jit(solution)/shard_map/ppermute | solution.py:422
  114.4 1.7 %collective-permute-start.35 = (bf16[1024,128]{1,0:T(8,128)(2,1)S(1)}, bf16[1024,128]{1,0:T(8,128)(2,1)S(1)}, u32[]{:S(2)}, u32[]{:S(2)}) collective-permute-start(bf16[1024,128]{1,0:T(8,128)(2,1)S(1)} %shard_map.116), channel_id=1, source_target_pairs={{0,4},{1,5},{2,6},{3,7},{4,0},{5,1},{6,2},{7,3},{8,12},{9,13},{10,... | collective-permute-start | bytes 786440 | tf_op jit(solution)/shard_map/ppermute | solution.py:422
  116.0 1.1 collective-permute-done.36.refs_4_
  117.1 1.1 collective-permute-done.31.refs_2_
  118.2 2.8 %collective-permute-done.35.refs_3_ = bf16[1024,128]{1,0:T(8,128)(2,1)S(1)} collective-permute-done((bf16[1024,128]{1,0:T(8,128)(2,1)S(1)}, bf16[1024,128]{1,0:T(8,128)(2,1)S(1)}, u32[]{:S(2)}, u32[]{:S(2)}) %collective-permute-start.35) | collective-permute-done | bytes 262176 | tf_op jit(solution)/shard_map/ppermute | solution.py:422
  121.0 1.0 shard_map.117
  (52 shorter events, 2.5 us)
Async XLA Ops:
  0.0 13.8 %collective-permute-start.3 = (bf16[128,1024]{1,0:T(8,128)(2,1)}, bf16[128,1024]{1,0:T(8,128)(2,1)S(1)}, u32[]{:S(2)}, u32[]{:S(2)}) collective-permute-start(bf16[128,1024]{1,0:T(8,128)(2,1)} %tokens_ref.2), channel_id=1, source_target_pairs={{0,16},{16,0},{1,17},{17,1},{2,18},{18,2},{3,19},{19,3},{4,20},{20... | collective-permute-start | bytes 786440 | tf_op jit(solution)/shard_map/ppermute | solution.py:419
  2.9 10.9 %collective-permute-start.4 = (bf16[128,1024]{1,0:T(8,128)(2,1)}, bf16[128,1024]{1,0:T(8,128)(2,1)S(1)}, u32[]{:S(2)}, u32[]{:S(2)}) collective-permute-start(bf16[128,1024]{1,0:T(8,128)(2,1)} %tokens_ref.2), channel_id=1, source_target_pairs={{0,2},{1,3},{2,0},{3,1},{4,6},{5,7},{6,4},{7,5},{8,10},{9,11},{10,... | collective-permute-start | bytes 786440 | tf_op jit(solution)/shard_map/ppermute | solution.py:422
  4.5 0.9 copy-start.5
  5.5 0.8 copy-start.6
  7.3 6.5 %collective-permute-start.1 = (bf16[32,1024]{1,0:T(8,128)(2,1)S(1)}, bf16[32,1024]{1,0:T(8,128)(2,1)S(1)}, u32[]{:S(2)}, u32[]{:S(2)}) collective-permute-start(bf16[32,1024]{1,0:T(8,128)(2,1)S(1)} %get-tuple-element.67), channel_id=1, source_target_pairs={{0,2},{1,3},{2,0},{3,1},{4,6},{5,7},{6,4},{7,5},{8,10},{9,11},{10,... | collective-permute-start | bytes 196616 | tf_op jit(solution)/shard_map/ppermute | solution.py:422
  7.8 5.9 %collective-permute-start.2 = (bf16[32,1024]{1,0:T(8,128)(2,1)S(1)}, bf16[32,1024]{1,0:T(8,128)(2,1)S(1)}, u32[]{:S(2)}, u32[]{:S(2)}) collective-permute-start(bf16[32,1024]{1,0:T(8,128)(2,1)S(1)} %get-tuple-element.68), channel_id=1, source_target_pairs={{0,18},{1,19},{2,16},{3,17},{4,22},{5,23},{6,20},{7,21},{8,26},{9,... | collective-permute-start | bytes 196616 | tf_op jit(solution)/shard_map/ppermute | solution.py:452
  9.3 4.4 %collective-permute-start = (bf16[32,1024]{1,0:T(8,128)(2,1)S(1)}, bf16[32,1024]{1,0:T(8,128)(2,1)S(1)}, u32[]{:S(2)}, u32[]{:S(2)}) collective-permute-start(bf16[32,1024]{1,0:T(8,128)(2,1)S(1)} %get-tuple-element.66), channel_id=1, source_target_pairs={{0,16},{16,0},{1,17},{17,1},{2,18},{18,2},{3,19},{19,3},{4,20},{20... | collective-permute-start | bytes 196616 | tf_op jit(solution)/shard_map/ppermute | solution.py:419
  13.8 15.7 %collective-permute-start.7 = (bf16[704,1024]{1,0:T(8,128)(2,1)}, bf16[704,1024]{1,0:T(8,128)(2,1)S(1)}, u32[]{:S(2)}, u32[]{:S(2)}) collective-permute-start(bf16[704,1024]{1,0:T(8,128)(2,1)} %bitcast.23), channel_id=1, source_target_pairs={{0,1},{1,0},{2,3},{3,2},{4,5},{5,4},{6,7},{7,6},{8,9},{9,8},{10,11... | collective-permute-start | bytes 4325384 | tf_op jit(solution)/shard_map/ppermute | solution.py:422
  13.9 15.6 %collective-permute-start.8 = (bf16[704,1024]{1,0:T(8,128)(2,1)}, bf16[704,1024]{1,0:T(8,128)(2,1)S(1)}, u32[]{:S(2)}, u32[]{:S(2)}) collective-permute-start(bf16[704,1024]{1,0:T(8,128)(2,1)} %bitcast.25), channel_id=1, source_target_pairs={{0,1},{1,0},{2,3},{3,2},{4,5},{5,4},{6,7},{7,6},{8,9},{9,8},{10,11... | collective-permute-start | bytes 4325384 | tf_op jit(solution)/shard_map/ppermute | solution.py:422
  14.4 14.9 %collective-permute-start.5 = (bf16[4,32,1024]{2,1,0:T(8,128)(2,1)S(1)}, bf16[4,32,1024]{2,1,0:T(8,128)(2,1)S(1)}, u32[]{:S(2)}, u32[]{:S(2)}) collective-permute-start(bf16[4,32,1024]{2,1,0:T(8,128)(2,1)S(1)} %pad_maximum_fusion.refs_6_), channel_id=1, source_target_pairs={{0,8},{1,9},{2,10},{3,11},{4,12},{5,13},{6,14},{7,15},{8,0},{9,1},... | collective-permute-start | bytes 786440 | tf_op jit(solution)/shard_map/ppermute | solution.py:422
  17.0 12.5 %collective-permute-start.6 = (bf16[4,32,1024]{2,1,0:T(8,128)(2,1)S(1)}, bf16[4,32,1024]{2,1,0:T(8,128)(2,1)S(1)}, u32[]{:S(2)}, u32[]{:S(2)}) collective-permute-start(bf16[4,32,1024]{2,1,0:T(8,128)(2,1)S(1)} %pad_maximum_fusion.refs_6_), channel_id=1, source_target_pairs={{0,4},{1,5},{2,6},{3,7},{4,0},{5,1},{6,2},{7,3},{8,12},{9,13},{10,... | collective-permute-start | bytes 786440 | tf_op jit(solution)/shard_map/ppermute | solution.py:422
  18.6 10.9 %collective-permute-start.9 = (bf16[128,1024]{1,0:T(8,128)(2,1)S(1)}, bf16[128,1024]{1,0:T(8,128)(2,1)S(1)}, u32[]{:S(2)}, u32[]{:S(2)}) collective-permute-start(bf16[128,1024]{1,0:T(8,128)(2,1)S(1)} %collective-permute-done.3.refs_3_), channel_id=1, source_target_pairs={{0,2},{1,3},{2,0},{3,1},{4,6},{5,7},{6,4},{7,5},{8,10},{9,11},{10,... | collective-permute-start | bytes 786440 | tf_op jit(solution)/shard_map/ppermute | solution.py:422
  20.1 0.9 copy-start.3
  21.0 0.7 copy-start.7
  21.7 0.7 copy-start.8
  22.4 0.7 copy-start.9
  29.5 11.8 %collective-permute-start.17 = (bf16[704,1024]{1,0:T(8,128)(2,1)}, bf16[704,1024]{1,0:T(8,128)(2,1)S(1)}, u32[]{:S(2)}, u32[]{:S(2)}) collective-permute-start(bf16[704,1024]{1,0:T(8,128)(2,1)} %bitcast.21), channel_id=1, source_target_pairs={{0,1},{1,0},{2,3},{3,2},{4,5},{5,4},{6,7},{7,6},{8,9},{9,8},{10,11... | collective-permute-start | bytes 4325384 | tf_op jit(solution)/shard_map/ppermute | solution.py:422
  29.6 9.8 %collective-permute-start.13 = (bf16[4,32,1024]{2,1,0:T(8,128)(2,1)S(1)}, bf16[4,32,1024]{2,1,0:T(8,128)(2,1)S(1)}, u32[]{:S(2)}, u32[]{:S(2)}) collective-permute-start(bf16[4,32,1024]{2,1,0:T(8,128)(2,1)S(1)} %collective-permute-done.5.refs_10_), channel_id=1, source_target_pairs={{0,4},{1,5},{2,6},{3,7},{4,0},{5,1},{6,2},{7,3},{8,12},{9,13},{10,... | collective-permute-start | bytes 786440 | tf_op jit(solution)/shard_map/ppermute | solution.py:422
  31.1 3.7 %collective-permute-start.15 = (f32[16,128]{1,0:T(8,128)S(1)}, f32[16,128]{1,0:T(8,128)S(1)}, u32[]{:S(2)}, u32[]{:S(2)}) collective-permute-start(f32[16,128]{1,0:T(8,128)S(1)} %get-tuple-element.85.first_ref), channel_id=1, source_target_pairs={{0,2},{1,3},{2,0},{3,1},{4,6},{5,7},{6,4},{7,5},{8,10},{9,11},{10,... | collective-permute-start | bytes 24584 | tf_op jit(solution)/shard_map/ppermute | solution.py:422
  34.7 4.6 %collective-permute-start.16 = (f32[2,16,128]{2,1,0:T(8,128)S(1)}, f32[2,16,128]{2,1,0:T(8,128)S(1)}, u32[]{:S(2)}, u32[]{:S(2)}) collective-permute-start(f32[2,16,128]{2,1,0:T(8,128)S(1)} %shard_map.102.first_ref), channel_id=1, source_target_pairs={{0,8},{1,9},{2,10},{3,11},{4,12},{5,13},{6,14},{7,15},{8,0},{9,1},... | collective-permute-start | bytes 49160 | tf_op jit(solution)/shard_map/ppermute | solution.py:422
  37.1 2.8 %collective-permute-start.10 = (bf16[4,32,1024]{2,1,0:T(8,128)(2,1)S(1)}, bf16[4,32,1024]{2,1,0:T(8,128)(2,1)S(1)}, u32[]{:S(2)}, u32[]{:S(2)}) collective-permute-start(bf16[4,32,1024]{2,1,0:T(8,128)(2,1)S(1)} %pad_maximum_fusion.refs_6_), channel_id=1, source_target_pairs={{0,1},{1,0},{2,3},{3,2},{4,5},{5,4},{6,7},{7,6},{8,9},{9,8},{10,11... | collective-permute-start | bytes 786440 | tf_op jit(solution)/shard_map/ppermute | solution.py:422
  37.1 3.8 %collective-permute-start.12 = (bf16[4,32,1024]{2,1,0:T(8,128)(2,1)S(1)}, bf16[4,32,1024]{2,1,0:T(8,128)(2,1)S(1)}, u32[]{:S(2)}, u32[]{:S(2)}) collective-permute-start(bf16[4,32,1024]{2,1,0:T(8,128)(2,1)S(1)} %collective-permute-done.5.refs_10_), channel_id=1, source_target_pairs={{0,1},{1,0},{2,3},{3,2},{4,5},{5,4},{6,7},{7,6},{8,9},{9,8},{10,11... | collective-permute-start | bytes 786440 | tf_op jit(solution)/shard_map/ppermute | solution.py:422
  39.4 1.5 %collective-permute-start.11 = (bf16[4,32,1024]{2,1,0:T(8,128)(2,1)S(1)}, bf16[4,32,1024]{2,1,0:T(8,128)(2,1)S(1)}, u32[]{:S(2)}, u32[]{:S(2)}) collective-permute-start(bf16[4,32,1024]{2,1,0:T(8,128)(2,1)S(1)} %collective-permute-done.6.refs_8_), channel_id=1, source_target_pairs={{0,1},{1,0},{2,3},{3,2},{4,5},{5,4},{6,7},{7,6},{8,9},{9,8},{10,11... | collective-permute-start | bytes 786440 | tf_op jit(solution)/shard_map/ppermute | solution.py:422
  39.4 1.9 %collective-permute-start.14 = (bf16[4,32,1024]{2,1,0:T(8,128)(2,1)S(1)}, bf16[4,32,1024]{2,1,0:T(8,128)(2,1)S(1)}, u32[]{:S(2)}, u32[]{:S(2)}) collective-permute-start(bf16[4,32,1024]{2,1,0:T(8,128)(2,1)S(1)} %collective-permute-done.13.refs_12_), channel_id=1, source_target_pairs={{0,1},{1,0},{2,3},{3,2},{4,5},{5,4},{6,7},{7,6},{8,9},{9,8},{10,11... | collective-permute-start | bytes 786440 | tf_op jit(solution)/shard_map/ppermute | solution.py:422
  41.3 7.4 %copy-start = (bf16[1,704,1024]{2,1,0:T(8,128)(2,1)S(1)}, bf16[1,704,1024]{2,1,0:T(8,128)(2,1)}, u32[]{:S(2)}) copy-start(bf16[1,704,1024]{2,1,0:T(8,128)(2,1)} %param.19) | copy-start | bytes 4325380
  41.3 7.4 %copy-start.1 = (bf16[1,1024,704]{1,2,0:T(8,128)(2,1)S(1)}, bf16[1,1024,704]{1,2,0:T(8,128)(2,1)}, u32[]{:S(2)}) copy-start(bf16[1,1024,704]{1,2,0:T(8,128)(2,1)} %param.17) | copy-start | bytes 4325380
  41.3 7.4 %copy-start.2 = (bf16[1,1024,704]{1,2,0:T(8,128)(2,1)S(1)}, bf16[1,1024,704]{1,2,0:T(8,128)(2,1)}, u32[]{:S(2)}) copy-start(bf16[1,1024,704]{1,2,0:T(8,128)(2,1)} %param.18) | copy-start | bytes 4325380
  45.3 8.4 %collective-permute-start.18 = (bf16[2,64,1024]{2,1,0:T(8,128)(2,1)S(1)}, bf16[2,64,1024]{2,1,0:T(8,128)(2,1)S(1)}, u32[]{:S(2)}, u32[]{:S(2)}) collective-permute-start(bf16[2,64,1024]{2,1,0:T(8,128)(2,1)S(1)} %get-tuple-element.88), channel_id=1, source_target_pairs={{0,2},{1,3},{2,0},{3,1},{4,6},{5,7},{6,4},{7,5},{8,10},{9,11},{10,... | collective-permute-start | bytes 786440 | tf_op jit(solution)/shard_map/ppermute | solution.py:422
  46.9 8.1 %collective-permute-start.19 = (bf16[2,64,1024]{2,1,0:T(8,128)(2,1)S(1)}, bf16[2,64,1024]{2,1,0:T(8,128)(2,1)S(1)}, u32[]{:S(2)}, u32[]{:S(2)}) collective-permute-start(bf16[2,64,1024]{2,1,0:T(8,128)(2,1)S(1)} %get-tuple-element.89), channel_id=1, source_target_pairs={{0,16},{16,0},{1,17},{17,1},{2,18},{18,2},{3,19},{19,3},{4,20},{20... | collective-permute-start | bytes 786440 | tf_op jit(solution)/shard_map/ppermute | solution.py:419
  47.4 3.9 %collective-permute-start.20 = (f32[2,2,16,128]{3,2,1,0:T(8,128)S(1)}, f32[2,2,16,128]{3,2,1,0:T(8,128)S(1)}, u32[]{:S(2)}, u32[]{:S(2)}) collective-permute-start(f32[2,2,16,128]{3,2,1,0:T(8,128)S(1)} %shard_map.103.refs_14_.refs_3_), channel_id=1, source_target_pairs={{0,4},{1,5},{2,6},{3,7},{4,0},{5,1},{6,2},{7,3},{8,12},{9,13},{10,... | collective-permute-start | bytes 98312 | tf_op jit(solution)/shard_map/ppermute | solution.py:422
  55.0 5.0 %collective-permute-start.22 = (bf16[64,1024]{1,0:T(8,128)(2,1)S(1)}, bf16[64,1024]{1,0:T(8,128)(2,1)S(1)}, u32[]{:S(2)}, u32[]{:S(2)}) collective-permute-start(bf16[64,1024]{1,0:T(8,128)(2,1)S(1)} %shard_map.107), channel_id=1, source_target_pairs={{0,2},{1,3},{2,0},{3,1},{4,6},{5,7},{6,4},{7,5},{8,10},{9,11},{10,... | collective-permute-start | bytes 393224 | tf_op jit(solution)/shard_map/ppermute | solution.py:422
  55.6 5.1 %copy-start.4 = (bf16[128,1024]{1,0:T(8,128)(2,1)S(1)}, bf16[128,1024]{1,0:T(8,128)(2,1)}, u32[]{:S(2)}) copy-start(bf16[128,1024]{1,0:T(8,128)(2,1)} %tokens_ref.2) | copy-start | bytes 786436
  55.6 5.1 %copy-start.10 = (f32[1024]{0:T(1024)S(1)}, f32[1024]{0:T(1024)}, u32[]{:S(2)}) copy-start(f32[1024]{0:T(1024)} %param.14) | copy-start | bytes 12292
  55.6 5.0 %collective-permute-start.21 = (bf16[64,1024]{1,0:T(8,128)(2,1)S(1)}, bf16[64,1024]{1,0:T(8,128)(2,1)S(1)}, u32[]{:S(2)}, u32[]{:S(2)}) collective-permute-start(bf16[64,1024]{1,0:T(8,128)(2,1)S(1)} %shard_map.106), channel_id=1, source_target_pairs={{0,16},{16,0},{1,17},{17,1},{2,18},{18,2},{3,19},{19,3},{4,20},{20... | collective-permute-start | bytes 393224 | tf_op jit(solution)/shard_map/ppermute | solution.py:419
  60.9 6.4 %collective-permute-start.23 = (bf16[128,1024]{1,0:T(8,128)(2,1)S(1)}, bf16[128,1024]{1,0:T(8,128)(2,1)S(1)}, u32[]{:S(2)}, u32[]{:S(2)}) collective-permute-start(bf16[128,1024]{1,0:T(8,128)(2,1)S(1)} %get-tuple-element.121.refs_1_), channel_id=1, source_target_pairs={{0,2},{1,3},{2,0},{3,1},{4,6},{5,7},{6,4},{7,5},{8,10},{9,11},{10,... | collective-permute-start | bytes 786440 | tf_op jit(solution)/shard_map/ppermute | solution.py:422
  62.5 12.3 %collective-permute-start.24 = (bf16[128,1024]{1,0:T(8,128)(2,1)S(1)}, bf16[128,1024]{1,0:T(8,128)(2,1)S(1)}, u32[]{:S(2)}, u32[]{:S(2)}) collective-permute-start(bf16[128,1024]{1,0:T(8,128)(2,1)S(1)} %get-tuple-element.121.refs_1_), channel_id=1, source_target_pairs={{0,8},{1,9},{2,10},{3,11},{4,12},{5,13},{6,14},{7,15},{8,0},{9,1},... | collective-permute-start | bytes 786440 | tf_op jit(solution)/shard_map/ppermute | solution.py:422
  74.8 7.4 %collective-permute-start.28 = (bf16[128,1024]{1,0:T(8,128)(2,1)S(1)}, bf16[128,1024]{1,0:T(8,128)(2,1)S(1)}, u32[]{:S(2)}, u32[]{:S(2)}) collective-permute-start(bf16[128,1024]{1,0:T(8,128)(2,1)S(1)} %collective-permute-done.24.refs_1_), channel_id=1, source_target_pairs={{0,4},{1,5},{2,6},{3,7},{4,0},{5,1},{6,2},{7,3},{8,12},{9,13},{10,... | collective-permute-start | bytes 786440 | tf_op jit(solution)/shard_map/ppermute | solution.py:422
  74.8 8.1 %collective-permute-start.25 = (bf16[128,1024]{1,0:T(8,128)(2,1)S(1)}, bf16[128,1024]{1,0:T(8,128)(2,1)S(1)}, u32[]{:S(2)}, u32[]{:S(2)}) collective-permute-start(bf16[128,1024]{1,0:T(8,128)(2,1)S(1)} %collective-permute-done.24.refs_1_), channel_id=1, source_target_pairs={{0,2},{1,3},{2,0},{3,1},{4,6},{5,7},{6,4},{7,5},{8,10},{9,11},{10,... | collective-permute-start | bytes 786440 | tf_op jit(solution)/shard_map/ppermute | solution.py:422
  82.2 6.5 %collective-permute-start.32 = (bf16[128,1024]{1,0:T(8,128)(2,1)S(1)}, bf16[128,1024]{1,0:T(8,128)(2,1)S(1)}, u32[]{:S(2)}, u32[]{:S(2)}) collective-permute-start(bf16[128,1024]{1,0:T(8,128)(2,1)S(1)} %get-tuple-element.121.refs_1_), channel_id=1, source_target_pairs={{0,4},{1,5},{2,6},{3,7},{4,0},{5,1},{6,2},{7,3},{8,12},{9,13},{10,... | collective-permute-start | bytes 786440 | tf_op jit(solution)/shard_map/ppermute | solution.py:422
  82.5 8.6 %collective-permute-start.29 = (bf16[128,1024]{1,0:T(8,128)(2,1)S(1)}, bf16[128,1024]{1,0:T(8,128)(2,1)S(1)}, u32[]{:S(2)}, u32[]{:S(2)}) collective-permute-start(bf16[128,1024]{1,0:T(8,128)(2,1)S(1)} %collective-permute-done.28.refs_1_), channel_id=1, source_target_pairs={{0,2},{1,3},{2,0},{3,1},{4,6},{5,7},{6,4},{7,5},{8,10},{9,11},{10,... | collective-permute-start | bytes 786440 | tf_op jit(solution)/shard_map/ppermute | solution.py:422
  86.2 10.5 %collective-permute-start.26 = (bf16[1024,128]{1,0:T(8,128)(2,1)S(1)}, bf16[1024,128]{1,0:T(8,128)(2,1)S(1)}, u32[]{:S(2)}, u32[]{:S(2)}) collective-permute-start(bf16[1024,128]{1,0:T(8,128)(2,1)S(1)} %get-tuple-element.117.refs_10_), channel_id=1, source_target_pairs={{0,2},{1,3},{2,0},{3,1},{4,6},{5,7},{6,4},{7,5},{8,10},{9,11},{10,... | collective-permute-start | bytes 786440 | tf_op jit(solution)/shard_map/ppermute | solution.py:422
  88.7 13.6 %collective-permute-start.33 = (bf16[128,1024]{1,0:T(8,128)(2,1)S(1)}, bf16[128,1024]{1,0:T(8,128)(2,1)S(1)}, u32[]{:S(2)}, u32[]{:S(2)}) collective-permute-start(bf16[128,1024]{1,0:T(8,128)(2,1)S(1)} %collective-permute-done.32.refs_1_), channel_id=1, source_target_pairs={{0,2},{1,3},{2,0},{3,1},{4,6},{5,7},{6,4},{7,5},{8,10},{9,11},{10,... | collective-permute-start | bytes 786440 | tf_op jit(solution)/shard_map/ppermute | solution.py:422
  94.5 13.3 %collective-permute-start.30 = (bf16[1024,128]{1,0:T(8,128)(2,1)S(1)}, bf16[1024,128]{1,0:T(8,128)(2,1)S(1)}, u32[]{:S(2)}, u32[]{:S(2)}) collective-permute-start(bf16[1024,128]{1,0:T(8,128)(2,1)S(1)} %get-tuple-element.120.refs_11_), channel_id=1, source_target_pairs={{0,2},{1,3},{2,0},{3,1},{4,6},{5,7},{6,4},{7,5},{8,10},{9,11},{10,... | collective-permute-start | bytes 786440 | tf_op jit(solution)/shard_map/ppermute | solution.py:422
  96.8 11.0 %collective-permute-start.27 = (bf16[1024,128]{1,0:T(8,128)(2,1)S(1)}, bf16[1024,128]{1,0:T(8,128)(2,1)S(1)}, u32[]{:S(2)}, u32[]{:S(2)}) collective-permute-start(bf16[1024,128]{1,0:T(8,128)(2,1)S(1)} %shard_map.112.refs_10_), channel_id=1, source_target_pairs={{0,8},{1,9},{2,10},{3,11},{4,12},{5,13},{6,14},{7,15},{8,0},{9,1},... | collective-permute-start | bytes 786440 | tf_op jit(solution)/shard_map/ppermute | solution.py:422
  105.7 8.6 %collective-permute-start.34 = (bf16[1024,128]{1,0:T(8,128)(2,1)S(1)}, bf16[1024,128]{1,0:T(8,128)(2,1)S(1)}, u32[]{:S(2)}, u32[]{:S(2)}) collective-permute-start(bf16[1024,128]{1,0:T(8,128)(2,1)S(1)} %get-tuple-element.123), channel_id=1, source_target_pairs={{0,2},{1,3},{2,0},{3,1},{4,6},{5,7},{6,4},{7,5},{8,10},{9,11},{10,... | collective-permute-start | bytes 786440 | tf_op jit(solution)/shard_map/ppermute | solution.py:422
  106.3 10.8 %collective-permute-start.36 = (bf16[1024,128]{1,0:T(8,128)(2,1)S(1)}, bf16[1024,128]{1,0:T(8,128)(2,1)S(1)}, u32[]{:S(2)}, u32[]{:S(2)}) collective-permute-start(bf16[1024,128]{1,0:T(8,128)(2,1)S(1)} %get-tuple-element.124.refs_10_), channel_id=1, source_target_pairs={{0,2},{1,3},{2,0},{3,1},{4,6},{5,7},{6,4},{7,5},{8,10},{9,11},{10,... | collective-permute-start | bytes 786440 | tf_op jit(solution)/shard_map/ppermute | solution.py:422
  107.9 10.2 %collective-permute-start.31 = (bf16[1024,128]{1,0:T(8,128)(2,1)S(1)}, bf16[1024,128]{1,0:T(8,128)(2,1)S(1)}, u32[]{:S(2)}, u32[]{:S(2)}) collective-permute-start(bf16[1024,128]{1,0:T(8,128)(2,1)S(1)} %shard_map.114), channel_id=1, source_target_pairs={{0,12},{1,13},{2,14},{3,15},{4,8},{5,9},{6,10},{7,11},{8,4},{9,5},... | collective-permute-start | bytes 786440 | tf_op jit(solution)/shard_map/ppermute | solution.py:422
  114.4 6.6 %collective-permute-start.35 = (bf16[1024,128]{1,0:T(8,128)(2,1)S(1)}, bf16[1024,128]{1,0:T(8,128)(2,1)S(1)}, u32[]{:S(2)}, u32[]{:S(2)}) collective-permute-start(bf16[1024,128]{1,0:T(8,128)(2,1)S(1)} %shard_map.116), channel_id=1, source_target_pairs={{0,4},{1,5},{2,6},{3,7},{4,0},{5,1},{6,2},{7,3},{8,12},{9,13},{10,... | collective-permute-start | bytes 786440 | tf_op jit(solution)/shard_map/ppermute | solution.py:422
